TPU v7x, 32 devices: a whole 2x2x4 slice. The times are simulated.
32 devices in a mesh: samp: 4 (over y, x), feat: 8 (over z, core).
Axes of the slice: x: 2, y: 2, z: 4, core: 2. Of those that a mesh axis runs over, the one named last changes fastest.
Arguments:
- data: float32 [4096, 16384], P('samp', 'feat'), may hold values from -0.07216878 to 0.07216878, as said below
- targets: float32 [4096, 128], P(('samp', 'feat')), may hold values from -36 to 36
- coef: float32 [16384, 128], P('feat'), may hold values from -6 to 6
- coef_dual: float32 [16384, 128], P('feat'), may hold values from -3 to 3
- tile_coef_dual: float32 [4, 16384, 128], P('samp', 'feat'), may hold values from -3 to 3
- share: float32 [4096, 128], P(('samp', 'feat')), may hold values from -36 to 36
- share_dual: float32 [4096, 128], P('samp'), may hold values from -6 to 6
- tile_share: float32 [8, 4096, 128], P('feat', 'samp'), may hold values from -6 to 6
Outputs:
- coef_out: float32 [16384, 128], P('feat')
- coef_dual_out: float32 [16384, 128], P('feat')
- tile_coef_dual_out: float32 [4, 16384, 128], P('samp', 'feat')
- share_out: float32 [4096, 128], P(('samp', 'feat'))
- share_dual_out: float32 [4096, 128], P('samp')
- tile_share_out: float32 [8, 4096, 128], P('feat', 'samp')
Inputs may be any that keep to these rules, and one draw needn't show every extreme that they name: `data`: independent entries of mean zero and variance 1 / 3072.
All inputs are finite; a program needn't handle non-finite values.
Results may differ from a plain program's by a relative error of at most 0.0001.
Values sent between devices are 32-bit elements; how exact they have to be, the bound alone decides.
No kernel may reach another device: no remote copies, remote signals or barrier semaphores. Data moves between devices by JAX's collectives and lax.ppermute only.
A program may use at most 64 MiB of HBM per device.

v0:
```python
import jax
import jax.numpy as jnp
from jax import lax
from jax.sharding import PartitionSpec as P

ITERS = 2
CHEB = 5


cheb_low = 1.0
cheb_high = 3.2
l1_weight = 0.2
huber_width = 4.0


def chebyshev(apply_fn, rhs, start):
    theta = (cheb_high + cheb_low) / 2.0
    delta = (cheb_high - cheb_low) / 2.0
    sigma = theta / delta
    iterate = start
    resid = rhs - apply_fn(iterate)
    search = resid / theta
    rho_old = 1.0 / sigma
    for step in range(CHEB):
        iterate = iterate + search
        if step + 1 < CHEB:
            resid = resid - apply_fn(search)
            rho_new = 1.0 / (2.0 * sigma - rho_old)
            search = rho_new * rho_old * search + 2.0 * rho_new / delta * resid
            rho_old = rho_new
    return iterate


def shards(data, targets, coef, coef_dual, tile_coef_dual, share, share_dual, tile_share):
    high = lax.Precision.HIGHEST
    feat_count = lax.axis_size("feat")
    samp_count = lax.axis_size("samp")
    own_rows = share.shape[0]
    feat_index = lax.axis_index("feat")
    tile_dual = tile_coef_dual[0]
    tile_out = tile_share[0]

    def transpose_mul(vector):
        return jnp.einsum("sf,sk->fk", data, vector, precision=high)

    def forward_mul(vector):
        return jnp.dot(data, vector, precision=high)

    def apply_fn(vector):
        return vector + transpose_mul(forward_mul(vector))

    for sweep in range(ITERS):
        value = coef - coef_dual
        half_coef = value - jnp.clip(value, -l1_weight, l1_weight)
        dual_rows = lax.dynamic_slice_in_dim(share_dual, feat_index * own_rows, own_rows, 0)
        resid_t = share - dual_rows - targets
        half_share = targets + resid_t - jnp.clip(resid_t / 2.0, -huber_width, huber_width)
        start = coef - tile_dual
        rhs = start + transpose_mul(tile_out + share_dual)
        proj_coef = chebyshev(apply_fn, rhs, start)
        proj_share = forward_mul(proj_coef)
        summed = lax.psum(proj_coef, "samp")
        coef_new = (half_coef + summed) / (samp_count + 1)
        whole_sum = lax.psum(proj_share, "feat")
        half_all = lax.all_gather(half_share, "feat", axis=0, tiled=True)
        excess = (half_all - whole_sum) / (feat_count + 1)
        excess_own = lax.dynamic_slice_in_dim(excess, feat_index * own_rows, own_rows, 0)
        share = half_share - excess_own
        tile_out = proj_share + excess
        share_dual = share_dual + excess
        coef_dual = coef_dual + half_coef - coef_new
        tile_dual = tile_dual + proj_coef - coef_new
        coef = coef_new
    return (coef, coef_dual, tile_dual[None], share, share_dual, tile_out[None])


def solution(mesh):
    return jax.shard_map(
        shards,
        mesh=mesh,
        in_specs=(
            P("samp", "feat"),
            P(("samp", "feat"), None),
            P("feat", None),
            P("feat", None),
            P("samp", "feat", None),
            P(("samp", "feat"), None),
            P("samp", None),
            P("feat", "samp", None),
        ),
        out_specs=(
            P("feat", None),
            P("feat", None),
            P("samp", "feat", None),
            P(("samp", "feat"), None),
            P("samp", None),
            P("feat", "samp", None),
        ),
        check_vma=False,
    )
```

profile of v0, /device:TPU:0, one launch (start us, length us, event | category | flops | bytes accessed | tf_op | source)
XLA Modules:
  0.0 437.1 jit_solution(12634982800931088488)
XLA Ops:
  10.5 12.6 %fusion.53 = f32[128,1024]{1,0:T(8,128)S(1)} fusion(f32[2048,128]{0,1:T(8,128)S(1)} %bitcast_subtract_fusion, f32[1024,2048]{1,0:T(8,128)} %param.8), kind=kOutput, calls=%fused_computation.89 | convolution fusion | flops 3221225472 | bytes 9961472 | tf_op jit(solution)/shard_map/dot_general | solution.py:47
  32.4 8.8 %fusion.31 = f32[128,1024]{1,0:T(8,128)S(1)} fusion(f32[1024,2048]{1,0:T(8,128)S(1)} %copy-done, f32[2048,128]{0,1:T(8,128)S(1)} %fusion.1), kind=kOutput, calls=%fused_computation.60 | convolution fusion | flops 3221487616 | bytes 9961472 | tf_op jit(solution)/shard_map/dot_general | solution.py:47
  45.8 8.7 %fusion.50 = f32[128,1024]{1,0:T(8,128)S(1)} fusion(f32[1024,2048]{1,0:T(8,128)S(1)} %copy-done, f32[2048,128]{0,1:T(8,128)S(1)} %fusion.4, f32[2048,128]{0,1:T(8,128)S(1)} %fusion.1), kind=kOutput, calls=%fused_computation.86 | convolution fusion | flops 3222011904 | bytes 11010048 | tf_op jit(solution)/shard_map/dot_general | solution.py:47
  54.5 4.8 %multiply_add_fusion.4 = (f32[2048,128]{0,1:T(8,128)S(1)}, f32[2048,128]{0,1:T(8,128)S(1)}) fusion(f32[2048,128]{0,1:T(8,128)S(1)} %fusion.4, f32[2048,128]{0,1:T(8,128)S(1)} %fusion.1, f32[128,1024]{1,0:T(8,128)S(1)} %fusion.50, f32[1024,2048]{1,0:T(8,128)S(1)} %copy-done), kind=kOutput, calls=%fused_computation.56 | convolution fusion | flops 3223322624 | bytes 13107200 | tf_op jit(solution)/shard_map/sf,sk->fk/dot_general | solution.py:44
  59.2 9.2 %fusion.54 = f32[128,1024]{1,0:T(8,128)S(1)} fusion(f32[2048,128]{0,1:T(8,128)S(1)} %get-tuple-element.19, f32[1024,2048]{1,0:T(8,128)S(1)} %copy-done), kind=kOutput, calls=%fused_computation.90 | convolution fusion | flops 3221225472 | bytes 9961472 | tf_op jit(solution)/shard_map/dot_general | solution.py:47
  73.2 8.5 %fusion.33 = f32[128,1024]{1,0:T(8,128)S(1)} fusion(f32[1024,2048]{1,0:T(8,128)S(1)} %copy-done, f32[2048,128]{0,1:T(8,128)S(1)} %fusion.8, f32[2048,128]{0,1:T(8,128)S(1)} %get-tuple-element.19), kind=kOutput, calls=%fused_computation.62 | convolution fusion | flops 3222011904 | bytes 11010048 | tf_op jit(solution)/shard_map/dot_general | solution.py:47
  81.7 5.1 %fusion.13 = f32[2048,128]{0,1:T(8,128)S(1)} fusion(f32[2048,128]{0,1:T(8,128)S(1)} %fusion.8, f32[128,1024]{1,0:T(8,128)S(1)} %fusion.33, f32[1024,2048]{1,0:T(8,128)S(1)} %copy-done, f32[2048,128]{0,1:T(8,128)S(1)} %get-tuple-element.19, f32[2048,128]{0,1:T(8,128)S(1)} %bitcast_subtract_fusion, f32[2048,128]{0,1:T(8,128)S(1)} %fusion.1, ...), kind=kOutput, calls=%fused_computation.25 | convolution fusion | flops 3225681920 | bytes 15204352 | tf_op jit(solution)/shard_map/sf,sk->fk/dot_general | solution.py:44
  86.8 12.2 %convolution_bitcast_fusion.13 = f32[1024,128]{0,1:T(8,128)} fusion(f32[2048,128]{0,1:T(8,128)S(1)} %fusion.13, f32[1024,2048]{1,0:T(8,128)} %param.8), kind=kOutput, calls=%fused_computation.43 | convolution fusion | flops 3221225472 | bytes 9961472 | tf_op jit(solution)/shard_map/dot_general | solution.py:47
  104.6 18.3 %all_gather.6 = f32[1024,128]{0,1:T(8,128)} all-gather(f32[128,128]{0,1:T(8,128)S(1)} %clamp_subtract_fusion.3), channel_id=1, replica_groups=mesh['samp'=4,'feat'=8] {'feat'}, dimensions={0}, use_global_device_ids=true | all-gather | bytes 589824 | tf_op jit(solution)/shard_map/all_gather | solution.py:65
  122.9 35.8 %all-reduce.7.cloned.1.call-done = f32[1024,128]{0,1:T(8,128)} async-done(((f32[1024,128]{0,1:T(8,128)}), f32[1024,128]{0,1:T(8,128)}) %all-reduce.7.cloned.1.call-update) | async-done | bytes 524304 | tf_op jit(solution)/shard_map/psum | solution.py:64
  161.2 53.0 %all-reduce.5.cloned.1.call-done = f32[2048,128]{0,1:T(8,128)} async-done(((f32[2048,128]{0,1:T(8,128)}), f32[2048,128]{0,1:T(8,128)}) %all-reduce.5.cloned.1.call-update) | async-done | bytes 1048592 | tf_op jit(solution)/shard_map/psum | solution.py:62
  216.4 11.7 %fusion.55 = f32[128,1024]{1,0:T(8,128)S(1)} fusion(f32[2048,128]{0,1:T(8,128)S(1)} %fusion.43, f32[1024,2048]{1,0:T(8,128)} %param.8), kind=kOutput, calls=%fused_computation.91 | convolution fusion | flops 3221225472 | bytes 9961472 | tf_op jit(solution)/shard_map/dot_general | solution.py:47
  232.9 4.8 %fusion.15 = f32[2048,128]{0,1:T(8,128)S(1)} fusion(f32[2048,128]{0,1:T(8,128)S(1)} %fusion.16, f32[2048,128]{0,1:T(8,128)S(1)} %fusion.43, f32[1024,2048]{1,0:T(8,128)S(1)} %bitcast.141, f32[1024,128]{0,1:T(8,128)S(1)} %copy-done.4, f32[1024,128]{0,1:T(8,128)S(1)} %copy-done.5, f32[1024,128]{0,1:T(8,128)S(1)} %copy-done.6), kind=kOutput, calls=%fused_computation.27 | convolution fusion | flops 3222011904 | bytes 13107200 | tf_op jit(solution)/shard_map/sf,sk->fk/dot_general | solution.py:44
  237.6 8.8 %fusion.29 = f32[128,1024]{1,0:T(8,128)S(1)} fusion(f32[1024,2048]{1,0:T(8,128)S(1)} %bitcast.141, f32[2048,128]{0,1:T(8,128)S(1)} %fusion.15), kind=kOutput, calls=%fused_computation.58 | convolution fusion | flops 3221487616 | bytes 9961472 | tf_op jit(solution)/shard_map/dot_general | solution.py:47
  251.0 8.7 %fusion.51 = f32[128,1024]{1,0:T(8,128)S(1)} fusion(f32[1024,2048]{1,0:T(8,128)S(1)} %bitcast.141, f32[2048,128]{0,1:T(8,128)S(1)} %fusion.18, f32[2048,128]{0,1:T(8,128)S(1)} %fusion.15), kind=kOutput, calls=%fused_computation.87 | convolution fusion | flops 3222011904 | bytes 11010048 | tf_op jit(solution)/shard_map/dot_general | solution.py:47
  259.7 4.8 %multiply_add_fusion.1 = (f32[2048,128]{0,1:T(8,128)S(1)}, f32[2048,128]{0,1:T(8,128)S(1)}) fusion(f32[2048,128]{0,1:T(8,128)S(1)} %fusion.18, f32[2048,128]{0,1:T(8,128)S(1)} %fusion.15, f32[128,1024]{1,0:T(8,128)S(1)} %fusion.51, f32[1024,2048]{1,0:T(8,128)S(1)} %bitcast.141), kind=kOutput, calls=%fused_computation.51 | convolution fusion | flops 3223322624 | bytes 13107200 | tf_op jit(solution)/shard_map/sf,sk->fk/dot_general | solution.py:44
  264.5 9.2 %fusion.56 = f32[128,1024]{1,0:T(8,128)S(1)} fusion(f32[2048,128]{0,1:T(8,128)S(1)} %get-tuple-element.21, f32[1024,2048]{1,0:T(8,128)S(1)} %bitcast.141), kind=kOutput, calls=%fused_computation.92 | convolution fusion | flops 3221225472 | bytes 9961472 | tf_op jit(solution)/shard_map/dot_general | solution.py:47
  278.4 8.5 %fusion.34 = f32[128,1024]{1,0:T(8,128)S(1)} fusion(f32[1024,2048]{1,0:T(8,128)S(1)} %bitcast.141, f32[2048,128]{0,1:T(8,128)S(1)} %fusion.22, f32[2048,128]{0,1:T(8,128)S(1)} %get-tuple-element.21), kind=kOutput, calls=%fused_computation.63 | convolution fusion | flops 3222011904 | bytes 11010048 | tf_op jit(solution)/shard_map/dot_general | solution.py:47
  286.9 6.1 %fusion.27 = f32[2048,128]{0,1:T(8,128)} fusion(f32[2048,128]{0,1:T(8,128)S(1)} %fusion.22, f32[128,1024]{1,0:T(8,128)S(1)} %fusion.34, f32[1024,2048]{1,0:T(8,128)S(1)} %bitcast.141, f32[2048,128]{0,1:T(8,128)S(1)} %get-tuple-element.21, f32[2048,128]{0,1:T(8,128)S(1)} %fusion.43, f32[2048,128]{0,1:T(8,128)S(1)} %fusion.15, f32[2048,128]{0,1:T(8,128)S(1)} %fusion.18), kind=kOutput, calls=%fused_computation.39 | convolution fusion | flops 3225681920 | bytes 15204352 | tf_op jit(solution)/shard_map/sf,sk->fk/dot_general | solution.py:44
  292.9 13.2 %convolution_bitcast_fusion.12 = f32[1024,128]{0,1:T(8,128)} fusion(f32[2048,128]{0,1:T(8,128)} %fusion.27, f32[1024,2048]{1,0:T(8,128)} %param.8), kind=kOutput, calls=%fused_computation.42 | convolution fusion | flops 3221225472 | bytes 9961472 | tf_op jit(solution)/shard_map/dot_general | solution.py:47
  307.7 16.8 %all_gather.7 = f32[1024,128]{0,1:T(8,128)} all-gather(f32[128,128]{0,1:T(8,128)S(1)} %clamp_subtract_fusion.2), channel_id=1, replica_groups=mesh['samp'=4,'feat'=8] {'feat'}, dimensions={0}, use_global_device_ids=true | all-gather | bytes 589824 | tf_op jit(solution)/shard_map/all_gather | solution.py:65
  324.5 38.5 %all-reduce.11.cloned.1.call-done = f32[1024,128]{0,1:T(8,128)} async-done(((f32[1024,128]{0,1:T(8,128)}), f32[1024,128]{0,1:T(8,128)}) %all-reduce.11.cloned.1.call-update) | async-done | bytes 524304 | tf_op jit(solution)/shard_map/psum | solution.py:64
  373.1 44.9 %all-reduce.9.cloned.1.call-done = f32[2048,128]{0,1:T(8,128)} async-done(((f32[2048,128]{0,1:T(8,128)}), f32[2048,128]{0,1:T(8,128)}) %all-reduce.9.cloned.1.call-update) | async-done | bytes 1048592 | tf_op jit(solution)/shard_map/psum | solution.py:62
  418.0 4.8 %subtract_bitcast_fusion = (f32[1,2048,128]{1,2,0:T(8,128)}, f32[2048,128]{0,1:T(8,128)}, f32[2048,128]{0,1:T(8,128)}) fusion(f32[2048,128]{0,1:T(8,128)} %fusion.27, f32[2048,128]{0,1:T(8,128)S(1)} %copy-done.2, f32[1,2048,128]{1,2,0:T(8,128)S(1)} %copy.16, f32[2048,128]{0,1:T(8,128)} %all-reduce.5.cloned.1.call-done, f32[2048,128]{0,1:T(8,128)S(1)} %copy.14, ...), kind=kLoop, calls=%fused_computation.47 | loop fusion | flops 4718592 | bytes 10485760 | tf_op jit(solution)/shard_map/broadcast_in_dim | solution.py:74
  (62 shorter events, 65.2 us)
Async XLA Ops:
  7.2 151.6 %all-reduce.7.cloned.1.call-start = ((), (), s32[]{:S(2)}) async-start(), calls=%async_computation.1 | async-start | bytes 1048576 | tf_op jit(solution)/shard_map/psum | solution.py:64
  10.3 12.7 %copy-start = (f32[1024,2048]{1,0:T(8,128)S(1)}, f32[1024,2048]{1,0:T(8,128)}, u32[]{:S(2)}) copy-start(f32[1024,2048]{1,0:T(8,128)} %param.8) | copy-start | bytes 25165828
  10.5 17.2 %copy-start.7 = (f32[1024,128]{1,0:T(8,128)S(1)}, f32[1024,128]{1,0:T(8,128)}, u32[]{:S(2)}) copy-start(f32[1024,128]{1,0:T(8,128)} %param.14) | copy-start | bytes 1572868
  10.5 17.2 %copy-start.8 = (f32[1,1024,128]{2,1,0:T(8,128)S(1)}, f32[1,1024,128]{2,1,0:T(8,128)}, u32[]{:S(2)}) copy-start(f32[1,1024,128]{2,1,0:T(8,128)} %param.15) | copy-start | bytes 1572868
  86.8 12.3 %copy-start.1 = (f32[2048,128]{0,1:T(8,128)}, f32[2048,128]{0,1:T(8,128)S(1)}, u32[]{:S(2)}) copy-start(f32[2048,128]{0,1:T(8,128)S(1)} %fusion.13) | copy-start | bytes 3145732
  86.8 15.1 %copy-start.9 = (f32[128,128]{1,0:T(8,128)S(1)}, f32[128,128]{1,0:T(8,128)}, u32[]{:S(2)}) copy-start(f32[128,128]{1,0:T(8,128)} %param.9) | copy-start | bytes 196612
  86.8 15.2 %copy-start.10 = (f32[128,128]{1,0:T(8,128)S(1)}, f32[128,128]{1,0:T(8,128)}, u32[]{:S(2)}) copy-start(f32[128,128]{1,0:T(8,128)} %param.13) | copy-start | bytes 196612
  99.1 115.2 %all-reduce.5.cloned.1.call-start = ((), (), s32[]{:S(2)}) async-start(), calls=%async_computation | async-start | bytes 2097152 | tf_op jit(solution)/shard_map/psum | solution.py:62
  99.8 263.1 %all-reduce.11.cloned.1.call-start = ((), (), s32[]{:S(2)}) async-start(), calls=%async_computation.3 | async-start | bytes 1048576 | tf_op jit(solution)/shard_map/psum | solution.py:64
  103.7 124.5 %copy-start.3 = (f32[2048,128]{0,1:T(8,128)}, f32[2048,128]{0,1:T(8,128)S(1)}, u32[]{:S(2)}) copy-start(f32[2048,128]{0,1:T(8,128)S(1)} %copy.15) | copy-start | bytes 3145732
  214.2 14.0 %slice-start = ((s8[8388608]{0:T(1024)(128)(4,1)}), s8[4194304]{0:T(1024)(128)(4,1)S(1)}, s32[]{:S(2)}) async-start(s8[8388608]{0:T(1024)(128)(4,1)} %bitcast.140), calls=%async_computation.4 | async-start | bytes 8388608
  216.4 11.8 %slice-start.1 = ((s8[8388608]{0:T(1024)(128)(4,1)}), s8[4194304]{0:T(1024)(128)(4,1)S(1)}, s32[]{:S(2)}) async-start(s8[8388608]{0:T(1024)(128)(4,1)} %bitcast.140), calls=%async_computation.5 | async-start | bytes 8388608
  216.4 16.4 %copy-start.4 = (f32[1024,128]{0,1:T(8,128)S(1)}, f32[1024,128]{0,1:T(8,128)}, u32[]{:S(2)}) copy-start(f32[1024,128]{0,1:T(8,128)} %get-tuple-element.14) | copy-start | bytes 1572868
  216.4 16.4 %copy-start.5 = (f32[1024,128]{0,1:T(8,128)S(1)}, f32[1024,128]{0,1:T(8,128)}, u32[]{:S(2)}) copy-start(f32[1024,128]{0,1:T(8,128)} %convolution_bitcast_fusion.13) | copy-start | bytes 1572868
  216.4 16.4 %copy-start.6 = (f32[1024,128]{0,1:T(8,128)S(1)}, f32[1024,128]{0,1:T(8,128)}, u32[]{:S(2)}) copy-start(f32[1024,128]{0,1:T(8,128)} %get-tuple-element.15) | copy-start | bytes 1572868
  292.9 125.0 %copy-start.2 = (f32[2048,128]{0,1:T(8,128)S(1)}, f32[2048,128]{0,1:T(8,128)}, u32[]{:S(2)}) copy-start(f32[2048,128]{0,1:T(8,128)} %copy-done.1) | copy-start | bytes 3145732
  306.2 111.8 %all-reduce.9.cloned.1.call-start = ((), (), s32[]{:S(2)}) async-start(), calls=%async_computation.2 | async-start | bytes 2097152 | tf_op jit(solution)/shard_map/psum | solution.py:62
Sparse Core Ops, SparseCore 0:
  99.2 59.4 all-reduce.6
  162.7 51.5 all-reduce.4
  306.3 56.5 all-reduce.10
  366.4 51.5 all-reduce.8
where the time goes:
time: 441 us; the launch traced here: 437 us
  matrix products  178 us (40%)
  waiting for transfers between devices  173 us (39%)
  blocking collectives  35.1 us (8%)
  local copies, waits for them, and re-layouts  19.3 us (4%)
  other arithmetic  16.8 us (4%)
  between operations  14.4 us (3%)
    dot_general x12, matrix products, forward_mul(): return jnp.dot(data, vector, precision=high)  120 us
    psum x2, waiting for transfers between devices, shards(): summed = lax.psum(proj_coef, 'samp')  97.9 us
    psum x2, waiting for transfers between devices, shards(): whole_sum = lax.psum(proj_share, 'feat')  74.3 us
    dot_general x12, matrix products, transpose_mul(): return jnp.einsum('sf,sk->fk', data, vector, precision=high)  57.8 us
    all_gather x2, blocking collectives, shards(): half_all = lax.all_gather(half_share, 'feat', axis=0, tiled=True)  35.1 us
    unnamed x38, local copies, waits for them, and re-layouts  19.3 us
  transfers between devices with their start and end apart: 4, of which 4 were waited for; matrix products, arithmetic and copies ran while one was open for 4% of the time, Pallas kernels for 0%

commit v1 on v0

v1 whole, which is shorter than its diff:
```python
import functools

import jax
import jax.numpy as jnp
from jax import lax
from jax.experimental import pallas as pl
from jax.experimental.pallas import tpu as pltpu
from jax.sharding import PartitionSpec as P

CHEB = 5

cheb_low = 1.0
cheb_high = 3.2
l1_weight = 0.2
huber_width = 4.0

F32 = jnp.float32
BF16 = jnp.bfloat16
MIB = 1 << 20


def chebyshev_coefs():
    theta = (cheb_high + cheb_low) / 2.0
    delta = (cheb_high - cheb_low) / 2.0
    sigma = theta / delta
    rho = 1.0 / sigma
    pairs = []
    for _ in range(CHEB - 1):
        rho_new = 1.0 / (2.0 * sigma - rho)
        pairs.append((rho_new * rho, 2.0 * rho_new / delta))
        rho = rho_new
    return theta, pairs


def split(value):
    high = value.astype(BF16)
    return high, (value - high.astype(F32)).astype(BF16)


def dot_nn(a, b):
    return jnp.dot(a, b, preferred_element_type=F32)


def dot_nt(a, b):
    return lax.dot_general(a, b, (((1,), (1,)), ((), ())), preferred_element_type=F32)


def prox_coef(value):
    return value - jnp.clip(value, -l1_weight, l1_weight)


def prox_share(share, dual, targets):
    resid = share - dual - targets
    return targets + resid - jnp.clip(resid / 2.0, -huber_width, huber_width)


class Plan:
    def __init__(self, axis, size, order):
        self.axis, self.size, self.order = axis, size, order
        self.levels = len(order) - 1
        self.chunks = 1 << self.levels

    def key(self):
        index = lax.axis_index(self.axis)
        key = 0
        for level in range(self.levels):
            bit = lax.rem(lax.div(index, 1 << self.order[level]), 2)
            key = key + bit * (1 << (self.levels - 1 - level))
        return key

    def place(self, location, key):
        out = 0
        for bit in range(self.levels):
            own = lax.rem(lax.div(key, 1 << bit), 2)
            out = out + ((1 - own) if (location >> bit) & 1 else own) * (1 << bit)
        return out

    def permute(self, value, bit):
        return lax.ppermute(value, self.axis, [(i, i ^ (1 << bit)) for i in range(self.size)])


def butterfly(parts):
    state = [(plan, keep, send) for plan, keep, send in parts]
    rounds = max(plan.levels for plan, _, _ in parts)
    current = [None] * len(state)
    for level in range(rounds):
        for n, (plan, keep, send) in enumerate(state):
            if level >= plan.levels:
                continue
            if level > 0:
                half = current[n].shape[0] // 2
                keep, send = current[n][:half], current[n][half:]
            current[n] = keep + plan.permute(send, plan.order[level])
    for n, (plan, _, _) in enumerate(state):
        current[n] = current[n] + plan.permute(current[n], plan.order[plan.levels])
    halves = [None] * len(state)
    for level in reversed(range(rounds)):
        for n, (plan, _, _) in enumerate(state):
            if level >= plan.levels:
                continue
            other = plan.permute(current[n], plan.order[level])
            halves[n] = (current[n], other)
            if level > 0:
                current[n] = jnp.concatenate([current[n], other], axis=0)
    return halves


class Sizes:
    def __init__(self, mesh_shape, data_shape, cols):
        self.n_samp, self.n_feat = mesh_shape["samp"], mesh_shape["feat"]
        self.rows, self.feats = data_shape
        self.cols = cols
        bits = (self.n_samp - 1).bit_length()
        order = list(range(bits))
        self.colors = [
            Plan("samp", self.n_samp, order[n % bits:] + order[: n % bits]) for n in range(2)
        ]
        self.feat_plan = Plan("feat", self.n_feat, list(range((self.n_feat - 1).bit_length())))
        self.color_rows = self.feats // 2
        self.coef_chunk = self.color_rows // self.colors[0].chunks
        self.share_chunk = self.rows // self.feat_plan.chunks
        self.own = self.rows // self.n_feat
        self.row_block = min(256, self.rows)
        self.feat_block = min(256, self.feats)


def coef_places(sz):
    out = []
    for color, plan in enumerate(sz.colors):
        key = plan.key()
        for location in range(plan.chunks):
            offset = color * sz.color_rows + plan.place(location, key) * sz.coef_chunk
            out.append((color, location, pl.multiple_of(offset, 8)))
    return out


def share_places(sz):
    key = sz.feat_plan.key()
    return [
        (location, pl.multiple_of(sz.feat_plan.place(location, key) * sz.share_chunk, 8))
        for location in range(sz.feat_plan.chunks)
    ]


def half_of(location, chunks, chunk_rows):
    half = chunks // 2
    return location // half, (location % half) * chunk_rows


def chebyshev_steps(sz, g_hi, g_lo, resid, search, search2, total, part):
    theta, pairs = chebyshev_coefs()
    cols, block = sz.cols, sz.row_block
    blocks = sz.rows // block
    search[...] = resid[...] * (1.0 / theta)
    total[...] = search[...]
    high, low = split(search[...])
    search2[:, :cols] = high
    search2[:, cols:] = low
    for step in range(CHEB):
        last = step + 1 == CHEB
        for r in range(blocks):
            rows = pl.ds(r * block, block)
            wide = dot_nn(g_hi[rows, :], search2[...])
            prod = wide[:, :cols] + wide[:, cols:] + dot_nn(g_lo[rows, :], search2[:, :cols])
            if step == 0:
                part[rows, :] = prod
            else:
                part[rows, :] += prod
            if not last:
                c_old, c_res = pairs[step]
                old = search[rows, :]
                res = resid[rows, :] - old - prod
                new = c_old * old + c_res * res
                resid[rows, :] = res
                search[rows, :] = new
                total[rows, :] += new
        if not last:
            high, low = split(search[...])
            search2[:, :cols] = high
            search2[:, cols:] = low


def spread_coef(sz, a_hi, a_lo, start, total, wide_t, proj):
    cols, block = sz.cols, sz.feat_block
    high, low = split(total[...].T)
    wide_t[:cols, :] = high
    wide_t[cols:, :] = low
    for f in range(sz.feats // block):
        columns = pl.ds(f * block, block)
        wide = dot_nn(wide_t[...], a_hi[:, columns])
        out = wide[:cols] + wide[cols:] + dot_nn(wide_t[:cols, :], a_lo[:, columns])
        proj[columns, :] = start[columns, :] + out.T


def emit_coef(sz, proj, keeps, sends):
    for color, location, offset in coef_places(sz):
        which, row = half_of(location, sz.colors[color].chunks, sz.coef_chunk)
        target = (keeps, sends)[which][color]
        target[pl.ds(row, sz.coef_chunk), :] = proj[pl.ds(offset, sz.coef_chunk), :]


def emit_share(sz, proj_share, half_share, scratch, keep, send):
    own = pl.ds(pl.multiple_of(lax.axis_index("feat") * sz.own, 8), sz.own)
    scratch[...] = proj_share[...]
    scratch[own, :] = scratch[own, :] - half_share
    for location, offset in share_places(sz):
        which, row = half_of(location, sz.feat_plan.chunks, sz.share_chunk)
        target = (keep, send)[which]
        target[pl.ds(row, sz.share_chunk), :] = scratch[pl.ds(offset, sz.share_chunk), :]


def first_kernel(sz, data, targets, coef, tile_dual, share, share_dual, tile_share,
                 a_hi_out, a_lo_out, g_hi_out, g_lo_out, keep0, keep1, send0, send1,
                 keep_s, send_s, dual_plus, out_sum, proj_share,
                 a32, a_hi, a_lo, g_hi, g_lo, start, start2, resid, search, search2, total, part,
                 wide_t, proj, in_sem, out_sem):
    cols, block = sz.cols, sz.row_block
    blocks = sz.rows // block
    loads = []
    for r in range(blocks):
        rows = pl.ds(r * block, block)
        copy = pltpu.make_async_copy(data.at[rows, :], a32.at[rows, :], in_sem.at[r])
        copy.start()
        loads.append(copy)
    start[...] = coef[...] - tile_dual[...]
    high, low = split(start[...])
    start2[:, :cols] = high
    start2[:, cols:] = low
    stores = []
    for r in range(blocks):
        rows = pl.ds(r * block, block)
        loads[r].wait()
        high, low = split(a32[rows, :])
        a_hi[rows, :] = high
        a_lo[rows, :] = low
        for n, (src, dst) in enumerate(((a_hi, a_hi_out), (a_lo, a_lo_out))):
            copy = pltpu.make_async_copy(src.at[rows, :], dst.at[rows, :], out_sem.at[2 * r + n])
            copy.start()
            stores.append(copy)
        wide = dot_nn(a_hi[rows, :], start2[...])
        prod = wide[:, :cols] + wide[:, cols:] + dot_nn(a_lo[rows, :], start2[:, :cols])
        proj_share[rows, :] = prod
        resid[rows, :] = tile_share[rows, :] + share_dual[rows, :] - prod
        for c in range(r + 1):
            others = pl.ds(c * block, block)
            gram = dot_nt(a_hi[rows, :], a_hi[others, :])
            cross = dot_nt(a_hi[rows, :], a_lo[others, :])
            if c == r:
                gram = 0.5 * gram + cross
                gram = gram + gram.T
            else:
                gram = gram + cross + dot_nt(a_lo[rows, :], a_hi[others, :])
            high, low = split(gram)
            g_hi[rows, others] = high
            g_lo[rows, others] = low
            if c != r:
                high, low = split(gram.T)
                g_hi[others, rows] = high
                g_lo[others, rows] = low
    for n, (src, dst) in enumerate(((g_hi, g_hi_out), (g_lo, g_lo_out))):
        copy = pltpu.make_async_copy(src, dst, out_sem.at[2 * blocks + n])
        copy.start()
        stores.append(copy)
    chebyshev_steps(sz, g_hi, g_lo, resid, search, search2, total, part)
    spread_coef(sz, a_hi, a_lo, start, total, wide_t, proj)
    emit_coef(sz, proj, (keep0, keep1), (send0, send1))
    dual_plus[...] = tile_dual[...] + proj[...]
    proj_share[...] += part[...]
    out_sum[...] = proj_share[...] + share_dual[...]
    own = pl.ds(pl.multiple_of(lax.axis_index("feat") * sz.own, 8), sz.own)
    half_share = prox_share(share[...], share_dual[own, :], targets[...])
    emit_share(sz, proj_share, half_share, resid, keep_s, send_s)
    for copy in stores:
        copy.wait()


def second_kernel(sz, a_hi_in, a_lo_in, g_hi_in, g_lo_in, sum00, sum01, sum10, sum11,
                  esum0, esum1, coef, coef_dual, dual_plus, out_sum, targets, share, share_dual,
                  keep0, keep1, send0, send1, keep_s, send_s,
                  half_out, coef_plus, tile_plus, half_share_out, share_dual_out, proj_share,
                  a_hi, a_lo, g_hi, g_lo, start, start2, resid, search, search2, total, part,
                  wide_t, proj, in_sem):
    cols, block = sz.cols, sz.row_block
    blocks = sz.rows // block
    loads = []
    for r in range(blocks):
        rows = pl.ds(r * block, block)
        for n, (src, dst) in enumerate(((a_hi_in, a_hi), (a_lo_in, a_lo))):
            copy = pltpu.make_async_copy(src.at[rows, :], dst.at[rows, :], in_sem.at[2 * r + n])
            copy.start()
            loads.append(copy)
    for n, (src, dst) in enumerate(((g_hi_in, g_hi), (g_lo_in, g_lo))):
        copy = pltpu.make_async_copy(src, dst, in_sem.at[2 * blocks + n])
        copy.start()
        loads.append(copy)
    sums = ((sum00, sum01), (sum10, sum11))
    for color, location, offset in coef_places(sz):
        rows = pl.ds(offset, sz.coef_chunk)
        which, row = half_of(location, sz.colors[color].chunks, sz.coef_chunk)
        total_coef = sums[color][which][pl.ds(row, sz.coef_chunk), :]
        dual = coef_dual[rows, :]
        half = prox_coef(coef[rows, :] - dual)
        new = (half + total_coef) / (sz.n_samp + 1)
        dual = dual + half - new
        half = prox_coef(new - dual)
        half_out[rows, :] = half
        coef_plus[rows, :] = dual + half
        tile = dual_plus[rows, :] - new
        tile_plus[rows, :] = tile
        first = new - tile
        start[rows, :] = first
        high, low = split(first)
        start2[rows, :cols] = high
        start2[rows, cols:] = low
    esums = (esum0, esum1)
    for location, offset in share_places(sz):
        rows = pl.ds(offset, sz.share_chunk)
        which, row = half_of(location, sz.feat_plan.chunks, sz.share_chunk)
        excess = esums[which][pl.ds(row, sz.share_chunk), :] * (-1.0 / (sz.n_feat + 1))
        search[rows, :] = excess
        share_dual_out[rows, :] = share_dual[rows, :] + excess
        resid[rows, :] = out_sum[rows, :] + 2.0 * excess
    own = pl.ds(pl.multiple_of(lax.axis_index("feat") * sz.own, 8), sz.own)
    share_now = prox_share(share[...], share_dual[own, :], targets[...]) - search[own, :]
    half_share = prox_share(share_now, share_dual_out[own, :], targets[...])
    half_share_out[...] = half_share
    for r in range(blocks):
        rows = pl.ds(r * block, block)
        loads[2 * r].wait()
        loads[2 * r + 1].wait()
        wide = dot_nn(a_hi[rows, :], start2[...])
        prod = wide[:, :cols] + wide[:, cols:] + dot_nn(a_lo[rows, :], start2[:, :cols])
        proj_share[rows, :] = prod
        resid[rows, :] = resid[rows, :] - prod
    loads[2 * blocks].wait()
    loads[2 * blocks + 1].wait()
    chebyshev_steps(sz, g_hi, g_lo, resid, search, search2, total, part)
    spread_coef(sz, a_hi, a_lo, start, total, wide_t, proj)
    emit_coef(sz, proj, (keep0, keep1), (send0, send1))
    tile_plus[...] += proj[...]
    proj_share[...] += part[...]
    emit_share(sz, proj_share, half_share, resid, keep_s, send_s)


def last_kernel(sz, sum00, sum01, sum10, sum11, esum0, esum1, half_coef, coef_plus, tile_plus,
                half_share, share_dual, proj_share,
                coef_out, coef_dual_out, tile_out, share_out, share_dual_out, tile_share_out):
    sums = ((sum00, sum01), (sum10, sum11))
    for color, location, offset in coef_places(sz):
        rows = pl.ds(offset, sz.coef_chunk)
        which, row = half_of(location, sz.colors[color].chunks, sz.coef_chunk)
        total_coef = sums[color][which][pl.ds(row, sz.coef_chunk), :]
        new = (half_coef[rows, :] + total_coef) / (sz.n_samp + 1)
        coef_out[rows, :] = new
        coef_dual_out[rows, :] = coef_plus[rows, :] - new
        tile_out[rows, :] = tile_plus[rows, :] - new
    esums = (esum0, esum1)
    for location, offset in share_places(sz):
        rows = pl.ds(offset, sz.share_chunk)
        which, row = half_of(location, sz.feat_plan.chunks, sz.share_chunk)
        excess = esums[which][pl.ds(row, sz.share_chunk), :] * (-1.0 / (sz.n_feat + 1))
        share_dual_out[rows, :] = share_dual[rows, :] + excess
        tile_share_out[rows, :] = proj_share[rows, :] + excess
    own = pl.ds(pl.multiple_of(lax.axis_index("feat") * sz.own, 8), sz.own)
    share_out[...] = half_share[...] - (share_dual_out[own, :] - share_dual[own, :])


def shards(mesh_shape, data, targets, coef, coef_dual, tile_coef_dual, share, share_dual, tile_share):
    cols = coef.shape[1]
    sz = Sizes(mesh_shape, data.shape, cols)
    rows, feats = data.shape
    blocks = rows // sz.row_block
    f32 = lambda *shape: jax.ShapeDtypeStruct(shape, F32)
    b16 = lambda *shape: jax.ShapeDtypeStruct(shape, BF16)
    vmem = pl.BlockSpec(memory_space=pltpu.VMEM)
    anyw = pl.BlockSpec(memory_space=pl.ANY)
    v32 = lambda *shape: pltpu.VMEM(shape, F32)
    v16 = lambda *shape: pltpu.VMEM(shape, BF16)
    params = pltpu.CompilerParams(vmem_limit_bytes=56 * MIB)
    flops = 2 * rows * feats * cols

    half_coef_rows = f32(sz.color_rows // 2, cols)
    half_share_rows = f32(rows // 2, cols)
    sends = [half_coef_rows] * 4 + [half_share_rows] * 2
    matrices = [v16(rows, feats)] * 2 + [v16(rows, rows)] * 2
    work = [
        v32(feats, cols), v16(feats, 2 * cols), v32(rows, cols), v32(rows, cols),
        v16(rows, 2 * cols), v32(rows, cols), v32(rows, cols), v16(2 * cols, rows),
        v32(feats, cols),
    ]
    tile_dual = tile_coef_dual[0]

    outs = pl.pallas_call(
        functools.partial(first_kernel, sz),
        out_shape=[b16(rows, feats)] * 2 + [b16(rows, rows)] * 2 + sends
        + [f32(feats, cols), f32(rows, cols), f32(rows, cols)],
        in_specs=[anyw] + [vmem] * 6,
        out_specs=[anyw] * 4 + [vmem] * 9,
        scratch_shapes=[v32(rows, feats)] + matrices + work
        + [pltpu.SemaphoreType.DMA((blocks,)), pltpu.SemaphoreType.DMA((2 * blocks + 2,))],
        compiler_params=params,
        cost_estimate=pl.CostEstimate(flops=30 * flops, bytes_accessed=32 * MIB, transcendentals=0),
        name="first",
    )(data, targets, coef, tile_dual, share, share_dual, tile_share[0])
    mats, (keep0, keep1, send0, send1, keep_s, send_s), (dual_plus, out_sum, _) = (
        outs[:4], outs[4:10], outs[10:])

    def sums(keep0, keep1, send0, send1, keep_s, send_s):
        return butterfly([
            (sz.colors[0], keep0, send0), (sz.colors[1], keep1, send1), (sz.feat_plan, keep_s, send_s)])

    (s00, s01), (s10, s11), (e0, e1) = sums(keep0, keep1, send0, send1, keep_s, send_s)
    outs = pl.pallas_call(
        functools.partial(second_kernel, sz),
        out_shape=sends + [f32(feats, cols)] * 3
        + [f32(sz.own, cols), f32(rows, cols), f32(rows, cols)],
        in_specs=[anyw] * 4 + [vmem] * 13,
        out_specs=[vmem] * 12,
        scratch_shapes=matrices + work + [pltpu.SemaphoreType.DMA((2 * blocks + 2,))],
        compiler_params=params,
        cost_estimate=pl.CostEstimate(flops=14 * flops, bytes_accessed=20 * MIB, transcendentals=0),
        name="second",
    )(*mats, s00, s01, s10, s11, e0, e1, coef, coef_dual, dual_plus, out_sum, targets, share, share_dual)
    half_coef, coef_plus, tile_plus, half_share, dual_now, proj_share = outs[6:]
    (s00, s01), (s10, s11), (e0, e1) = sums(*outs[:6])
    coef_out, coef_dual_out, tile_out, share_out, share_dual_out, tile_share_out = pl.pallas_call(
        functools.partial(last_kernel, sz),
        out_shape=[f32(feats, cols)] * 3 + [f32(sz.own, cols), f32(rows, cols), f32(rows, cols)],
        in_specs=[vmem] * 12,
        out_specs=[vmem] * 6,
        compiler_params=params,
        cost_estimate=pl.CostEstimate(flops=feats * cols * 8, bytes_accessed=10 * MIB, transcendentals=0),
        name="last",
    )(s00, s01, s10, s11, e0, e1, half_coef, coef_plus, tile_plus, half_share, dual_now, proj_share)
    return (coef_out, coef_dual_out, tile_out[None], share_out, share_dual_out, tile_share_out[None])


def solution(mesh):
    mesh_shape = dict(mesh.shape)
    return jax.shard_map(
        functools.partial(shards, mesh_shape),
        mesh=mesh,
        in_specs=(
            P("samp", "feat"),
            P(("samp", "feat"), None),
            P("feat", None),
            P("feat", None),
            P("samp", "feat", None),
            P(("samp", "feat"), None),
            P("samp", None),
            P("feat", "samp", None),
        ),
        out_specs=(
            P("feat", None),
            P("feat", None),
            P("samp", "feat", None),
            P(("samp", "feat"), None),
            P("samp", None),
            P("feat", "samp", None),
        ),
        check_vma=False,
    )
```

time: 441 us -> 114 us (0.26)
  matrix products: 178 us -> 0 us
  waiting for transfers between devices: 173 us -> 31.8 us
  Pallas kernels: 0 us -> 48.7 us
  blocking collectives: 35.1 us -> 0 us
  starting transfers between devices: 0.16 us -> 25.1 us
  local copies, waits for them, and re-layouts: 19.3 us -> 1.56 us
  between operations: 14.4 us -> 0.86 us
  other arithmetic: 16.8 us -> 6.16 us
    dot_general x24 -> x0, matrix products: 178 us -> none  [the longest x12 120 us: forward_mul(): return jnp.dot(data, vector, precision=high)]
    psum x4 -> x0, waiting for transfers between devices: 172 us -> none  [the longest x2 97.9 us: shards(): summed = lax.psum(proj_coef, 'samp')]
    pallas_call x0 -> x3, Pallas kernels: none -> 48.7 us  [the longest x1 26.8 us: shards(): pl.pallas_call(functools.partial(first_kernel, sz), out_shape=[b16(rows,...]
    all_gather x2 -> x0, blocking collectives: 35.1 us -> none  [shards(): half_all = lax.all_gather(half_share, 'feat', axis=0, tiled=True)]
    ppermute x0 -> x22, waiting for transfers between devices: none -> 31.8 us  [permute(): lax.ppermute(value, self.axis, [(i, i ^ 1 << bit) for i in range(self.siz...]
    ppermute x0 -> x22, starting transfers between devices: none -> 25.1 us  [permute(): lax.ppermute(value, self.axis, [(i, i ^ 1 << bit) for i in range(self.siz...]
    unnamed x38 -> x24, local copies, waits for them, and re-layouts: 19.3 us -> 1.54 us
    broadcast_in_dim x2 -> x0, other arithmetic: 7.29 us -> none  [shards(): return (coef, coef_dual, tile_dual[None], share, share_dual, tile_out[None])]
  transfers between devices with their start and end apart: 4 -> 22, of which waited for: 4 -> 10; matrix products, arithmetic and copies ran while one was open for 4% -> 5% of each run, Pallas kernels for 0% -> 0%
where the time goes in v1:
time: 114 us
  Pallas kernels  48.7 us (43%)
  waiting for transfers between devices  31.8 us (28%)
  starting transfers between devices  25.1 us (22%)
  other arithmetic  6.16 us (5%)
  local copies, waits for them, and re-layouts  1.56 us (1%)
    ppermute x22, waiting for transfers between devices, permute(): lax.ppermute(value, self.axis, [(i, i ^ 1 << bit) for i in range(self.siz...  31.8 us
    pallas_call x1, Pallas kernels, shards(): pl.pallas_call(functools.partial(first_kernel, sz), out_shape=[b16(rows,...  26.8 us
    ppermute x22, starting transfers between devices, permute(): lax.ppermute(value, self.axis, [(i, i ^ 1 << bit) for i in range(self.siz...  25.1 us
    pallas_call x1, Pallas kernels, shards(): pl.pallas_call(functools.partial(second_kernel, sz), out_shape=sends + [f...  17 us
    add x8, other arithmetic, butterfly(): current[n] = keep + plan.permute(send, plan.order[level])  5.98 us
    pallas_call x1, Pallas kernels, shards(): pl.pallas_call(functools.partial(last_kernel, sz), out_shape=[f32(feats,...  4.87 us
  transfers between devices with their start and end apart: 22, of which 10 were waited for; matrix products, arithmetic and copies ran while one was open for 5% of the time, Pallas kernels for 0%

profile of v1, /device:TPU:0, one launch (start us, length us, event | category | flops | bytes accessed | tf_op | source)
XLA Modules:
  0.0 114.2 jit_solution(674850779511038241)
XLA Ops:
  0.6 26.8 %first.1 = (bf16[1024,2048]{1,0:T(8,128)(2,1)}, bf16[1024,2048]{1,0:T(8,128)(2,1)}, bf16[1024,1024]{1,0:T(8,128)(2,1)}, bf16[1024,1024]{1,0:T(8,128)(2,1)}, f32[...) custom-call(f32[1024,2048]{1,0:T(8,128)} %data.1, ...), custom_call_target="tpu_custom_call" | custom-call | flops 16106127360 | bytes 33554432 | tf_op jit(solution)/shard_map/first/pallas_call | solution.py:393
  28.0 2.6 %collective-permute-start = (f32[512,128]{1,0:T(8,128)}, f32[512,128]{1,0:T(8,128)S(1)}, u32[]{:S(2)}, u32[]{:S(2)}) collective-permute-start(f32[512,128]{1,0:T(8,128)} %get-tuple-element.41), channel_id=1, source_target_pairs={{0,8},{8,0},{16,24},{24,16},{1,9},{9,1},{17,25},{25,17},{2,10},{10... | collective-permute-start | bytes 786440 | tf_op jit(solution)/shard_map/ppermute | solution.py:79
  30.5 1.5 %collective-permute-start.3 = (f32[512,128]{1,0:T(8,128)}, f32[512,128]{1,0:T(8,128)S(1)}, u32[]{:S(2)}, u32[]{:S(2)}) collective-permute-start(f32[512,128]{1,0:T(8,128)} %get-tuple-element.43), channel_id=1, source_target_pairs={{0,16},{8,24},{16,0},{24,8},{1,17},{9,25},{17,1},{25,9},{2,18},{10... | collective-permute-start | bytes 786440 | tf_op jit(solution)/shard_map/ppermute | solution.py:79
  32.1 1.0 add.46
  33.1 1.6 %collective-permute-start.7 = (f32[256,128]{1,0:T(8,128)S(1)}, f32[256,128]{1,0:T(8,128)S(1)}, u32[]{:S(2)}, u32[]{:S(2)}) collective-permute-start(f32[256,128]{1,0:T(8,128)S(1)} %slice.17), channel_id=1, source_target_pairs={{0,2},{1,3},{2,0},{3,1},{4,6},{5,7},{6,4},{7,5},{8,10},{9,11},{10,... | collective-permute-start | bytes 393224 | tf_op jit(solution)/shard_map/ppermute | solution.py:79
  34.7 2.9 %collective-permute-done = f32[512,128]{1,0:T(8,128)S(1)} collective-permute-done((f32[512,128]{1,0:T(8,128)}, f32[512,128]{1,0:T(8,128)S(1)}, u32[]{:S(2)}, u32[]{:S(2)}) %collective-permute-start) | collective-permute-done | bytes 262176 | tf_op jit(solution)/shard_map/ppermute | solution.py:79
  38.6 1.8 %collective-permute-start.1 = (f32[512,128]{1,0:T(8,128)S(1)}, f32[512,128]{1,0:T(8,128)S(1)}, u32[]{:S(2)}, u32[]{:S(2)}) collective-permute-start(f32[512,128]{1,0:T(8,128)S(1)} %add.42), channel_id=1, source_target_pairs={{0,16},{8,24},{16,0},{24,8},{1,17},{9,25},{17,1},{25,9},{2,18},{10... | collective-permute-start | bytes 786440 | tf_op jit(solution)/shard_map/ppermute | solution.py:79
  40.5 1.0 add.44
  41.5 1.6 %collective-permute-start.4 = (f32[512,128]{1,0:T(8,128)S(1)}, f32[512,128]{1,0:T(8,128)S(1)}, u32[]{:S(2)}, u32[]{:S(2)}) collective-permute-start(f32[512,128]{1,0:T(8,128)S(1)} %add.44), channel_id=1, source_target_pairs={{0,8},{8,0},{16,24},{24,16},{1,9},{9,1},{17,25},{25,17},{2,10},{10... | collective-permute-start | bytes 786440 | tf_op jit(solution)/shard_map/ppermute | solution.py:79
  43.1 2.7 %collective-permute-start.8 = (f32[256,128]{1,0:T(8,128)S(1)}, f32[256,128]{1,0:T(8,128)S(1)}, u32[]{:S(2)}, u32[]{:S(2)}) collective-permute-start(f32[256,128]{1,0:T(8,128)S(1)} %slice_add_fusion.1), channel_id=1, source_target_pairs={{0,4},{1,5},{2,6},{3,7},{4,0},{5,1},{6,2},{7,3},{8,12},{9,13},{10,... | collective-permute-start | bytes 393224 | tf_op jit(solution)/shard_map/ppermute | solution.py:79
  45.7 5.6 %collective-permute-done.8 = f32[256,128]{1,0:T(8,128)S(1)} collective-permute-done((f32[256,128]{1,0:T(8,128)S(1)}, f32[256,128]{1,0:T(8,128)S(1)}, u32[]{:S(2)}, u32[]{:S(2)}) %collective-permute-start.8) | collective-permute-done | bytes 131104 | tf_op jit(solution)/shard_map/ppermute | solution.py:79
  53.4 3.0 %collective-permute-done.9 = f32[256,128]{1,0:T(8,128)S(1)} collective-permute-done((f32[256,128]{1,0:T(8,128)S(1)}, f32[256,128]{1,0:T(8,128)S(1)}, u32[]{:S(2)}, u32[]{:S(2)}) %collective-permute-start.9) | collective-permute-done | bytes 131104 | tf_op jit(solution)/shard_map/ppermute | solution.py:79
  56.5 3.2 %collective-permute-done.2.sum01 = f32[512,128]{1,0:T(8,128)S(1)} collective-permute-done((f32[512,128]{1,0:T(8,128)S(1)}, f32[512,128]{1,0:T(8,128)S(1)}, u32[]{:S(2)}, u32[]{:S(2)}) %collective-permute-start.2) | collective-permute-done | bytes 262176 | tf_op jit(solution)/shard_map/ppermute | solution.py:79
  60.9 17.0 %second.1 = (f32[512,128]{1,0:T(8,128)}, f32[512,128]{1,0:T(8,128)}, f32[512,128]{1,0:T(8,128)}, f32[512,128]{1,0:T(8,128)}, f32[512,128]{1,0:T(8,128)}, /*index...) custom-call(bf16[1024,2048]{1,0:T(8,128)(2,1)} %get-tuple-element.36, ...), custom_call_target="tpu_custom_call" | custom-call | flops 7516192768 | bytes 20971520 | tf_op jit(solution)/shard_map/second/pallas_call | solution.py:413
  78.0 1.6 %collective-permute-start.11 = (f32[512,128]{1,0:T(8,128)}, f32[512,128]{1,0:T(8,128)S(1)}, u32[]{:S(2)}, u32[]{:S(2)}) collective-permute-start(f32[512,128]{1,0:T(8,128)} %get-tuple-element.49), channel_id=1, source_target_pairs={{0,8},{8,0},{16,24},{24,16},{1,9},{9,1},{17,25},{25,17},{2,10},{10... | collective-permute-start | bytes 786440 | tf_op jit(solution)/shard_map/ppermute | solution.py:79
  80.0 1.0 add.53
  81.8 5.1 %collective-permute-done.11 = f32[512,128]{1,0:T(8,128)S(1)} collective-permute-done((f32[512,128]{1,0:T(8,128)}, f32[512,128]{1,0:T(8,128)S(1)}, u32[]{:S(2)}, u32[]{:S(2)}) %collective-permute-start.11) | collective-permute-done | bytes 262176 | tf_op jit(solution)/shard_map/ppermute | solution.py:79
  89.4 1.6 %collective-permute-start.15 = (f32[512,128]{1,0:T(8,128)S(1)}, f32[512,128]{1,0:T(8,128)S(1)}, u32[]{:S(2)}, u32[]{:S(2)}) collective-permute-start(f32[512,128]{1,0:T(8,128)S(1)} %add.51), channel_id=1, source_target_pairs={{0,8},{8,0},{16,24},{24,16},{1,9},{9,1},{17,25},{25,17},{2,10},{10... | collective-permute-start | bytes 786440 | tf_op jit(solution)/shard_map/ppermute | solution.py:79
  91.0 3.4 %collective-permute-start.19 = (f32[256,128]{1,0:T(8,128)S(1)}, f32[256,128]{1,0:T(8,128)S(1)}, u32[]{:S(2)}, u32[]{:S(2)}) collective-permute-start(f32[256,128]{1,0:T(8,128)S(1)} %slice_add_fusion), channel_id=1, source_target_pairs={{0,4},{1,5},{2,6},{3,7},{4,0},{5,1},{6,2},{7,3},{8,12},{9,13},{10,... | collective-permute-start | bytes 393224 | tf_op jit(solution)/shard_map/ppermute | solution.py:79
  94.5 5.3 %collective-permute-done.19 = f32[256,128]{1,0:T(8,128)S(1)} collective-permute-done((f32[256,128]{1,0:T(8,128)S(1)}, f32[256,128]{1,0:T(8,128)S(1)}, u32[]{:S(2)}, u32[]{:S(2)}) %collective-permute-start.19) | collective-permute-done | bytes 131104 | tf_op jit(solution)/shard_map/ppermute | solution.py:79
  100.6 1.6 %collective-permute-start.16 = (f32[512,128]{1,0:T(8,128)S(1)}, f32[512,128]{1,0:T(8,128)S(1)}, u32[]{:S(2)}, u32[]{:S(2)}) collective-permute-start(f32[512,128]{1,0:T(8,128)S(1)} %add.52.sum10), channel_id=1, source_target_pairs={{0,16},{8,24},{16,0},{24,8},{1,17},{9,25},{17,1},{25,9},{2,18},{10... | collective-permute-start | bytes 786440 | tf_op jit(solution)/shard_map/ppermute | solution.py:79
  102.2 3.0 %collective-permute-done.20 = f32[256,128]{1,0:T(8,128)S(1)} collective-permute-done((f32[256,128]{1,0:T(8,128)S(1)}, f32[256,128]{1,0:T(8,128)S(1)}, u32[]{:S(2)}, u32[]{:S(2)}) %collective-permute-start.20) | collective-permute-done | bytes 131104 | tf_op jit(solution)/shard_map/ppermute | solution.py:79
  105.3 2.8 %collective-permute-done.13.sum01 = f32[512,128]{1,0:T(8,128)S(1)} collective-permute-done((f32[512,128]{1,0:T(8,128)S(1)}, f32[512,128]{1,0:T(8,128)S(1)}, u32[]{:S(2)}, u32[]{:S(2)}) %collective-permute-start.13) | collective-permute-done | bytes 262176 | tf_op jit(solution)/shard_map/ppermute | solution.py:79
  109.3 4.9 %last.1 = (f32[2048,128]{1,0:T(8,128)}, f32[2048,128]{1,0:T(8,128)}, f32[2048,128]{1,0:T(8,128)}, f32[128,128]{1,0:T(8,128)}, f32[1024,128]{1,0:T(8,128)}, /*index=5*/f32[1024,128]{1,0:T(8,128)}) custom-call(f32[512,128]{1,0:T(8,128)} %copy-done, f32[512,128]{1,0:T(8,128)} %copy-done.5, f32[512,128]{1,0:T(8,128)} %copy-done.1, f32[512,128]{1,0:T(8,128)} %copy-done.6, ...), custom_call_target="tpu_custom_call" | custom-call | flops 2097152 | bytes 10485760 | tf_op jit(solution)/shard_map/last/pallas_call | solution.py:426
  (65 shorter events, 10.6 us)
Async XLA Ops:
  27.5 4.6 %collective-permute-start.6 = (f32[512,128]{1,0:T(8,128)}, f32[512,128]{1,0:T(8,128)S(1)}, u32[]{:S(2)}, u32[]{:S(2)}) collective-permute-start(f32[512,128]{1,0:T(8,128)} %get-tuple-element.45), channel_id=1, source_target_pairs={{0,1},{1,0},{2,3},{3,2},{4,5},{5,4},{6,7},{7,6},{8,9},{9,8},{10,11... | collective-permute-start | bytes 786440 | tf_op jit(solution)/shard_map/ppermute | solution.py:79
  28.0 9.7 %collective-permute-start = (f32[512,128]{1,0:T(8,128)}, f32[512,128]{1,0:T(8,128)S(1)}, u32[]{:S(2)}, u32[]{:S(2)}) collective-permute-start(f32[512,128]{1,0:T(8,128)} %get-tuple-element.41), channel_id=1, source_target_pairs={{0,8},{8,0},{16,24},{24,16},{1,9},{9,1},{17,25},{25,17},{2,10},{10... | collective-permute-start | bytes 786440 | tf_op jit(solution)/shard_map/ppermute | solution.py:79
  30.5 10.0 %collective-permute-start.3 = (f32[512,128]{1,0:T(8,128)}, f32[512,128]{1,0:T(8,128)S(1)}, u32[]{:S(2)}, u32[]{:S(2)}) collective-permute-start(f32[512,128]{1,0:T(8,128)} %get-tuple-element.43), channel_id=1, source_target_pairs={{0,16},{8,24},{16,0},{24,8},{1,17},{9,25},{17,1},{25,9},{2,18},{10... | collective-permute-start | bytes 786440 | tf_op jit(solution)/shard_map/ppermute | solution.py:79
  33.1 10.0 %collective-permute-start.7 = (f32[256,128]{1,0:T(8,128)S(1)}, f32[256,128]{1,0:T(8,128)S(1)}, u32[]{:S(2)}, u32[]{:S(2)}) collective-permute-start(f32[256,128]{1,0:T(8,128)S(1)} %slice.17), channel_id=1, source_target_pairs={{0,2},{1,3},{2,0},{3,1},{4,6},{5,7},{6,4},{7,5},{8,10},{9,11},{10,... | collective-permute-start | bytes 393224 | tf_op jit(solution)/shard_map/ppermute | solution.py:79
  38.6 13.5 %collective-permute-start.1 = (f32[512,128]{1,0:T(8,128)S(1)}, f32[512,128]{1,0:T(8,128)S(1)}, u32[]{:S(2)}, u32[]{:S(2)}) collective-permute-start(f32[512,128]{1,0:T(8,128)S(1)} %add.42), channel_id=1, source_target_pairs={{0,16},{8,24},{16,0},{24,8},{1,17},{9,25},{17,1},{25,9},{2,18},{10... | collective-permute-start | bytes 786440 | tf_op jit(solution)/shard_map/ppermute | solution.py:79
  41.5 11.3 %collective-permute-start.4 = (f32[512,128]{1,0:T(8,128)S(1)}, f32[512,128]{1,0:T(8,128)S(1)}, u32[]{:S(2)}, u32[]{:S(2)}) collective-permute-start(f32[512,128]{1,0:T(8,128)S(1)} %add.44), channel_id=1, source_target_pairs={{0,8},{8,0},{16,24},{24,16},{1,9},{9,1},{17,25},{25,17},{2,10},{10... | collective-permute-start | bytes 786440 | tf_op jit(solution)/shard_map/ppermute | solution.py:79
  43.1 8.3 %collective-permute-start.8 = (f32[256,128]{1,0:T(8,128)S(1)}, f32[256,128]{1,0:T(8,128)S(1)}, u32[]{:S(2)}, u32[]{:S(2)}) collective-permute-start(f32[256,128]{1,0:T(8,128)S(1)} %slice_add_fusion.1), channel_id=1, source_target_pairs={{0,4},{1,5},{2,6},{3,7},{4,0},{5,1},{6,2},{7,3},{8,12},{9,13},{10,... | collective-permute-start | bytes 393224 | tf_op jit(solution)/shard_map/ppermute | solution.py:79
  51.4 5.0 %collective-permute-start.9 = (f32[256,128]{1,0:T(8,128)S(1)}, f32[256,128]{1,0:T(8,128)S(1)}, u32[]{:S(2)}, u32[]{:S(2)}) collective-permute-start(f32[256,128]{1,0:T(8,128)S(1)} %add.48), channel_id=1, source_target_pairs={{0,2},{1,3},{2,0},{3,1},{4,6},{5,7},{6,4},{7,5},{8,10},{9,11},{10,... | collective-permute-start | bytes 393224 | tf_op jit(solution)/shard_map/ppermute | solution.py:79
  52.1 8.0 %copy-start.3 = (f32[512,128]{1,0:T(8,128)}, f32[512,128]{1,0:T(8,128)S(1)}, u32[]{:S(2)}) copy-start(f32[512,128]{1,0:T(8,128)S(1)} %add.43.sum00) | copy-start | bytes 786436
  52.1 7.6 %collective-permute-start.2 = (f32[512,128]{1,0:T(8,128)S(1)}, f32[512,128]{1,0:T(8,128)S(1)}, u32[]{:S(2)}, u32[]{:S(2)}) collective-permute-start(f32[512,128]{1,0:T(8,128)S(1)} %add.43.sum00), channel_id=1, source_target_pairs={{0,8},{8,0},{16,24},{24,16},{1,9},{9,1},{17,25},{25,17},{2,10},{10... | collective-permute-start | bytes 786440 | tf_op jit(solution)/shard_map/ppermute | solution.py:79
  52.8 7.3 %collective-permute-start.5 = (f32[512,128]{1,0:T(8,128)S(1)}, f32[512,128]{1,0:T(8,128)S(1)}, u32[]{:S(2)}, u32[]{:S(2)}) collective-permute-start(f32[512,128]{1,0:T(8,128)S(1)} %add.45.sum10), channel_id=1, source_target_pairs={{0,16},{8,24},{16,0},{24,8},{1,17},{9,25},{17,1},{25,9},{2,18},{10... | collective-permute-start | bytes 786440 | tf_op jit(solution)/shard_map/ppermute | solution.py:79
  56.4 3.7 %collective-permute-start.10 = (f32[512,128]{1,0:T(8,128)S(1)}, f32[512,128]{1,0:T(8,128)S(1)}, u32[]{:S(2)}, u32[]{:S(2)}) collective-permute-start(f32[512,128]{1,0:T(8,128)S(1)} %pad_maximum_fusion.esum0), channel_id=1, source_target_pairs={{0,1},{1,0},{2,3},{3,2},{4,5},{5,4},{6,7},{7,6},{8,9},{9,8},{10,11... | collective-permute-start | bytes 786440 | tf_op jit(solution)/shard_map/ppermute | solution.py:79
  77.9 2.1 %collective-permute-start.17 = (f32[512,128]{1,0:T(8,128)}, f32[512,128]{1,0:T(8,128)S(1)}, u32[]{:S(2)}, u32[]{:S(2)}) collective-permute-start(f32[512,128]{1,0:T(8,128)} %get-tuple-element.53), channel_id=1, source_target_pairs={{0,1},{1,0},{2,3},{3,2},{4,5},{5,4},{6,7},{7,6},{8,9},{9,8},{10,11... | collective-permute-start | bytes 786440 | tf_op jit(solution)/shard_map/ppermute | solution.py:79
  78.0 8.9 %collective-permute-start.11 = (f32[512,128]{1,0:T(8,128)}, f32[512,128]{1,0:T(8,128)S(1)}, u32[]{:S(2)}, u32[]{:S(2)}) collective-permute-start(f32[512,128]{1,0:T(8,128)} %get-tuple-element.49), channel_id=1, source_target_pairs={{0,8},{8,0},{16,24},{24,16},{1,9},{9,1},{17,25},{25,17},{2,10},{10... | collective-permute-start | bytes 786440 | tf_op jit(solution)/shard_map/ppermute | solution.py:79
  79.5 8.9 %collective-permute-start.14 = (f32[512,128]{1,0:T(8,128)}, f32[512,128]{1,0:T(8,128)S(1)}, u32[]{:S(2)}, u32[]{:S(2)}) collective-permute-start(f32[512,128]{1,0:T(8,128)} %get-tuple-element.51), channel_id=1, source_target_pairs={{0,16},{8,24},{16,0},{24,8},{1,17},{9,25},{17,1},{25,9},{2,18},{10... | collective-permute-start | bytes 786440 | tf_op jit(solution)/shard_map/ppermute | solution.py:79
  81.0 10.0 %collective-permute-start.18 = (f32[256,128]{1,0:T(8,128)S(1)}, f32[256,128]{1,0:T(8,128)S(1)}, u32[]{:S(2)}, u32[]{:S(2)}) collective-permute-start(f32[256,128]{1,0:T(8,128)S(1)} %slice.19), channel_id=1, source_target_pairs={{0,2},{1,3},{2,0},{3,1},{4,6},{5,7},{6,4},{7,5},{8,10},{9,11},{10,... | collective-permute-start | bytes 393224 | tf_op jit(solution)/shard_map/ppermute | solution.py:79
  87.9 12.0 %collective-permute-start.12 = (f32[512,128]{1,0:T(8,128)S(1)}, f32[512,128]{1,0:T(8,128)S(1)}, u32[]{:S(2)}, u32[]{:S(2)}) collective-permute-start(f32[512,128]{1,0:T(8,128)S(1)} %add.49), channel_id=1, source_target_pairs={{0,16},{8,24},{16,0},{24,8},{1,17},{9,25},{17,1},{25,9},{2,18},{10... | collective-permute-start | bytes 786440 | tf_op jit(solution)/shard_map/ppermute | solution.py:79
  89.4 11.1 %collective-permute-start.15 = (f32[512,128]{1,0:T(8,128)S(1)}, f32[512,128]{1,0:T(8,128)S(1)}, u32[]{:S(2)}, u32[]{:S(2)}) collective-permute-start(f32[512,128]{1,0:T(8,128)S(1)} %add.51), channel_id=1, source_target_pairs={{0,8},{8,0},{16,24},{24,16},{1,9},{9,1},{17,25},{25,17},{2,10},{10... | collective-permute-start | bytes 786440 | tf_op jit(solution)/shard_map/ppermute | solution.py:79
  91.0 8.8 %collective-permute-start.19 = (f32[256,128]{1,0:T(8,128)S(1)}, f32[256,128]{1,0:T(8,128)S(1)}, u32[]{:S(2)}, u32[]{:S(2)}) collective-permute-start(f32[256,128]{1,0:T(8,128)S(1)} %slice_add_fusion), channel_id=1, source_target_pairs={{0,4},{1,5},{2,6},{3,7},{4,0},{5,1},{6,2},{7,3},{8,12},{9,13},{10,... | collective-permute-start | bytes 393224 | tf_op jit(solution)/shard_map/ppermute | solution.py:79
  99.8 5.4 %collective-permute-start.20 = (f32[256,128]{1,0:T(8,128)S(1)}, f32[256,128]{1,0:T(8,128)S(1)}, u32[]{:S(2)}, u32[]{:S(2)}) collective-permute-start(f32[256,128]{1,0:T(8,128)S(1)} %add.55), channel_id=1, source_target_pairs={{0,2},{1,3},{2,0},{3,1},{4,6},{5,7},{6,4},{7,5},{8,10},{9,11},{10,... | collective-permute-start | bytes 393224 | tf_op jit(solution)/shard_map/ppermute | solution.py:79
  99.9 8.6 %copy-start = (f32[512,128]{1,0:T(8,128)}, f32[512,128]{1,0:T(8,128)S(1)}, u32[]{:S(2)}) copy-start(f32[512,128]{1,0:T(8,128)S(1)} %add.50.sum00) | copy-start | bytes 786436
  99.9 8.2 %collective-permute-start.13 = (f32[512,128]{1,0:T(8,128)S(1)}, f32[512,128]{1,0:T(8,128)S(1)}, u32[]{:S(2)}, u32[]{:S(2)}) collective-permute-start(f32[512,128]{1,0:T(8,128)S(1)} %add.50.sum00), channel_id=1, source_target_pairs={{0,8},{8,0},{16,24},{24,16},{1,9},{9,1},{17,25},{25,17},{2,10},{10... | collective-permute-start | bytes 786440 | tf_op jit(solution)/shard_map/ppermute | solution.py:79
  100.6 7.9 %collective-permute-start.16 = (f32[512,128]{1,0:T(8,128)S(1)}, f32[512,128]{1,0:T(8,128)S(1)}, u32[]{:S(2)}, u32[]{:S(2)}) collective-permute-start(f32[512,128]{1,0:T(8,128)S(1)} %add.52.sum10), channel_id=1, source_target_pairs={{0,16},{8,24},{16,0},{24,8},{1,17},{9,25},{17,1},{25,9},{2,18},{10... | collective-permute-start | bytes 786440 | tf_op jit(solution)/shard_map/ppermute | solution.py:79
  105.2 3.3 %collective-permute-start.21 = (f32[512,128]{1,0:T(8,128)S(1)}, f32[512,128]{1,0:T(8,128)S(1)}, u32[]{:S(2)}, u32[]{:S(2)}) collective-permute-start(f32[512,128]{1,0:T(8,128)S(1)} %pad_maximum_fusion.1.esum0), channel_id=1, source_target_pairs={{0,1},{1,0},{2,3},{3,2},{4,5},{5,4},{6,7},{7,6},{8,9},{9,8},{10,11... | collective-permute-start | bytes 786440 | tf_op jit(solution)/shard_map/ppermute | solution.py:79
  (10 other events, 26.7 us)

commit v2 on v1

--- a/solution.py
+++ b/solution.py
@@ -17,6 +17,7 @@
 F32 = jnp.float32
 BF16 = jnp.bfloat16
 MIB = 1 << 20
+LIMIT = 16
 
 
 def chebyshev_coefs():
@@ -147,21 +148,37 @@
     return location // half, (location % half) * chunk_rows
 
 
+def put_split(target, rows, cols, value):
+    high, low = split(value)
+    target[rows, :cols] = high
+    target[rows, cols:] = low
+
+
+def put_wide(wide_t, cols, value):
+    high, low = split(value.T)
+    wide_t[:cols, :] = high
+    wide_t[cols:, :] = low
+
+
+def triple(a_hi, a_lo, rows, value2, cols):
+    wide = dot_nn(a_hi[rows, :], value2[...])
+    return wide[:, :cols] + wide[:, cols:] + dot_nn(a_lo[rows, :], value2[:, :cols])
+
+
 def chebyshev_steps(sz, g_hi, g_lo, resid, search, search2, total, part):
     theta, pairs = chebyshev_coefs()
     cols, block = sz.cols, sz.row_block
-    blocks = sz.rows // block
-    search[...] = resid[...] * (1.0 / theta)
-    total[...] = search[...]
-    high, low = split(search[...])
-    search2[:, :cols] = high
-    search2[:, cols:] = low
+    blocks = [pl.ds(r * block, block) for r in range(sz.rows // block)]
+    for rows in blocks:
+        first = resid[rows, :] * (1.0 / theta)
+        search[rows, :] = first
+        total[rows, :] = first
+        put_split(search2.at[0], rows, cols, first)
     for step in range(CHEB):
         last = step + 1 == CHEB
-        for r in range(blocks):
-            rows = pl.ds(r * block, block)
-            wide = dot_nn(g_hi[rows, :], search2[...])
-            prod = wide[:, :cols] + wide[:, cols:] + dot_nn(g_lo[rows, :], search2[:, :cols])
+        now, later = search2.at[step % 2], search2.at[(step + 1) % 2]
+        for rows in blocks:
+            prod = triple(g_hi, g_lo, rows, now, cols)
             if step == 0:
                 part[rows, :] = prod
             else:
@@ -174,22 +191,19 @@
                 resid[rows, :] = res
                 search[rows, :] = new
                 total[rows, :] += new
-        if not last:
-            high, low = split(search[...])
-            search2[:, :cols] = high
-            search2[:, cols:] = low
-
-
-def spread_coef(sz, a_hi, a_lo, start, total, wide_t, proj):
+                put_split(later, rows, cols, new)
+
+
+def spread_kernel(sz, wide_t, a_hi, a_lo, start, dual, keep0, keep1, send0, send1, plus, proj):
     cols, block = sz.cols, sz.feat_block
-    high, low = split(total[...].T)
-    wide_t[:cols, :] = high
-    wide_t[cols:, :] = low
     for f in range(sz.feats // block):
         columns = pl.ds(f * block, block)
         wide = dot_nn(wide_t[...], a_hi[:, columns])
         out = wide[:cols] + wide[cols:] + dot_nn(wide_t[:cols, :], a_lo[:, columns])
-        proj[columns, :] = start[columns, :] + out.T
+        value = start[columns, :] + out.T
+        proj[columns, :] = value
+        plus[columns, :] = dual[columns, :] + value
+    emit_coef(sz, proj, (keep0, keep1), (send0, send1))
 
 
 def emit_coef(sz, proj, keeps, sends):
@@ -199,9 +213,8 @@
         target[pl.ds(row, sz.coef_chunk), :] = proj[pl.ds(offset, sz.coef_chunk), :]
 
 
-def emit_share(sz, proj_share, half_share, scratch, keep, send):
+def emit_share(sz, scratch, half_share, keep, send):
     own = pl.ds(pl.multiple_of(lax.axis_index("feat") * sz.own, 8), sz.own)
-    scratch[...] = proj_share[...]
     scratch[own, :] = scratch[own, :] - half_share
     for location, offset in share_places(sz):
         which, row = half_of(location, sz.feat_plan.chunks, sz.share_chunk)
@@ -209,11 +222,9 @@
         target[pl.ds(row, sz.share_chunk), :] = scratch[pl.ds(offset, sz.share_chunk), :]
 
 
-def first_kernel(sz, data, targets, coef, tile_dual, share, share_dual, tile_share,
-                 a_hi_out, a_lo_out, g_hi_out, g_lo_out, keep0, keep1, send0, send1,
-                 keep_s, send_s, dual_plus, out_sum, proj_share,
-                 a32, a_hi, a_lo, g_hi, g_lo, start, start2, resid, search, search2, total, part,
-                 wide_t, proj, in_sem, out_sem):
+def first_kernel(sz, data, coef, tile_dual, share, share_dual, targets, tile_share,
+                 a_hi, a_lo, g_hi, g_lo, start, wide_t, keep_s, send_s, out_sum,
+                 a32, start2, resid, search, search2, total, part, in_sem):
     cols, block = sz.cols, sz.row_block
     blocks = sz.rows // block
     loads = []
@@ -222,24 +233,17 @@
         copy = pltpu.make_async_copy(data.at[rows, :], a32.at[rows, :], in_sem.at[r])
         copy.start()
         loads.append(copy)
-    start[...] = coef[...] - tile_dual[...]
-    high, low = split(start[...])
-    start2[:, :cols] = high
-    start2[:, cols:] = low
-    stores = []
+    first = coef[...] - tile_dual[...]
+    start[...] = first
+    put_split(start2, slice(None), cols, first)
     for r in range(blocks):
         rows = pl.ds(r * block, block)
         loads[r].wait()
         high, low = split(a32[rows, :])
         a_hi[rows, :] = high
         a_lo[rows, :] = low
-        for n, (src, dst) in enumerate(((a_hi, a_hi_out), (a_lo, a_lo_out))):
-            copy = pltpu.make_async_copy(src.at[rows, :], dst.at[rows, :], out_sem.at[2 * r + n])
-            copy.start()
-            stores.append(copy)
-        wide = dot_nn(a_hi[rows, :], start2[...])
-        prod = wide[:, :cols] + wide[:, cols:] + dot_nn(a_lo[rows, :], start2[:, :cols])
-        proj_share[rows, :] = prod
+        prod = triple(a_hi, a_lo, rows, start2, cols)
+        out_sum[rows, :] = prod
         resid[rows, :] = tile_share[rows, :] + share_dual[rows, :] - prod
         for c in range(r + 1):
             others = pl.ds(c * block, block)
@@ -257,42 +261,21 @@
                 high, low = split(gram.T)
                 g_hi[others, rows] = high
                 g_lo[others, rows] = low
-    for n, (src, dst) in enumerate(((g_hi, g_hi_out), (g_lo, g_lo_out))):
-        copy = pltpu.make_async_copy(src, dst, out_sem.at[2 * blocks + n])
-        copy.start()
-        stores.append(copy)
     chebyshev_steps(sz, g_hi, g_lo, resid, search, search2, total, part)
-    spread_coef(sz, a_hi, a_lo, start, total, wide_t, proj)
-    emit_coef(sz, proj, (keep0, keep1), (send0, send1))
-    dual_plus[...] = tile_dual[...] + proj[...]
-    proj_share[...] += part[...]
-    out_sum[...] = proj_share[...] + share_dual[...]
+    put_wide(wide_t, cols, total[...])
+    part[...] += out_sum[...]
+    out_sum[...] = part[...] + share_dual[...]
     own = pl.ds(pl.multiple_of(lax.axis_index("feat") * sz.own, 8), sz.own)
     half_share = prox_share(share[...], share_dual[own, :], targets[...])
-    emit_share(sz, proj_share, half_share, resid, keep_s, send_s)
-    for copy in stores:
-        copy.wait()
-
-
-def second_kernel(sz, a_hi_in, a_lo_in, g_hi_in, g_lo_in, sum00, sum01, sum10, sum11,
+    emit_share(sz, part, half_share, keep_s, send_s)
+
+
+def second_kernel(sz, a_hi, a_lo, g_hi, g_lo, sum00, sum01, sum10, sum11,
                   esum0, esum1, coef, coef_dual, dual_plus, out_sum, targets, share, share_dual,
-                  keep0, keep1, send0, send1, keep_s, send_s,
-                  half_out, coef_plus, tile_plus, half_share_out, share_dual_out, proj_share,
-                  a_hi, a_lo, g_hi, g_lo, start, start2, resid, search, search2, total, part,
-                  wide_t, proj, in_sem):
+                  start, tile_now, half_out, coef_plus, wide_t, keep_s, send_s,
+                  half_share_out, share_dual_out, proj_share,
+                  start2, resid, search, search2, total, part):
     cols, block = sz.cols, sz.row_block
-    blocks = sz.rows // block
-    loads = []
-    for r in range(blocks):
-        rows = pl.ds(r * block, block)
-        for n, (src, dst) in enumerate(((a_hi_in, a_hi), (a_lo_in, a_lo))):
-            copy = pltpu.make_async_copy(src.at[rows, :], dst.at[rows, :], in_sem.at[2 * r + n])
-            copy.start()
-            loads.append(copy)
-    for n, (src, dst) in enumerate(((g_hi_in, g_hi), (g_lo_in, g_lo))):
-        copy = pltpu.make_async_copy(src, dst, in_sem.at[2 * blocks + n])
-        copy.start()
-        loads.append(copy)
     sums = ((sum00, sum01), (sum10, sum11))
     for color, location, offset in coef_places(sz):
         rows = pl.ds(offset, sz.coef_chunk)
@@ -306,12 +289,10 @@
         half_out[rows, :] = half
         coef_plus[rows, :] = dual + half
         tile = dual_plus[rows, :] - new
-        tile_plus[rows, :] = tile
+        tile_now[rows, :] = tile
         first = new - tile
         start[rows, :] = first
-        high, low = split(first)
-        start2[rows, :cols] = high
-        start2[rows, cols:] = low
+        put_split(start2, rows, cols, first)
     esums = (esum0, esum1)
     for location, offset in share_places(sz):
         rows = pl.ds(offset, sz.share_chunk)
@@ -324,22 +305,16 @@
     share_now = prox_share(share[...], share_dual[own, :], targets[...]) - search[own, :]
     half_share = prox_share(share_now, share_dual_out[own, :], targets[...])
     half_share_out[...] = half_share
-    for r in range(blocks):
+    for r in range(sz.rows // block):
         rows = pl.ds(r * block, block)
-        loads[2 * r].wait()
-        loads[2 * r + 1].wait()
-        wide = dot_nn(a_hi[rows, :], start2[...])
-        prod = wide[:, :cols] + wide[:, cols:] + dot_nn(a_lo[rows, :], start2[:, :cols])
+        prod = triple(a_hi, a_lo, rows, start2, cols)
         proj_share[rows, :] = prod
         resid[rows, :] = resid[rows, :] - prod
-    loads[2 * blocks].wait()
-    loads[2 * blocks + 1].wait()
     chebyshev_steps(sz, g_hi, g_lo, resid, search, search2, total, part)
-    spread_coef(sz, a_hi, a_lo, start, total, wide_t, proj)
-    emit_coef(sz, proj, (keep0, keep1), (send0, send1))
-    tile_plus[...] += proj[...]
-    proj_share[...] += part[...]
-    emit_share(sz, proj_share, half_share, resid, keep_s, send_s)
+    put_wide(wide_t, cols, total[...])
+    part[...] += proj_share[...]
+    proj_share[...] = part[...]
+    emit_share(sz, part, half_share, keep_s, send_s)
 
 
 def last_kernel(sz, sum00, sum01, sum10, sum11, esum0, esum1, half_coef, coef_plus, tile_plus,
@@ -371,67 +346,61 @@
     rows, feats = data.shape
     blocks = rows // sz.row_block
     f32 = lambda *shape: jax.ShapeDtypeStruct(shape, F32)
-    b16 = lambda *shape: jax.ShapeDtypeStruct(shape, BF16)
-    vmem = pl.BlockSpec(memory_space=pltpu.VMEM)
-    anyw = pl.BlockSpec(memory_space=pl.ANY)
     v32 = lambda *shape: pltpu.VMEM(shape, F32)
     v16 = lambda *shape: pltpu.VMEM(shape, BF16)
-    params = pltpu.CompilerParams(vmem_limit_bytes=56 * MIB)
     flops = 2 * rows * feats * cols
 
-    half_coef_rows = f32(sz.color_rows // 2, cols)
-    half_share_rows = f32(rows // 2, cols)
-    sends = [half_coef_rows] * 4 + [half_share_rows] * 2
+    def kernel(body, name, outs, scratch, work, limit, *operands, streamed=0):
+        vmem = pl.BlockSpec(memory_space=pltpu.VMEM)
+        hbm = pl.BlockSpec(memory_space=pltpu.HBM)
+        return pl.pallas_call(
+            functools.partial(body, sz),
+            out_shape=outs,
+            in_specs=[hbm] * streamed + [vmem] * (len(operands) - streamed),
+            out_specs=[vmem] * len(outs),
+            scratch_shapes=scratch,
+            compiler_params=pltpu.CompilerParams(vmem_limit_bytes=limit * MIB),
+            cost_estimate=pl.CostEstimate(flops=work, bytes_accessed=8 * MIB, transcendentals=0),
+            name=name,
+        )(*operands)
+
+    coef_sends = [v32(sz.color_rows // 2, cols)] * 4
+    share_sends = [v32(rows // 2, cols)] * 2
     matrices = [v16(rows, feats)] * 2 + [v16(rows, rows)] * 2
-    work = [
-        v32(feats, cols), v16(feats, 2 * cols), v32(rows, cols), v32(rows, cols),
-        v16(rows, 2 * cols), v32(rows, cols), v32(rows, cols), v16(2 * cols, rows),
-        v32(feats, cols),
-    ]
+    vector = v32(rows, cols)
+    wide_t = v16(2 * cols, rows)
+    work = [v16(feats, 2 * cols), vector, vector, v16(2, rows, 2 * cols), vector, vector]
     tile_dual = tile_coef_dual[0]
 
-    outs = pl.pallas_call(
-        functools.partial(first_kernel, sz),
-        out_shape=[b16(rows, feats)] * 2 + [b16(rows, rows)] * 2 + sends
-        + [f32(feats, cols), f32(rows, cols), f32(rows, cols)],
-        in_specs=[anyw] + [vmem] * 6,
-        out_specs=[anyw] * 4 + [vmem] * 9,
-        scratch_shapes=[v32(rows, feats)] + matrices + work
-        + [pltpu.SemaphoreType.DMA((blocks,)), pltpu.SemaphoreType.DMA((2 * blocks + 2,))],
-        compiler_params=params,
-        cost_estimate=pl.CostEstimate(flops=30 * flops, bytes_accessed=32 * MIB, transcendentals=0),
-        name="first",
-    )(data, targets, coef, tile_dual, share, share_dual, tile_share[0])
-    mats, (keep0, keep1, send0, send1, keep_s, send_s), (dual_plus, out_sum, _) = (
-        outs[:4], outs[4:10], outs[10:])
+    def spread(wide, a_hi, a_lo, start, dual):
+        return kernel(
+            spread_kernel, "spread", coef_sends + [v32(feats, cols)], [v32(feats, cols)], 3 * flops, LIMIT,
+            wide, a_hi, a_lo, start, dual)
 
     def sums(keep0, keep1, send0, send1, keep_s, send_s):
         return butterfly([
             (sz.colors[0], keep0, send0), (sz.colors[1], keep1, send1), (sz.feat_plan, keep_s, send_s)])
 
-    (s00, s01), (s10, s11), (e0, e1) = sums(keep0, keep1, send0, send1, keep_s, send_s)
-    outs = pl.pallas_call(
-        functools.partial(second_kernel, sz),
-        out_shape=sends + [f32(feats, cols)] * 3
-        + [f32(sz.own, cols), f32(rows, cols), f32(rows, cols)],
-        in_specs=[anyw] * 4 + [vmem] * 13,
-        out_specs=[vmem] * 12,
-        scratch_shapes=matrices + work + [pltpu.SemaphoreType.DMA((2 * blocks + 2,))],
-        compiler_params=params,
-        cost_estimate=pl.CostEstimate(flops=14 * flops, bytes_accessed=20 * MIB, transcendentals=0),
-        name="second",
-    )(*mats, s00, s01, s10, s11, e0, e1, coef, coef_dual, dual_plus, out_sum, targets, share, share_dual)
-    half_coef, coef_plus, tile_plus, half_share, dual_now, proj_share = outs[6:]
-    (s00, s01), (s10, s11), (e0, e1) = sums(*outs[:6])
-    coef_out, coef_dual_out, tile_out, share_out, share_dual_out, tile_share_out = pl.pallas_call(
-        functools.partial(last_kernel, sz),
-        out_shape=[f32(feats, cols)] * 3 + [f32(sz.own, cols), f32(rows, cols), f32(rows, cols)],
-        in_specs=[vmem] * 12,
-        out_specs=[vmem] * 6,
-        compiler_params=params,
-        cost_estimate=pl.CostEstimate(flops=feats * cols * 8, bytes_accessed=10 * MIB, transcendentals=0),
-        name="last",
-    )(s00, s01, s10, s11, e0, e1, half_coef, coef_plus, tile_plus, half_share, dual_now, proj_share)
+    a_hi, a_lo, g_hi, g_lo, start, wide, keep_s, send_s, out_sum = kernel(
+        first_kernel, "first", matrices + [v32(feats, cols), wide_t] + share_sends + [vector],
+        [v32(rows, feats)] + work + [pltpu.SemaphoreType.DMA((blocks,))], 30 * flops, LIMIT,
+        data, coef, tile_dual, share, share_dual, targets, tile_share[0], streamed=1)
+    *parts, dual_plus = spread(wide, a_hi, a_lo, start, tile_dual)
+    (s00, s01), (s10, s11), (e0, e1) = sums(*parts, keep_s, send_s)
+    (start, tile_now, half_coef, coef_plus, wide, keep_s, send_s, half_share, dual_now,
+     proj_share) = kernel(
+        second_kernel, "second",
+        [v32(feats, cols)] * 4 + [wide_t] + share_sends + [v32(sz.own, cols), vector, vector],
+        work, 11 * flops, LIMIT,
+        a_hi, a_lo, g_hi, g_lo, s00, s01, s10, s11, e0, e1, coef, coef_dual, dual_plus, out_sum,
+        targets, share, share_dual)
+    *parts, tile_plus = spread(wide, a_hi, a_lo, start, tile_now)
+    (s00, s01), (s10, s11), (e0, e1) = sums(*parts, keep_s, send_s)
+    coef_out, coef_dual_out, tile_out, share_out, share_dual_out, tile_share_out = kernel(
+        last_kernel, "last",
+        [f32(feats, cols)] * 3 + [f32(sz.own, cols), f32(rows, cols), f32(rows, cols)],
+        [], flops // 100, LIMIT,
+        s00, s01, s10, s11, e0, e1, half_coef, coef_plus, tile_plus, half_share, dual_now, proj_share)
     return (coef_out, coef_dual_out, tile_out[None], share_out, share_dual_out, tile_share_out[None])
 
 

time: 114 us -> 104 us (0.912)
  Pallas kernels: 48.7 us -> 33 us
  local copies, waits for them, and re-layouts: 1.56 us -> 9.63 us
  other arithmetic: 6.16 us -> 0.39 us
  waiting for transfers between devices: 31.8 us -> 33.7 us
    pallas_call x3 -> x5, Pallas kernels: 48.7 us -> 33 us  [kernel(): pl.pallas_call(functools.partial(body, sz), out_shape=outs, in_specs=[hbm...]
    unnamed x24, local copies, waits for them, and re-layouts: 1.54 us -> 9.61 us
    add x8, other arithmetic: 5.98 us -> 0.2 us  [butterfly(): current[n] = keep + plan.permute(send, plan.order[level])]
    ppermute x22, waiting for transfers between devices: 31.8 us -> 33.7 us  [permute(): lax.ppermute(value, self.axis, [(i, i ^ 1 << bit) for i in range(self.siz...]
  transfers between devices with their start and end apart: 22 -> 22, of which waited for: 10 -> 11; matrix products, arithmetic and copies ran while one was open for 5% -> 0% of each run, Pallas kernels for 0% -> 4%
where the time goes in v2:
time: 104 us; the launch traced here: 103 us
  waiting for transfers between devices  33.7 us (32%)
  Pallas kernels  33 us (32%)
  starting transfers between devices  25.6 us (25%)
  local copies, waits for them, and re-layouts  9.63 us (9%)
    ppermute x22, waiting for transfers between devices, permute(): lax.ppermute(value, self.axis, [(i, i ^ 1 << bit) for i in range(self.siz...  33.7 us
    pallas_call x5, Pallas kernels, kernel(): pl.pallas_call(functools.partial(body, sz), out_shape=outs, in_specs=[hbm...  33 us
    ppermute x22, starting transfers between devices, permute(): lax.ppermute(value, self.axis, [(i, i ^ 1 << bit) for i in range(self.siz...  25.6 us
    unnamed x24, local copies, waits for them, and re-layouts  9.61 us
  transfers between devices with their start and end apart: 22, of which 11 were waited for; matrix products, arithmetic and copies ran while one was open for 0% of the time, Pallas kernels for 4%

profile of v2, /device:TPU:0, one launch (start us, length us, event | category | flops | bytes accessed | tf_op | source)
XLA Modules:
  0.0 103.1 jit_solution(3767265182015850420)
XLA Ops:
  0.6 1.2 %copy-done = f32[1,2048,128]{2,1,0:T(8,128)S(1)} copy-done((f32[1,2048,128]{2,1,0:T(8,128)S(1)}, f32[1,2048,128]{2,1,0:T(8,128)}, u32[]{:S(2)}) %copy-start) | copy-done | bytes 1048600
  1.9 3.4 %copy-done.2 = f32[1024,2048]{1,0:T(8,128)S(1)} copy-done((f32[1024,2048]{1,0:T(8,128)S(1)}, f32[1024,2048]{1,0:T(8,128)}, u32[]{:S(2)}) %copy-start.2) | copy-done | bytes 8388632
  5.2 1.2 %copy-done.3 = f32[2048,128]{1,0:T(8,128)S(1)} copy-done((f32[2048,128]{1,0:T(8,128)S(1)}, f32[2048,128]{1,0:T(8,128)}, u32[]{:S(2)}) %copy-start.3) | copy-done | bytes 1048600
  10.2 17.6 %first.1 = (bf16[1024,2048]{1,0:T(8,128)(2,1)S(1)}, bf16[1024,2048]{1,0:T(8,128)(2,1)S(1)}, bf16[1024,1024]{1,0:T(8,128)(2,1)S(1)}, bf16[1024,1024]{1,0:T(8,128)...) custom-call(f32[1024,2048]{1,0:T(8,128)S(1)} %copy-done.2, ...), custom_call_target="tpu_custom_call" | custom-call | flops 16106127360 | bytes 8388608 | tf_op jit(solution)/shard_map/first/pallas_call | solution.py:356
  28.4 2.1 %spread.2 = (f32[512,128]{1,0:T(8,128)S(1)}, f32[512,128]{1,0:T(8,128)S(1)}, f32[512,128]{1,0:T(8,128)S(1)}, f32[512,128]{1,0:T(8,128)S(1)}, f32[2048,128]{1,0:T(8,128)S(1)}) custom-call(bf16[256,1024]{1,0:T(8,128)(2,1)S(1)} %get-tuple-element.45.wide_t, bf16[1024,2048]{1,0:T(8,128)(2,1)S(1)} %get-tuple-element.41.a_hi, ...), custom_call_target="tpu_custom_call" | custom-call | flops 1610612736 | bytes 8388608 | tf_op jit(solution)/shard_map/spread/pallas_call | solution.py:356
  30.5 2.6 %collective-permute-start = (f32[512,128]{1,0:T(8,128)S(1)}, f32[512,128]{1,0:T(8,128)S(1)}, u32[]{:S(2)}, u32[]{:S(2)}) collective-permute-start(f32[512,128]{1,0:T(8,128)S(1)} %get-tuple-element.48), channel_id=1, source_target_pairs={{0,8},{8,0},{16,24},{24,16},{1,9},{9,1},{17,25},{25,17},{2,10},{10... | collective-permute-start | bytes 786440 | tf_op jit(solution)/shard_map/ppermute | solution.py:80
  33.1 1.5 %collective-permute-start.3 = (f32[512,128]{1,0:T(8,128)S(1)}, f32[512,128]{1,0:T(8,128)S(1)}, u32[]{:S(2)}, u32[]{:S(2)}) collective-permute-start(f32[512,128]{1,0:T(8,128)S(1)} %get-tuple-element.50), channel_id=1, source_target_pairs={{0,16},{8,24},{16,0},{24,8},{1,17},{9,25},{17,1},{25,9},{2,18},{10... | collective-permute-start | bytes 786440 | tf_op jit(solution)/shard_map/ppermute | solution.py:80
  34.7 1.6 %collective-permute-start.7 = (f32[256,128]{1,0:T(8,128)S(1)}, f32[256,128]{1,0:T(8,128)S(1)}, u32[]{:S(2)}, u32[]{:S(2)}) collective-permute-start(f32[256,128]{1,0:T(8,128)S(1)} %slice.17), channel_id=1, source_target_pairs={{0,2},{1,3},{2,0},{3,1},{4,6},{5,7},{6,4},{7,5},{8,10},{9,11},{10,... | collective-permute-start | bytes 393224 | tf_op jit(solution)/shard_map/ppermute | solution.py:80
  36.3 3.7 %collective-permute-done = f32[512,128]{1,0:T(8,128)S(1)} collective-permute-done((f32[512,128]{1,0:T(8,128)S(1)}, f32[512,128]{1,0:T(8,128)S(1)}, u32[]{:S(2)}, u32[]{:S(2)}) %collective-permute-start) | collective-permute-done | bytes 262176 | tf_op jit(solution)/shard_map/ppermute | solution.py:80
  40.1 1.8 %collective-permute-start.1 = (f32[512,128]{1,0:T(8,128)S(1)}, f32[512,128]{1,0:T(8,128)S(1)}, u32[]{:S(2)}, u32[]{:S(2)}) collective-permute-start(f32[512,128]{1,0:T(8,128)S(1)} %add.42), channel_id=1, source_target_pairs={{0,16},{8,24},{16,0},{24,8},{1,17},{9,25},{17,1},{25,9},{2,18},{10... | collective-permute-start | bytes 786440 | tf_op jit(solution)/shard_map/ppermute | solution.py:80
  42.0 1.6 %collective-permute-start.4 = (f32[512,128]{1,0:T(8,128)S(1)}, f32[512,128]{1,0:T(8,128)S(1)}, u32[]{:S(2)}, u32[]{:S(2)}) collective-permute-start(f32[512,128]{1,0:T(8,128)S(1)} %add.44), channel_id=1, source_target_pairs={{0,8},{8,0},{16,24},{24,16},{1,9},{9,1},{17,25},{25,17},{2,10},{10... | collective-permute-start | bytes 786440 | tf_op jit(solution)/shard_map/ppermute | solution.py:80
  43.6 2.7 %collective-permute-start.8 = (f32[256,128]{1,0:T(8,128)S(1)}, f32[256,128]{1,0:T(8,128)S(1)}, u32[]{:S(2)}, u32[]{:S(2)}) collective-permute-start(f32[256,128]{1,0:T(8,128)S(1)} %slice_add_fusion.1), channel_id=1, source_target_pairs={{0,4},{1,5},{2,6},{3,7},{4,0},{5,1},{6,2},{7,3},{8,12},{9,13},{10,... | collective-permute-start | bytes 393224 | tf_op jit(solution)/shard_map/ppermute | solution.py:80
  46.2 5.7 %collective-permute-done.8 = f32[256,128]{1,0:T(8,128)S(1)} collective-permute-done((f32[256,128]{1,0:T(8,128)S(1)}, f32[256,128]{1,0:T(8,128)S(1)}, u32[]{:S(2)}, u32[]{:S(2)}) %collective-permute-start.8) | collective-permute-done | bytes 131104 | tf_op jit(solution)/shard_map/ppermute | solution.py:80
  54.4 2.5 %collective-permute-done.9 = f32[256,128]{1,0:T(8,128)S(1)} collective-permute-done((f32[256,128]{1,0:T(8,128)S(1)}, f32[256,128]{1,0:T(8,128)S(1)}, u32[]{:S(2)}, u32[]{:S(2)}) %collective-permute-start.9) | collective-permute-done | bytes 131104 | tf_op jit(solution)/shard_map/ppermute | solution.py:80
  57.0 3.2 %collective-permute-done.2.sum01 = f32[512,128]{1,0:T(8,128)S(1)} collective-permute-done((f32[512,128]{1,0:T(8,128)S(1)}, f32[512,128]{1,0:T(8,128)S(1)}, u32[]{:S(2)}, u32[]{:S(2)}) %collective-permute-start.2) | collective-permute-done | bytes 262176 | tf_op jit(solution)/shard_map/ppermute | solution.py:80
  60.7 8.9 %second.1 = (f32[2048,128]{1,0:T(8,128)S(1)}, f32[2048,128]{1,0:T(8,128)S(1)}, f32[2048,128]{1,0:T(8,128)S(1)}, f32[2048,128]{1,0:T(8,128)S(1)}, bf16[256,1024]{...) custom-call(bf16[1024,2048]{1,0:T(8,128)(2,1)S(1)} %get-tuple-elemen, ...), custom_call_target="tpu_custom_call" | custom-call | flops 5905580032 | bytes 8388608 | tf_op jit(solution)/shard_map/second/pallas_call | solution.py:356
  69.7 2.1 %spread.3 = (f32[512,128]{1,0:T(8,128)S(1)}, f32[512,128]{1,0:T(8,128)S(1)}, f32[512,128]{1,0:T(8,128)S(1)}, f32[512,128]{1,0:T(8,128)S(1)}, f32[2048,128]{1,0:T(8,128)S(1)}) custom-call(bf16[256,1024]{1,0:T(8,128)(2,1)S(1)} %get-tuple-element.55.wide_t, bf16[1024,2048]{1,0:T(8,128)(2,1)S(1)} %get-tuple-element.41.a_hi, ...), custom_call_target="tpu_custom_call" | custom-call | flops 1610612736 | bytes 8388608 | tf_op jit(solution)/shard_map/spread/pallas_call | solution.py:356
  71.8 1.6 %collective-permute-start.11 = (f32[512,128]{1,0:T(8,128)S(1)}, f32[512,128]{1,0:T(8,128)S(1)}, u32[]{:S(2)}, u32[]{:S(2)}) collective-permute-start(f32[512,128]{1,0:T(8,128)S(1)} %get-tuple-element.59), channel_id=1, source_target_pairs={{0,8},{8,0},{16,24},{24,16},{1,9},{9,1},{17,25},{25,17},{2,10},{10... | collective-permute-start | bytes 786440 | tf_op jit(solution)/shard_map/ppermute | solution.py:80
  74.7 5.9 %collective-permute-done.11 = f32[512,128]{1,0:T(8,128)S(1)} collective-permute-done((f32[512,128]{1,0:T(8,128)S(1)}, f32[512,128]{1,0:T(8,128)S(1)}, u32[]{:S(2)}, u32[]{:S(2)}) %collective-permute-start.11) | collective-permute-done | bytes 262176 | tf_op jit(solution)/shard_map/ppermute | solution.py:80
  82.8 3.5 %collective-permute-start.19 = (f32[256,128]{1,0:T(8,128)S(1)}, f32[256,128]{1,0:T(8,128)S(1)}, u32[]{:S(2)}, u32[]{:S(2)}) collective-permute-start(f32[256,128]{1,0:T(8,128)S(1)} %slice_add_fusion), channel_id=1, source_target_pairs={{0,4},{1,5},{2,6},{3,7},{4,0},{5,1},{6,2},{7,3},{8,12},{9,13},{10,... | collective-permute-start | bytes 393224 | tf_op jit(solution)/shard_map/ppermute | solution.py:80
  86.3 5.4 %collective-permute-done.19 = f32[256,128]{1,0:T(8,128)S(1)} collective-permute-done((f32[256,128]{1,0:T(8,128)S(1)}, f32[256,128]{1,0:T(8,128)S(1)}, u32[]{:S(2)}, u32[]{:S(2)}) %collective-permute-start.19) | collective-permute-done | bytes 131104 | tf_op jit(solution)/shard_map/ppermute | solution.py:80
  94.0 3.2 %collective-permute-done.20 = f32[256,128]{1,0:T(8,128)S(1)} collective-permute-done((f32[256,128]{1,0:T(8,128)S(1)}, f32[256,128]{1,0:T(8,128)S(1)}, u32[]{:S(2)}, u32[]{:S(2)}) %collective-permute-start.20) | collective-permute-done | bytes 131104 | tf_op jit(solution)/shard_map/ppermute | solution.py:80
  97.2 2.8 %collective-permute-done.13.sum01 = f32[512,128]{1,0:T(8,128)S(1)} collective-permute-done((f32[512,128]{1,0:T(8,128)S(1)}, f32[512,128]{1,0:T(8,128)S(1)}, u32[]{:S(2)}, u32[]{:S(2)}) %collective-permute-start.13) | collective-permute-done | bytes 262176 | tf_op jit(solution)/shard_map/ppermute | solution.py:80
  100.9 2.2 %last.1 = (f32[2048,128]{1,0:T(8,128)}, f32[2048,128]{1,0:T(8,128)}, f32[2048,128]{1,0:T(8,128)}, f32[128,128]{1,0:T(8,128)}, f32[1024,128]{1,0:T(8,128)}, /*index=5*/f32[1024,128]{1,0:T(8,128)}) custom-call(f32[512,128]{1,0:T(8,128)S(1)} %add.50.sum00, f32[512,128]{1,0:T(8,128)S(1)} %collective-permute-done.13.sum01, f32[512,128]{1,0:T(8,128)S(1)} %add.52.sum10, ...), custom_call_target="tpu_custom_call" | custom-call | flops 5368709 | bytes 8388608 | tf_op jit(solution)/shard_map/last/pallas_call | solution.py:356
  (67 shorter events, 14.3 us)
Async XLA Ops:
  27.9 6.8 %collective-permute-start.6 = (f32[512,128]{1,0:T(8,128)S(1)}, f32[512,128]{1,0:T(8,128)S(1)}, u32[]{:S(2)}, u32[]{:S(2)}) collective-permute-start(f32[512,128]{1,0:T(8,128)S(1)} %get-tuple-element.52), channel_id=1, source_target_pairs={{0,1},{1,0},{2,3},{3,2},{4,5},{5,4},{6,7},{7,6},{8,9},{9,8},{10,11... | collective-permute-start | bytes 786440 | tf_op jit(solution)/shard_map/ppermute | solution.py:80
  30.5 30.2 %copy-start.4 = (f32[2048,128]{1,0:T(8,128)S(1)}, f32[2048,128]{1,0:T(8,128)}, u32[]{:S(2)}) copy-start(f32[2048,128]{1,0:T(8,128)} %coef_dual.1) | copy-start | bytes 3145732
  30.5 30.2 %copy-start.7 = (f32[1024,128]{1,0:T(8,128)S(1)}, f32[1024,128]{1,0:T(8,128)}, u32[]{:S(2)}) copy-start(f32[1024,128]{1,0:T(8,128)} %share_dual.3) | copy-start | bytes 1572868
  30.5 9.5 %collective-permute-start = (f32[512,128]{1,0:T(8,128)S(1)}, f32[512,128]{1,0:T(8,128)S(1)}, u32[]{:S(2)}, u32[]{:S(2)}) collective-permute-start(f32[512,128]{1,0:T(8,128)S(1)} %get-tuple-element.48), channel_id=1, source_target_pairs={{0,8},{8,0},{16,24},{24,16},{1,9},{9,1},{17,25},{25,17},{2,10},{10... | collective-permute-start | bytes 786440 | tf_op jit(solution)/shard_map/ppermute | solution.py:80
  33.1 8.8 %collective-permute-start.3 = (f32[512,128]{1,0:T(8,128)S(1)}, f32[512,128]{1,0:T(8,128)S(1)}, u32[]{:S(2)}, u32[]{:S(2)}) collective-permute-start(f32[512,128]{1,0:T(8,128)S(1)} %get-tuple-element.50), channel_id=1, source_target_pairs={{0,16},{8,24},{16,0},{24,8},{1,17},{9,25},{17,1},{25,9},{2,18},{10... | collective-permute-start | bytes 786440 | tf_op jit(solution)/shard_map/ppermute | solution.py:80
  34.7 8.8 %collective-permute-start.7 = (f32[256,128]{1,0:T(8,128)S(1)}, f32[256,128]{1,0:T(8,128)S(1)}, u32[]{:S(2)}, u32[]{:S(2)}) collective-permute-start(f32[256,128]{1,0:T(8,128)S(1)} %slice.17), channel_id=1, source_target_pairs={{0,2},{1,3},{2,0},{3,1},{4,6},{5,7},{6,4},{7,5},{8,10},{9,11},{10,... | collective-permute-start | bytes 393224 | tf_op jit(solution)/shard_map/ppermute | solution.py:80
  40.1 12.5 %collective-permute-start.1 = (f32[512,128]{1,0:T(8,128)S(1)}, f32[512,128]{1,0:T(8,128)S(1)}, u32[]{:S(2)}, u32[]{:S(2)}) collective-permute-start(f32[512,128]{1,0:T(8,128)S(1)} %add.42), channel_id=1, source_target_pairs={{0,16},{8,24},{16,0},{24,8},{1,17},{9,25},{17,1},{25,9},{2,18},{10... | collective-permute-start | bytes 786440 | tf_op jit(solution)/shard_map/ppermute | solution.py:80
  42.0 11.3 %collective-permute-start.4 = (f32[512,128]{1,0:T(8,128)S(1)}, f32[512,128]{1,0:T(8,128)S(1)}, u32[]{:S(2)}, u32[]{:S(2)}) collective-permute-start(f32[512,128]{1,0:T(8,128)S(1)} %add.44), channel_id=1, source_target_pairs={{0,8},{8,0},{16,24},{24,16},{1,9},{9,1},{17,25},{25,17},{2,10},{10... | collective-permute-start | bytes 786440 | tf_op jit(solution)/shard_map/ppermute | solution.py:80
  43.6 8.3 %collective-permute-start.8 = (f32[256,128]{1,0:T(8,128)S(1)}, f32[256,128]{1,0:T(8,128)S(1)}, u32[]{:S(2)}, u32[]{:S(2)}) collective-permute-start(f32[256,128]{1,0:T(8,128)S(1)} %slice_add_fusion.1), channel_id=1, source_target_pairs={{0,4},{1,5},{2,6},{3,7},{4,0},{5,1},{6,2},{7,3},{8,12},{9,13},{10,... | collective-permute-start | bytes 393224 | tf_op jit(solution)/shard_map/ppermute | solution.py:80
  51.9 5.0 %collective-permute-start.9 = (f32[256,128]{1,0:T(8,128)S(1)}, f32[256,128]{1,0:T(8,128)S(1)}, u32[]{:S(2)}, u32[]{:S(2)}) collective-permute-start(f32[256,128]{1,0:T(8,128)S(1)} %add.48), channel_id=1, source_target_pairs={{0,2},{1,3},{2,0},{3,1},{4,6},{5,7},{6,4},{7,5},{8,10},{9,11},{10,... | collective-permute-start | bytes 393224 | tf_op jit(solution)/shard_map/ppermute | solution.py:80
  52.7 7.6 %collective-permute-start.2 = (f32[512,128]{1,0:T(8,128)S(1)}, f32[512,128]{1,0:T(8,128)S(1)}, u32[]{:S(2)}, u32[]{:S(2)}) collective-permute-start(f32[512,128]{1,0:T(8,128)S(1)} %add.43.sum00), channel_id=1, source_target_pairs={{0,8},{8,0},{16,24},{24,16},{1,9},{9,1},{17,25},{25,17},{2,10},{10... | collective-permute-start | bytes 786440 | tf_op jit(solution)/shard_map/ppermute | solution.py:80
  53.3 7.3 %collective-permute-start.5 = (f32[512,128]{1,0:T(8,128)S(1)}, f32[512,128]{1,0:T(8,128)S(1)}, u32[]{:S(2)}, u32[]{:S(2)}) collective-permute-start(f32[512,128]{1,0:T(8,128)S(1)} %add.45.sum10), channel_id=1, source_target_pairs={{0,16},{8,24},{16,0},{24,8},{1,17},{9,25},{17,1},{25,9},{2,18},{10... | collective-permute-start | bytes 786440 | tf_op jit(solution)/shard_map/ppermute | solution.py:80
  57.0 3.7 %collective-permute-start.10 = (f32[512,128]{1,0:T(8,128)S(1)}, f32[512,128]{1,0:T(8,128)S(1)}, u32[]{:S(2)}, u32[]{:S(2)}) collective-permute-start(f32[512,128]{1,0:T(8,128)S(1)} %pad_maximum_fusion.esum0), channel_id=1, source_target_pairs={{0,1},{1,0},{2,3},{3,2},{4,5},{5,4},{6,7},{7,6},{8,9},{9,8},{10,11... | collective-permute-start | bytes 786440 | tf_op jit(solution)/shard_map/ppermute | solution.py:80
  69.6 4.3 %collective-permute-start.17 = (f32[512,128]{1,0:T(8,128)S(1)}, f32[512,128]{1,0:T(8,128)S(1)}, u32[]{:S(2)}, u32[]{:S(2)}) collective-permute-start(f32[512,128]{1,0:T(8,128)S(1)} %get-tuple-element.63), channel_id=1, source_target_pairs={{0,1},{1,0},{2,3},{3,2},{4,5},{5,4},{6,7},{7,6},{8,9},{9,8},{10,11... | collective-permute-start | bytes 786440 | tf_op jit(solution)/shard_map/ppermute | solution.py:80
  71.8 8.8 %collective-permute-start.11 = (f32[512,128]{1,0:T(8,128)S(1)}, f32[512,128]{1,0:T(8,128)S(1)}, u32[]{:S(2)}, u32[]{:S(2)}) collective-permute-start(f32[512,128]{1,0:T(8,128)S(1)} %get-tuple-element.59), channel_id=1, source_target_pairs={{0,8},{8,0},{16,24},{24,16},{1,9},{9,1},{17,25},{25,17},{2,10},{10... | collective-permute-start | bytes 786440 | tf_op jit(solution)/shard_map/ppermute | solution.py:80
  73.3 8.4 %collective-permute-start.14 = (f32[512,128]{1,0:T(8,128)S(1)}, f32[512,128]{1,0:T(8,128)S(1)}, u32[]{:S(2)}, u32[]{:S(2)}) collective-permute-start(f32[512,128]{1,0:T(8,128)S(1)} %get-tuple-element.61), channel_id=1, source_target_pairs={{0,16},{8,24},{16,0},{24,8},{1,17},{9,25},{17,1},{25,9},{2,18},{10... | collective-permute-start | bytes 786440 | tf_op jit(solution)/shard_map/ppermute | solution.py:80
  74.0 8.9 %collective-permute-start.18 = (f32[256,128]{1,0:T(8,128)S(1)}, f32[256,128]{1,0:T(8,128)S(1)}, u32[]{:S(2)}, u32[]{:S(2)}) collective-permute-start(f32[256,128]{1,0:T(8,128)S(1)} %slice.19), channel_id=1, source_target_pairs={{0,2},{1,3},{2,0},{3,1},{4,6},{5,7},{6,4},{7,5},{8,10},{9,11},{10,... | collective-permute-start | bytes 393224 | tf_op jit(solution)/shard_map/ppermute | solution.py:80
  80.6 11.2 %collective-permute-start.12 = (f32[512,128]{1,0:T(8,128)S(1)}, f32[512,128]{1,0:T(8,128)S(1)}, u32[]{:S(2)}, u32[]{:S(2)}) collective-permute-start(f32[512,128]{1,0:T(8,128)S(1)} %add.49), channel_id=1, source_target_pairs={{0,16},{8,24},{16,0},{24,8},{1,17},{9,25},{17,1},{25,9},{2,18},{10... | collective-permute-start | bytes 786440 | tf_op jit(solution)/shard_map/ppermute | solution.py:80
  81.8 11.1 %collective-permute-start.15 = (f32[512,128]{1,0:T(8,128)S(1)}, f32[512,128]{1,0:T(8,128)S(1)}, u32[]{:S(2)}, u32[]{:S(2)}) collective-permute-start(f32[512,128]{1,0:T(8,128)S(1)} %add.51), channel_id=1, source_target_pairs={{0,8},{8,0},{16,24},{24,16},{1,9},{9,1},{17,25},{25,17},{2,10},{10... | collective-permute-start | bytes 786440 | tf_op jit(solution)/shard_map/ppermute | solution.py:80
  82.8 8.8 %collective-permute-start.19 = (f32[256,128]{1,0:T(8,128)S(1)}, f32[256,128]{1,0:T(8,128)S(1)}, u32[]{:S(2)}, u32[]{:S(2)}) collective-permute-start(f32[256,128]{1,0:T(8,128)S(1)} %slice_add_fusion), channel_id=1, source_target_pairs={{0,4},{1,5},{2,6},{3,7},{4,0},{5,1},{6,2},{7,3},{8,12},{9,13},{10,... | collective-permute-start | bytes 393224 | tf_op jit(solution)/shard_map/ppermute | solution.py:80
  91.7 5.5 %collective-permute-start.20 = (f32[256,128]{1,0:T(8,128)S(1)}, f32[256,128]{1,0:T(8,128)S(1)}, u32[]{:S(2)}, u32[]{:S(2)}) collective-permute-start(f32[256,128]{1,0:T(8,128)S(1)} %add.55), channel_id=1, source_target_pairs={{0,2},{1,3},{2,0},{3,1},{4,6},{5,7},{6,4},{7,5},{8,10},{9,11},{10,... | collective-permute-start | bytes 393224 | tf_op jit(solution)/shard_map/ppermute | solution.py:80
  91.8 8.3 %collective-permute-start.13 = (f32[512,128]{1,0:T(8,128)S(1)}, f32[512,128]{1,0:T(8,128)S(1)}, u32[]{:S(2)}, u32[]{:S(2)}) collective-permute-start(f32[512,128]{1,0:T(8,128)S(1)} %add.50.sum00), channel_id=1, source_target_pairs={{0,8},{8,0},{16,24},{24,16},{1,9},{9,1},{17,25},{25,17},{2,10},{10... | collective-permute-start | bytes 786440 | tf_op jit(solution)/shard_map/ppermute | solution.py:80
  93.0 7.9 %collective-permute-start.16 = (f32[512,128]{1,0:T(8,128)S(1)}, f32[512,128]{1,0:T(8,128)S(1)}, u32[]{:S(2)}, u32[]{:S(2)}) collective-permute-start(f32[512,128]{1,0:T(8,128)S(1)} %add.52.sum10), channel_id=1, source_target_pairs={{0,16},{8,24},{16,0},{24,8},{1,17},{9,25},{17,1},{25,9},{2,18},{10... | collective-permute-start | bytes 786440 | tf_op jit(solution)/shard_map/ppermute | solution.py:80
  97.2 3.7 %collective-permute-start.21 = (f32[512,128]{1,0:T(8,128)S(1)}, f32[512,128]{1,0:T(8,128)S(1)}, u32[]{:S(2)}, u32[]{:S(2)}) collective-permute-start(f32[512,128]{1,0:T(8,128)S(1)} %pad_maximum_fusion.1.esum0), channel_id=1, source_target_pairs={{0,1},{1,0},{2,3},{3,2},{4,5},{5,4},{6,7},{7,6},{8,9},{9,8},{10,11... | collective-permute-start | bytes 786440 | tf_op jit(solution)/shard_map/ppermute | solution.py:80
  (10 other events, 88.1 us)

commit v3 on v2

--- a/solution.py
+++ b/solution.py
@@ -18,6 +18,7 @@
 BF16 = jnp.bfloat16
 MIB = 1 << 20
 LIMIT = 16
+HALVES = 1
 
 
 def chebyshev_coefs():
@@ -80,30 +81,52 @@
         return lax.ppermute(value, self.axis, [(i, i ^ (1 << bit)) for i in range(self.size)])
 
 
-def butterfly(parts):
-    state = [(plan, keep, send) for plan, keep, send in parts]
-    rounds = max(plan.levels for plan, _, _ in parts)
-    current = [None] * len(state)
-    for level in range(rounds):
-        for n, (plan, keep, send) in enumerate(state):
-            if level >= plan.levels:
-                continue
-            if level > 0:
-                half = current[n].shape[0] // 2
-                keep, send = current[n][:half], current[n][half:]
-            current[n] = keep + plan.permute(send, plan.order[level])
-    for n, (plan, _, _) in enumerate(state):
-        current[n] = current[n] + plan.permute(current[n], plan.order[plan.levels])
-    halves = [None] * len(state)
-    for level in reversed(range(rounds)):
-        for n, (plan, _, _) in enumerate(state):
-            if level >= plan.levels:
-                continue
-            other = plan.permute(current[n], plan.order[level])
-            halves[n] = (current[n], other)
-            if level > 0:
-                current[n] = jnp.concatenate([current[n], other], axis=0)
-    return halves
+class Sum:
+    def __init__(self, plan, keep, send):
+        self.plan, self.step = plan, 0
+        self.current, self.halves = None, (keep, send)
+        self.flying = plan.permute(send, plan.order[0]) if plan.levels else None
+
+    def steps(self):
+        return 2 * self.plan.levels + 1
+
+    def advance(self, after=None):
+        plan, levels = self.plan, self.plan.levels
+        arrived = self.flying
+        if after is not None:
+            arrived, _ = lax.optimization_barrier((arrived, after))
+        if self.step < levels:
+            self.current = self.halves[0] + arrived
+            nxt = self.step + 1
+            if nxt < levels:
+                half = self.current.shape[0] // 2
+                self.halves = (self.current[:half], self.current[half:])
+                self.flying = plan.permute(self.halves[1], plan.order[nxt])
+            else:
+                self.flying = plan.permute(self.current, plan.order[levels])
+        else:
+            if self.step == levels:
+                self.current = self.current + arrived
+            else:
+                self.current = jnp.concatenate([self.current, arrived], axis=0)
+            level = 2 * levels - 1 - self.step
+            self.flying = plan.permute(self.current, plan.order[level])
+        self.step += 1
+        return self.current
+
+    def result(self):
+        return self.current, self.flying
+
+
+def run_sums(waves, feat, last):
+    rounds = waves[0][0].steps() - 1
+    extra = feat.steps() - 1
+    for turn in range(rounds):
+        after = [one.advance(last if turn == 0 else None) for wave in waves for one in wave]
+        goal = extra if turn + 1 == rounds else extra * (turn + 1) // rounds
+        while feat.step < goal:
+            feat.advance(after if turn + 1 == rounds else None)
+    return [one.result() for wave in waves for one in wave], feat.result()
 
 
 class Sizes:
@@ -114,10 +137,11 @@
         bits = (self.n_samp - 1).bit_length()
         order = list(range(bits))
         self.colors = [
-            Plan("samp", self.n_samp, order[n % bits:] + order[: n % bits]) for n in range(2)
+            Plan("samp", self.n_samp, order[n % bits:] + order[: n % bits]) for n in range(2 * HALVES)
         ]
         self.feat_plan = Plan("feat", self.n_feat, list(range((self.n_feat - 1).bit_length())))
-        self.color_rows = self.feats // 2
+        self.color_rows = self.feats // len(self.colors)
+        self.half_rows = self.feats // HALVES
         self.coef_chunk = self.color_rows // self.colors[0].chunks
         self.share_chunk = self.rows // self.feat_plan.chunks
         self.own = self.rows // self.n_feat
@@ -125,9 +149,10 @@
         self.feat_block = min(256, self.feats)
 
 
-def coef_places(sz):
+def coef_places(sz, half):
     out = []
-    for color, plan in enumerate(sz.colors):
+    for color in range(2):
+        plan = sz.colors[2 * half + color]
         key = plan.key()
         for location in range(plan.chunks):
             offset = color * sz.color_rows + plan.place(location, key) * sz.coef_chunk
@@ -194,22 +219,21 @@
                 put_split(later, rows, cols, new)
 
 
-def spread_kernel(sz, wide_t, a_hi, a_lo, start, dual, keep0, keep1, send0, send1, plus, proj):
-    cols, block = sz.cols, sz.feat_block
-    for f in range(sz.feats // block):
-        columns = pl.ds(f * block, block)
+def spread_kernel(half, sz, wide_t, a_hi, a_lo, start, dual, keep0, keep1, send0, send1, plus, proj):
+    cols, block = sz.cols, min(sz.feat_block, sz.half_rows)
+    base = half * sz.half_rows
+    for f in range(sz.half_rows // block):
+        columns = pl.ds(base + f * block, block)
+        rows = pl.ds(f * block, block)
         wide = dot_nn(wide_t[...], a_hi[:, columns])
         out = wide[:cols] + wide[cols:] + dot_nn(wide_t[:cols, :], a_lo[:, columns])
-        value = start[columns, :] + out.T
-        proj[columns, :] = value
-        plus[columns, :] = dual[columns, :] + value
-    emit_coef(sz, proj, (keep0, keep1), (send0, send1))
-
-
-def emit_coef(sz, proj, keeps, sends):
-    for color, location, offset in coef_places(sz):
-        which, row = half_of(location, sz.colors[color].chunks, sz.coef_chunk)
-        target = (keeps, sends)[which][color]
+        source = columns if start.shape[0] == sz.feats else rows
+        value = start[source, :] + out.T
+        proj[rows, :] = value
+        plus[rows, :] = dual[source, :] + value
+    for color, location, offset in coef_places(sz, half):
+        which, row = half_of(location, sz.colors[0].chunks, sz.coef_chunk)
+        target = ((keep0, keep1), (send0, send1))[which][color]
         target[pl.ds(row, sz.coef_chunk), :] = proj[pl.ds(offset, sz.coef_chunk), :]
 
 
@@ -222,29 +246,29 @@
         target[pl.ds(row, sz.share_chunk), :] = scratch[pl.ds(offset, sz.share_chunk), :]
 
 
-def first_kernel(sz, data, coef, tile_dual, share, share_dual, targets, tile_share,
+def first_kernel(sz, data, coef_in, tile_dual_in, share_dual_in, tile_share_in, share_in, targets_in,
                  a_hi, a_lo, g_hi, g_lo, start, wide_t, keep_s, send_s, out_sum,
-                 a32, start2, resid, search, search2, total, part, in_sem):
+                 a32, coef, tile_dual, share_dual, tile_share, share, targets,
+                 start2, resid, search, search2, total, part, a_sem, in_sem):
     cols, block = sz.cols, sz.row_block
     blocks = sz.rows // block
     loads = []
     for r in range(blocks):
         rows = pl.ds(r * block, block)
-        copy = pltpu.make_async_copy(data.at[rows, :], a32.at[rows, :], in_sem.at[r])
+        loads.append(pltpu.make_async_copy(data.at[rows, :], a32.at[rows, :], a_sem.at[r]))
+    smalls = [
+        pltpu.make_async_copy(src, dst, in_sem.at[n]) for n, (src, dst) in enumerate((
+            (coef_in, coef), (tile_dual_in, tile_dual), (share_dual_in, share_dual),
+            (tile_share_in, tile_share), (share_in, share), (targets_in, targets)))
+    ]
+    for copy in loads + smalls:
         copy.start()
-        loads.append(copy)
-    first = coef[...] - tile_dual[...]
-    start[...] = first
-    put_split(start2, slice(None), cols, first)
     for r in range(blocks):
         rows = pl.ds(r * block, block)
         loads[r].wait()
         high, low = split(a32[rows, :])
         a_hi[rows, :] = high
         a_lo[rows, :] = low
-        prod = triple(a_hi, a_lo, rows, start2, cols)
-        out_sum[rows, :] = prod
-        resid[rows, :] = tile_share[rows, :] + share_dual[rows, :] - prod
         for c in range(r + 1):
             others = pl.ds(c * block, block)
             gram = dot_nt(a_hi[rows, :], a_hi[others, :])
@@ -261,6 +285,16 @@
                 high, low = split(gram.T)
                 g_hi[others, rows] = high
                 g_lo[others, rows] = low
+    for copy in smalls:
+        copy.wait()
+    first = coef[...] - tile_dual[...]
+    start[...] = first
+    put_split(start2, slice(None), cols, first)
+    for r in range(blocks):
+        rows = pl.ds(r * block, block)
+        prod = triple(a_hi, a_lo, rows, start2, cols)
+        out_sum[rows, :] = prod
+        resid[rows, :] = tile_share[rows, :] + share_dual[rows, :] - prod
     chebyshev_steps(sz, g_hi, g_lo, resid, search, search2, total, part)
     put_wide(wide_t, cols, total[...])
     part[...] += out_sum[...]
@@ -270,29 +304,40 @@
     emit_share(sz, part, half_share, keep_s, send_s)
 
 
-def second_kernel(sz, a_hi, a_lo, g_hi, g_lo, sum00, sum01, sum10, sum11,
-                  esum0, esum1, coef, coef_dual, dual_plus, out_sum, targets, share, share_dual,
-                  start, tile_now, half_out, coef_plus, wide_t, keep_s, send_s,
-                  half_share_out, share_dual_out, proj_share,
-                  start2, resid, search, search2, total, part):
+def update_kernel(half, sz, *refs):
+    before = refs[9:10] if half else ()
+    a_hi, a_lo, sum00, sum01, sum10, sum11, coef, coef_dual, dual_plus = refs[:9]
+    start, tile_now, half_out, coef_plus, prod, start2 = refs[9 + len(before):]
     cols, block = sz.cols, sz.row_block
+    base = half * sz.half_rows
     sums = ((sum00, sum01), (sum10, sum11))
-    for color, location, offset in coef_places(sz):
+    for color, location, offset in coef_places(sz, half):
         rows = pl.ds(offset, sz.coef_chunk)
-        which, row = half_of(location, sz.colors[color].chunks, sz.coef_chunk)
+        whole = pl.ds(base + offset, sz.coef_chunk)
+        which, row = half_of(location, sz.colors[0].chunks, sz.coef_chunk)
         total_coef = sums[color][which][pl.ds(row, sz.coef_chunk), :]
-        dual = coef_dual[rows, :]
-        half = prox_coef(coef[rows, :] - dual)
-        new = (half + total_coef) / (sz.n_samp + 1)
-        dual = dual + half - new
-        half = prox_coef(new - dual)
-        half_out[rows, :] = half
-        coef_plus[rows, :] = dual + half
+        dual = coef_dual[whole, :]
+        prox = prox_coef(coef[whole, :] - dual)
+        new = (prox + total_coef) / (sz.n_samp + 1)
+        dual = dual + prox - new
+        prox = prox_coef(new - dual)
+        half_out[rows, :] = prox
+        coef_plus[rows, :] = dual + prox
         tile = dual_plus[rows, :] - new
         tile_now[rows, :] = tile
-        first = new - tile
-        start[rows, :] = first
-        put_split(start2, rows, cols, first)
+        start[rows, :] = new - tile
+    put_split(start2, slice(None), cols, start[...])
+    columns = pl.ds(base, sz.half_rows)
+    for r in range(sz.rows // block):
+        rows = pl.ds(r * block, block)
+        wide = dot_nn(a_hi[rows, columns], start2[...])
+        value = wide[:, :cols] + wide[:, cols:] + dot_nn(a_lo[rows, columns], start2[:, :cols])
+        prod[rows, :] = value + before[0][rows, :] if half else value
+
+
+def second_kernel(sz, g_hi, g_lo, prod, esum0, esum1, out_sum, targets, share, share_dual,
+                  wide_t, keep_s, send_s, half_share_out, share_dual_out, proj_share,
+                  resid, search, search2, total, part):
     esums = (esum0, esum1)
     for location, offset in share_places(sz):
         rows = pl.ds(offset, sz.share_chunk)
@@ -300,36 +345,33 @@
         excess = esums[which][pl.ds(row, sz.share_chunk), :] * (-1.0 / (sz.n_feat + 1))
         search[rows, :] = excess
         share_dual_out[rows, :] = share_dual[rows, :] + excess
-        resid[rows, :] = out_sum[rows, :] + 2.0 * excess
+        resid[rows, :] = out_sum[rows, :] + 2.0 * excess - prod[rows, :]
     own = pl.ds(pl.multiple_of(lax.axis_index("feat") * sz.own, 8), sz.own)
     share_now = prox_share(share[...], share_dual[own, :], targets[...]) - search[own, :]
     half_share = prox_share(share_now, share_dual_out[own, :], targets[...])
     half_share_out[...] = half_share
-    for r in range(sz.rows // block):
-        rows = pl.ds(r * block, block)
-        prod = triple(a_hi, a_lo, rows, start2, cols)
-        proj_share[rows, :] = prod
-        resid[rows, :] = resid[rows, :] - prod
     chebyshev_steps(sz, g_hi, g_lo, resid, search, search2, total, part)
-    put_wide(wide_t, cols, total[...])
-    part[...] += proj_share[...]
+    put_wide(wide_t, sz.cols, total[...])
+    part[...] += prod[...]
     proj_share[...] = part[...]
     emit_share(sz, part, half_share, keep_s, send_s)
 
 
-def last_kernel(sz, sum00, sum01, sum10, sum11, esum0, esum1, half_coef, coef_plus, tile_plus,
-                half_share, share_dual, proj_share,
-                coef_out, coef_dual_out, tile_out, share_out, share_dual_out, tile_share_out):
-    sums = ((sum00, sum01), (sum10, sum11))
-    for color, location, offset in coef_places(sz):
-        rows = pl.ds(offset, sz.coef_chunk)
-        which, row = half_of(location, sz.colors[color].chunks, sz.coef_chunk)
-        total_coef = sums[color][which][pl.ds(row, sz.coef_chunk), :]
-        new = (half_coef[rows, :] + total_coef) / (sz.n_samp + 1)
-        coef_out[rows, :] = new
-        coef_dual_out[rows, :] = coef_plus[rows, :] - new
-        tile_out[rows, :] = tile_plus[rows, :] - new
-    esums = (esum0, esum1)
+def last_kernel(sz, *refs):
+    coef_out, coef_dual_out, tile_out, share_out, share_dual_out, tile_share_out = refs[-6:]
+    for half in range(HALVES):
+        sum00, sum01, sum10, sum11, half_coef, coef_plus, tile_plus = refs[7 * half:7 * half + 7]
+        sums = ((sum00, sum01), (sum10, sum11))
+        for color, location, offset in coef_places(sz, half):
+            rows = pl.ds(offset, sz.coef_chunk)
+            whole = pl.ds(half * sz.half_rows + offset, sz.coef_chunk)
+            which, row = half_of(location, sz.colors[0].chunks, sz.coef_chunk)
+            total_coef = sums[color][which][pl.ds(row, sz.coef_chunk), :]
+            new = (half_coef[rows, :] + total_coef) / (sz.n_samp + 1)
+            coef_out[whole, :] = new
+            coef_dual_out[whole, :] = coef_plus[rows, :] - new
+            tile_out[whole, :] = tile_plus[rows, :] - new
+    *esums, half_share, share_dual, proj_share = refs[7 * HALVES:7 * HALVES + 5]
     for location, offset in share_places(sz):
         rows = pl.ds(offset, sz.share_chunk)
         which, row = half_of(location, sz.feat_plan.chunks, sz.share_chunk)
@@ -353,8 +395,12 @@
     def kernel(body, name, outs, scratch, work, limit, *operands, streamed=0):
         vmem = pl.BlockSpec(memory_space=pltpu.VMEM)
         hbm = pl.BlockSpec(memory_space=pltpu.HBM)
+        operands = [
+            pltpu.with_memory_space_constraint(x, pltpu.HBM) if n < streamed else x
+            for n, x in enumerate(operands)
+        ]
         return pl.pallas_call(
-            functools.partial(body, sz),
+            body,
             out_shape=outs,
             in_specs=[hbm] * streamed + [vmem] * (len(operands) - streamed),
             out_specs=[vmem] * len(outs),
@@ -368,39 +414,58 @@
     share_sends = [v32(rows // 2, cols)] * 2
     matrices = [v16(rows, feats)] * 2 + [v16(rows, rows)] * 2
     vector = v32(rows, cols)
+    half_coefs = v32(sz.half_rows, cols)
     wide_t = v16(2 * cols, rows)
-    work = [v16(feats, 2 * cols), vector, vector, v16(2, rows, 2 * cols), vector, vector]
+    work = [vector, vector, v16(2, rows, 2 * cols), vector, vector]
     tile_dual = tile_coef_dual[0]
 
-    def spread(wide, a_hi, a_lo, start, dual):
-        return kernel(
-            spread_kernel, "spread", coef_sends + [v32(feats, cols)], [v32(feats, cols)], 3 * flops, LIMIT,
-            wide, a_hi, a_lo, start, dual)
-
-    def sums(keep0, keep1, send0, send1, keep_s, send_s):
-        return butterfly([
-            (sz.colors[0], keep0, send0), (sz.colors[1], keep1, send1), (sz.feat_plan, keep_s, send_s)])
+    def project(wide, keep_s, send_s, starts, duals):
+        feat = Sum(sz.feat_plan, keep_s, send_s)
+        waves, pluses = [], []
+        for half in range(HALVES):
+            if half:
+                wide, _ = lax.optimization_barrier((wide, pluses[-1]))
+            keep0, keep1, send0, send1, plus = kernel(
+                functools.partial(spread_kernel, half, sz), f"spread{half}", coef_sends + [half_coefs],
+                [half_coefs], 3 * flops // HALVES, LIMIT, wide, a_hi, a_lo, starts[half], duals[half])
+            pluses.append(plus)
+            waves.append([
+                Sum(sz.colors[2 * half], keep0, send0), Sum(sz.colors[2 * half + 1], keep1, send1)])
+        feat.advance()
+        sums, esums = run_sums(waves, feat, pluses[-1])
+        groups = [sums[2 * half] + sums[2 * half + 1] for half in range(HALVES)]
+        return groups, esums, pluses
 
     a_hi, a_lo, g_hi, g_lo, start, wide, keep_s, send_s, out_sum = kernel(
-        first_kernel, "first", matrices + [v32(feats, cols), wide_t] + share_sends + [vector],
-        [v32(rows, feats)] + work + [pltpu.SemaphoreType.DMA((blocks,))], 30 * flops, LIMIT,
-        data, coef, tile_dual, share, share_dual, targets, tile_share[0], streamed=1)
-    *parts, dual_plus = spread(wide, a_hi, a_lo, start, tile_dual)
-    (s00, s01), (s10, s11), (e0, e1) = sums(*parts, keep_s, send_s)
-    (start, tile_now, half_coef, coef_plus, wide, keep_s, send_s, half_share, dual_now,
-     proj_share) = kernel(
-        second_kernel, "second",
-        [v32(feats, cols)] * 4 + [wide_t] + share_sends + [v32(sz.own, cols), vector, vector],
-        work, 11 * flops, LIMIT,
-        a_hi, a_lo, g_hi, g_lo, s00, s01, s10, s11, e0, e1, coef, coef_dual, dual_plus, out_sum,
-        targets, share, share_dual)
-    *parts, tile_plus = spread(wide, a_hi, a_lo, start, tile_now)
-    (s00, s01), (s10, s11), (e0, e1) = sums(*parts, keep_s, send_s)
+        functools.partial(first_kernel, sz), "first",
+        matrices + [v32(feats, cols), wide_t] + share_sends + [vector],
+        [v32(rows, feats), v32(feats, cols), v32(feats, cols), vector, vector, v32(sz.own, cols),
+         v32(sz.own, cols), v16(feats, 2 * cols)] + work
+        + [pltpu.SemaphoreType.DMA((blocks,)), pltpu.SemaphoreType.DMA((6,))], 30 * flops, 24,
+        data, coef, tile_dual, share_dual, tile_share[0], share, targets, streamed=7)
+    groups, esums, pluses = project(wide, keep_s, send_s, [start] * HALVES, [tile_dual] * HALVES)
+    starts, duals, saved, prod = [], [], [], []
+    for half in range(HALVES):
+        start, tile_now, half_coef, coef_plus, total = kernel(
+            functools.partial(update_kernel, half, sz), f"update{half}", [half_coefs] * 4 + [vector],
+            [v16(sz.half_rows, 2 * cols)], 2 * flops // HALVES, LIMIT,
+            a_hi, a_lo, *groups[half], coef, coef_dual, pluses[half], *prod)
+        starts.append(start)
+        duals.append(tile_now)
+        saved.append((half_coef, coef_plus))
+        prod = [total]
+    wide, keep_s, send_s, half_share, dual_now, proj_share = kernel(
+        functools.partial(second_kernel, sz), "second",
+        [wide_t] + share_sends + [v32(sz.own, cols), vector, vector],
+        work, 11 * flops, LIMIT, g_hi, g_lo, *prod, *esums, out_sum, targets, share, share_dual)
+    groups, esums, pluses = project(wide, keep_s, send_s, starts, duals)
+    halves = []
+    for half in range(HALVES):
+        halves += [*groups[half], *saved[half], pluses[half]]
     coef_out, coef_dual_out, tile_out, share_out, share_dual_out, tile_share_out = kernel(
-        last_kernel, "last",
+        functools.partial(last_kernel, sz), "last",
         [f32(feats, cols)] * 3 + [f32(sz.own, cols), f32(rows, cols), f32(rows, cols)],
-        [], flops // 100, LIMIT,
-        s00, s01, s10, s11, e0, e1, half_coef, coef_plus, tile_plus, half_share, dual_now, proj_share)
+        [], flops // 100, LIMIT, *halves, *esums, half_share, dual_now, proj_share)
     return (coef_out, coef_dual_out, tile_out[None], share_out, share_dual_out, tile_share_out[None])
 
 

time: 104 us -> 95.7 us (0.920)
  local copies, waits for them, and re-layouts: 9.63 us -> 0.06 us
  Pallas kernels: 33 us -> 35.3 us
    unnamed x24 -> x12, local copies, waits for them, and re-layouts: 9.61 us -> 0.04 us
    pallas_call x5 -> x6, Pallas kernels: 33 us -> 35.3 us  [kernel(): pl.pallas_call(body, out_shape=outs, in_specs=[hbm] * streamed + [vmem] *...]
  transfers between devices with their start and end apart: 22 -> 22, of which waited for: 11 -> 15; matrix products, arithmetic and copies ran while one was open for 0% -> 0% of each run, Pallas kernels for 4% -> 7%
where the time goes in v3:
time: 95.7 us; the launch traced here: 95.5 us
  Pallas kernels  35.3 us (37%)
  waiting for transfers between devices  33.6 us (35%)
  starting transfers between devices  25.3 us (26%)
    pallas_call x6, Pallas kernels, kernel(): pl.pallas_call(body, out_shape=outs, in_specs=[hbm] * streamed + [vmem] *...  35.3 us
    ppermute x22, waiting for transfers between devices, permute(): lax.ppermute(value, self.axis, [(i, i ^ 1 << bit) for i in range(self.siz...  33.6 us
    ppermute x22, starting transfers between devices, permute(): lax.ppermute(value, self.axis, [(i, i ^ 1 << bit) for i in range(self.siz...  25.3 us
  transfers between devices with their start and end apart: 22, of which 15 were waited for; matrix products, arithmetic and copies ran while one was open for 0% of the time, Pallas kernels for 7%

profile of v3, /device:TPU:0, one launch (start us, length us, event | category | flops | bytes accessed | tf_op | source)
XLA Modules:
  0.0 95.5 jit_solution(10181271470024140013)
XLA Ops:
  0.6 19.6 %first.1 = (bf16[1024,2048]{1,0:T(8,128)(2,1)S(1)}, bf16[1024,2048]{1,0:T(8,128)(2,1)S(1)}, bf16[1024,1024]{1,0:T(8,128)(2,1)S(1)}, bf16[1024,1024]{1,0:T(8,128)...) custom-call(f32[1024,2048]{1,0:T(8,128)} %data.1, ...), custom_call_target="tpu_custom_call" | custom-call | flops 16106127360 | bytes 8388608 | tf_op jit(solution)/shard_map/first/pallas_call | solution.py:402
  20.7 2.1 %spread0.2 = (f32[512,128]{1,0:T(8,128)S(1)}, f32[512,128]{1,0:T(8,128)S(1)}, f32[512,128]{1,0:T(8,128)S(1)}, f32[512,128]{1,0:T(8,128)S(1)}, f32[2048,128]{1,0:T(8,128)S(1)}) custom-call(bf16[256,1024]{1,0:T(8,128)(2,1)S(1)} %get-tuple-element.54.wide_t, bf16[1024,2048]{1,0:T(8,128)(2,1)S(1)} %get-tuple-element.52.a_hi.refs_0_, ...), custom_call_target="tpu_custom_call" | custom-call | flops 1610612736 | bytes 8388608 | tf_op jit(solution)/shard_map/spread0/pallas_call | solution.py:402
  22.9 2.6 %collective-permute-start = (f32[512,128]{1,0:T(8,128)S(1)}, f32[512,128]{1,0:T(8,128)S(1)}, u32[]{:S(2)}, u32[]{:S(2)}) collective-permute-start(f32[512,128]{1,0:T(8,128)S(1)} %get-tuple-element.57), channel_id=1, source_target_pairs={{0,8},{8,0},{16,24},{24,16},{1,9},{9,1},{17,25},{25,17},{2,10},{10... | collective-permute-start | bytes 786440 | tf_op jit(solution)/shard_map/ppermute | solution.py:81
  25.5 1.5 %collective-permute-start.3 = (f32[512,128]{1,0:T(8,128)S(1)}, f32[512,128]{1,0:T(8,128)S(1)}, u32[]{:S(2)}, u32[]{:S(2)}) collective-permute-start(f32[512,128]{1,0:T(8,128)S(1)} %get-tuple-element.61), channel_id=1, source_target_pairs={{0,16},{8,24},{16,0},{24,8},{1,17},{9,25},{17,1},{25,9},{2,18},{10... | collective-permute-start | bytes 786440 | tf_op jit(solution)/shard_map/ppermute | solution.py:81
  27.0 1.7 %collective-permute-start.7 = (f32[256,128]{1,0:T(8,128)S(1)}, f32[256,128]{1,0:T(8,128)S(1)}, u32[]{:S(2)}, u32[]{:S(2)}) collective-permute-start(f32[256,128]{1,0:T(8,128)S(1)} %slice.17), channel_id=1, source_target_pairs={{0,2},{1,3},{2,0},{3,1},{4,6},{5,7},{6,4},{7,5},{8,10},{9,11},{10,... | collective-permute-start | bytes 393224 | tf_op jit(solution)/shard_map/ppermute | solution.py:81
  28.7 3.7 %collective-permute-done = f32[512,128]{1,0:T(8,128)S(1)} collective-permute-done((f32[512,128]{1,0:T(8,128)S(1)}, f32[512,128]{1,0:T(8,128)S(1)}, u32[]{:S(2)}, u32[]{:S(2)}) %collective-permute-start) | collective-permute-done | bytes 262176 | tf_op jit(solution)/shard_map/ppermute | solution.py:81
  32.5 1.8 %collective-permute-start.1 = (f32[512,128]{1,0:T(8,128)S(1)}, f32[512,128]{1,0:T(8,128)S(1)}, u32[]{:S(2)}, u32[]{:S(2)}) collective-permute-start(f32[512,128]{1,0:T(8,128)S(1)} %add.42), channel_id=1, source_target_pairs={{0,16},{8,24},{16,0},{24,8},{1,17},{9,25},{17,1},{25,9},{2,18},{10... | collective-permute-start | bytes 786440 | tf_op jit(solution)/shard_map/ppermute | solution.py:81
  34.3 1.6 %collective-permute-start.4 = (f32[512,128]{1,0:T(8,128)S(1)}, f32[512,128]{1,0:T(8,128)S(1)}, u32[]{:S(2)}, u32[]{:S(2)}) collective-permute-start(f32[512,128]{1,0:T(8,128)S(1)} %add.44), channel_id=1, source_target_pairs={{0,8},{8,0},{16,24},{24,16},{1,9},{9,1},{17,25},{25,17},{2,10},{10... | collective-permute-start | bytes 786440 | tf_op jit(solution)/shard_map/ppermute | solution.py:81
  35.9 2.7 %collective-permute-start.8 = (f32[256,128]{1,0:T(8,128)S(1)}, f32[256,128]{1,0:T(8,128)S(1)}, u32[]{:S(2)}, u32[]{:S(2)}) collective-permute-start(f32[256,128]{1,0:T(8,128)S(1)} %slice_add_fusion.1), channel_id=1, source_target_pairs={{0,4},{1,5},{2,6},{3,7},{4,0},{5,1},{6,2},{7,3},{8,12},{9,13},{10,... | collective-permute-start | bytes 393224 | tf_op jit(solution)/shard_map/ppermute | solution.py:81
  38.6 2.1 %collective-permute-done.1 = f32[512,128]{1,0:T(8,128)S(1)} collective-permute-done((f32[512,128]{1,0:T(8,128)S(1)}, f32[512,128]{1,0:T(8,128)S(1)}, u32[]{:S(2)}, u32[]{:S(2)}) %collective-permute-start.1) | collective-permute-done | bytes 262176 | tf_op jit(solution)/shard_map/ppermute | solution.py:81
  42.1 2.2 %collective-permute-done.8 = f32[256,128]{1,0:T(8,128)S(1)} collective-permute-done((f32[256,128]{1,0:T(8,128)S(1)}, f32[256,128]{1,0:T(8,128)S(1)}, u32[]{:S(2)}, u32[]{:S(2)}) %collective-permute-start.8) | collective-permute-done | bytes 131104 | tf_op jit(solution)/shard_map/ppermute | solution.py:81
  46.6 2.7 %collective-permute-done.9 = f32[256,128]{1,0:T(8,128)S(1)} collective-permute-done((f32[256,128]{1,0:T(8,128)S(1)}, f32[256,128]{1,0:T(8,128)S(1)}, u32[]{:S(2)}, u32[]{:S(2)}) %collective-permute-start.9) | collective-permute-done | bytes 131104 | tf_op jit(solution)/shard_map/ppermute | solution.py:81
  49.4 3.1 %collective-permute-done.2.refs_3_ = f32[512,128]{1,0:T(8,128)S(1)} collective-permute-done((f32[512,128]{1,0:T(8,128)S(1)}, f32[512,128]{1,0:T(8,128)S(1)}, u32[]{:S(2)}, u32[]{:S(2)}) %collective-permute-start.2) | collective-permute-done | bytes 262176 | tf_op jit(solution)/shard_map/ppermute | solution.py:81
  52.8 2.9 %update0.1 = (f32[2048,128]{1,0:T(8,128)S(1)}, f32[2048,128]{1,0:T(8,128)S(1)}, f32[2048,128]{1,0:T(8,128)S(1)}, f32[2048,128]{1,0:T(8,128)S(1)}, f32[1024,128]{1,0:T(8,128)S(1)}) custom-call(bf16[1024,2048]{1,0:T(8,128)(2,1)S(1)} %get-tuple-element.52.a_hi.refs_0_, bf16[1024,2048]{1,0:T(8,128)(2,1)S(1)} %get-tuple-element.53.a_lo.refs_1_, ...), custom_call_target="tpu_custom_call" | custom-call | flops 1073741824 | bytes 8388608 | tf_op jit(solution)/shard_map/update0/pallas_call | solution.py:402
  55.7 6.4 %second.1 = (bf16[256,1024]{1,0:T(8,128)(2,1)S(1)}, f32[512,128]{1,0:T(8,128)S(1)}, f32[512,128]{1,0:T(8,128)S(1)}, f32[128,128]{1,0:T(8,128)S(1)}, f32[1024,128]{1,0:T(8,128)S(1)}, /*index=5*/f32[1024,128]{1,0:T(8,128)S(1)}) custom-call(bf16[1024,1024]{1,0:T(8,128)(2,1)S(1)} %get-tuple-element.50.g_hi, bf16[1024,1024]{1,0:T(8,128)(2,1)S(1)} %get-tuple-element.51.g_lo, ...), custom_call_target="tpu_custom_call" | custom-call | flops 5905580032 | bytes 8388608 | tf_op jit(solution)/shard_map/second/pallas_call | solution.py:402
  62.2 2.1 %spread0.3 = (f32[512,128]{1,0:T(8,128)S(1)}, f32[512,128]{1,0:T(8,128)S(1)}, f32[512,128]{1,0:T(8,128)S(1)}, f32[512,128]{1,0:T(8,128)S(1)}, f32[2048,128]{1,0:T(8,128)S(1)}) custom-call(bf16[256,1024]{1,0:T(8,128)(2,1)S(1)} %get-tuple-element.69.wide_t, bf16[1024,2048]{1,0:T(8,128)(2,1)S(1)} %get-tuple-element.52.a_hi.refs_0_, ...), custom_call_target="tpu_custom_call" | custom-call | flops 1610612736 | bytes 8388608 | tf_op jit(solution)/shard_map/spread0/pallas_call | solution.py:402
  64.3 1.5 %collective-permute-start.11 = (f32[512,128]{1,0:T(8,128)S(1)}, f32[512,128]{1,0:T(8,128)S(1)}, u32[]{:S(2)}, u32[]{:S(2)}) collective-permute-start(f32[512,128]{1,0:T(8,128)S(1)} %get-tuple-element.73), channel_id=1, source_target_pairs={{0,8},{8,0},{16,24},{24,16},{1,9},{9,1},{17,25},{25,17},{2,10},{10... | collective-permute-start | bytes 786440 | tf_op jit(solution)/shard_map/ppermute | solution.py:81
  67.1 6.0 %collective-permute-done.11 = f32[512,128]{1,0:T(8,128)S(1)} collective-permute-done((f32[512,128]{1,0:T(8,128)S(1)}, f32[512,128]{1,0:T(8,128)S(1)}, u32[]{:S(2)}, u32[]{:S(2)}) %collective-permute-start.11) | collective-permute-done | bytes 262176 | tf_op jit(solution)/shard_map/ppermute | solution.py:81
  75.3 3.4 %collective-permute-start.19 = (f32[256,128]{1,0:T(8,128)S(1)}, f32[256,128]{1,0:T(8,128)S(1)}, u32[]{:S(2)}, u32[]{:S(2)}) collective-permute-start(f32[256,128]{1,0:T(8,128)S(1)} %slice_add_fusion), channel_id=1, source_target_pairs={{0,4},{1,5},{2,6},{3,7},{4,0},{5,1},{6,2},{7,3},{8,12},{9,13},{10,... | collective-permute-start | bytes 393224 | tf_op jit(solution)/shard_map/ppermute | solution.py:81
  78.7 2.3 %collective-permute-done.12 = f32[512,128]{1,0:T(8,128)S(1)} collective-permute-done((f32[512,128]{1,0:T(8,128)S(1)}, f32[512,128]{1,0:T(8,128)S(1)}, u32[]{:S(2)}, u32[]{:S(2)}) %collective-permute-start.12) | collective-permute-done | bytes 262176 | tf_op jit(solution)/shard_map/ppermute | solution.py:81
  82.0 2.2 %collective-permute-done.19 = f32[256,128]{1,0:T(8,128)S(1)} collective-permute-done((f32[256,128]{1,0:T(8,128)S(1)}, f32[256,128]{1,0:T(8,128)S(1)}, u32[]{:S(2)}, u32[]{:S(2)}) %collective-permute-start.19) | collective-permute-done | bytes 131104 | tf_op jit(solution)/shard_map/ppermute | solution.py:81
  86.4 3.3 %collective-permute-done.20 = f32[256,128]{1,0:T(8,128)S(1)} collective-permute-done((f32[256,128]{1,0:T(8,128)S(1)}, f32[256,128]{1,0:T(8,128)S(1)}, u32[]{:S(2)}, u32[]{:S(2)}) %collective-permute-start.20) | collective-permute-done | bytes 131104 | tf_op jit(solution)/shard_map/ppermute | solution.py:81
  89.7 2.8 %collective-permute-done.13.refs_1_ = f32[512,128]{1,0:T(8,128)S(1)} collective-permute-done((f32[512,128]{1,0:T(8,128)S(1)}, f32[512,128]{1,0:T(8,128)S(1)}, u32[]{:S(2)}, u32[]{:S(2)}) %collective-permute-start.13) | collective-permute-done | bytes 262176 | tf_op jit(solution)/shard_map/ppermute | solution.py:81
  93.3 2.2 %last.1 = (f32[2048,128]{1,0:T(8,128)}, f32[2048,128]{1,0:T(8,128)}, f32[2048,128]{1,0:T(8,128)}, f32[128,128]{1,0:T(8,128)}, f32[1024,128]{1,0:T(8,128)}, /*index=5*/f32[1024,128]{1,0:T(8,128)}) custom-call(f32[512,128]{1,0:T(8,128)S(1)} %add.50.refs_0_, f32[512,128]{1,0:T(8,128)S(1)} %collective-permute-done.13.refs_1_, f32[512,128]{1,0:T(8,128)S(1)} %add.52.refs_2_, ...), custom_call_target="tpu_custom_call" | custom-call | flops 5368709 | bytes 8388608 | tf_op jit(solution)/shard_map/last/pallas_call | solution.py:402
  (56 shorter events, 12.3 us)
Async XLA Ops:
  20.2 6.8 %collective-permute-start.6 = (f32[512,128]{1,0:T(8,128)S(1)}, f32[512,128]{1,0:T(8,128)S(1)}, u32[]{:S(2)}, u32[]{:S(2)}) collective-permute-start(f32[512,128]{1,0:T(8,128)S(1)} %get-tuple-element.65), channel_id=1, source_target_pairs={{0,1},{1,0},{2,3},{3,2},{4,5},{5,4},{6,7},{7,6},{8,9},{9,8},{10,11... | collective-permute-start | bytes 786440 | tf_op jit(solution)/shard_map/ppermute | solution.py:81
  22.9 29.9 %copy-start = (f32[2048,128]{1,0:T(8,128)S(1)}, f32[2048,128]{1,0:T(8,128)}, u32[]{:S(2)}) copy-start(f32[2048,128]{1,0:T(8,128)} %refs_6_.1) | copy-start | bytes 3145732
  22.9 29.9 %copy-start.1 = (f32[2048,128]{1,0:T(8,128)S(1)}, f32[2048,128]{1,0:T(8,128)}, u32[]{:S(2)}) copy-start(f32[2048,128]{1,0:T(8,128)} %refs_7_.1) | copy-start | bytes 3145732
  22.9 9.5 %collective-permute-start = (f32[512,128]{1,0:T(8,128)S(1)}, f32[512,128]{1,0:T(8,128)S(1)}, u32[]{:S(2)}, u32[]{:S(2)}) collective-permute-start(f32[512,128]{1,0:T(8,128)S(1)} %get-tuple-element.57), channel_id=1, source_target_pairs={{0,8},{8,0},{16,24},{24,16},{1,9},{9,1},{17,25},{25,17},{2,10},{10... | collective-permute-start | bytes 786440 | tf_op jit(solution)/shard_map/ppermute | solution.py:81
  25.5 8.8 %collective-permute-start.3 = (f32[512,128]{1,0:T(8,128)S(1)}, f32[512,128]{1,0:T(8,128)S(1)}, u32[]{:S(2)}, u32[]{:S(2)}) collective-permute-start(f32[512,128]{1,0:T(8,128)S(1)} %get-tuple-element.61), channel_id=1, source_target_pairs={{0,16},{8,24},{16,0},{24,8},{1,17},{9,25},{17,1},{25,9},{2,18},{10... | collective-permute-start | bytes 786440 | tf_op jit(solution)/shard_map/ppermute | solution.py:81
  27.0 8.8 %collective-permute-start.7 = (f32[256,128]{1,0:T(8,128)S(1)}, f32[256,128]{1,0:T(8,128)S(1)}, u32[]{:S(2)}, u32[]{:S(2)}) collective-permute-start(f32[256,128]{1,0:T(8,128)S(1)} %slice.17), channel_id=1, source_target_pairs={{0,2},{1,3},{2,0},{3,1},{4,6},{5,7},{6,4},{7,5},{8,10},{9,11},{10,... | collective-permute-start | bytes 393224 | tf_op jit(solution)/shard_map/ppermute | solution.py:81
  32.5 8.2 %collective-permute-start.1 = (f32[512,128]{1,0:T(8,128)S(1)}, f32[512,128]{1,0:T(8,128)S(1)}, u32[]{:S(2)}, u32[]{:S(2)}) collective-permute-start(f32[512,128]{1,0:T(8,128)S(1)} %add.42), channel_id=1, source_target_pairs={{0,16},{8,24},{16,0},{24,8},{1,17},{9,25},{17,1},{25,9},{2,18},{10... | collective-permute-start | bytes 786440 | tf_op jit(solution)/shard_map/ppermute | solution.py:81
  34.3 7.7 %collective-permute-start.4 = (f32[512,128]{1,0:T(8,128)S(1)}, f32[512,128]{1,0:T(8,128)S(1)}, u32[]{:S(2)}, u32[]{:S(2)}) collective-permute-start(f32[512,128]{1,0:T(8,128)S(1)} %add.44), channel_id=1, source_target_pairs={{0,8},{8,0},{16,24},{24,16},{1,9},{9,1},{17,25},{25,17},{2,10},{10... | collective-permute-start | bytes 786440 | tf_op jit(solution)/shard_map/ppermute | solution.py:81
  35.9 8.3 %collective-permute-start.8 = (f32[256,128]{1,0:T(8,128)S(1)}, f32[256,128]{1,0:T(8,128)S(1)}, u32[]{:S(2)}, u32[]{:S(2)}) collective-permute-start(f32[256,128]{1,0:T(8,128)S(1)} %slice_add_fusion.1), channel_id=1, source_target_pairs={{0,4},{1,5},{2,6},{3,7},{4,0},{5,1},{6,2},{7,3},{8,12},{9,13},{10,... | collective-permute-start | bytes 393224 | tf_op jit(solution)/shard_map/ppermute | solution.py:81
  44.2 5.0 %collective-permute-start.9 = (f32[256,128]{1,0:T(8,128)S(1)}, f32[256,128]{1,0:T(8,128)S(1)}, u32[]{:S(2)}, u32[]{:S(2)}) collective-permute-start(f32[256,128]{1,0:T(8,128)S(1)} %add.48), channel_id=1, source_target_pairs={{0,2},{1,3},{2,0},{3,1},{4,6},{5,7},{6,4},{7,5},{8,10},{9,11},{10,... | collective-permute-start | bytes 393224 | tf_op jit(solution)/shard_map/ppermute | solution.py:81
  45.0 7.6 %collective-permute-start.2 = (f32[512,128]{1,0:T(8,128)S(1)}, f32[512,128]{1,0:T(8,128)S(1)}, u32[]{:S(2)}, u32[]{:S(2)}) collective-permute-start(f32[512,128]{1,0:T(8,128)S(1)} %add.43.refs_2_), channel_id=1, source_target_pairs={{0,8},{8,0},{16,24},{24,16},{1,9},{9,1},{17,25},{25,17},{2,10},{10... | collective-permute-start | bytes 786440 | tf_op jit(solution)/shard_map/ppermute | solution.py:81
  45.5 7.3 %collective-permute-start.5 = (f32[512,128]{1,0:T(8,128)S(1)}, f32[512,128]{1,0:T(8,128)S(1)}, u32[]{:S(2)}, u32[]{:S(2)}) collective-permute-start(f32[512,128]{1,0:T(8,128)S(1)} %add.45.refs_4_), channel_id=1, source_target_pairs={{0,16},{8,24},{16,0},{24,8},{1,17},{9,25},{17,1},{25,9},{2,18},{10... | collective-permute-start | bytes 786440 | tf_op jit(solution)/shard_map/ppermute | solution.py:81
  49.3 6.4 %collective-permute-start.10 = (f32[512,128]{1,0:T(8,128)S(1)}, f32[512,128]{1,0:T(8,128)S(1)}, u32[]{:S(2)}, u32[]{:S(2)}) collective-permute-start(f32[512,128]{1,0:T(8,128)S(1)} %pad_maximum_fusion.esum0), channel_id=1, source_target_pairs={{0,1},{1,0},{2,3},{3,2},{4,5},{5,4},{6,7},{7,6},{8,9},{9,8},{10,11... | collective-permute-start | bytes 786440 | tf_op jit(solution)/shard_map/ppermute | solution.py:81
  62.1 4.3 %collective-permute-start.17 = (f32[512,128]{1,0:T(8,128)S(1)}, f32[512,128]{1,0:T(8,128)S(1)}, u32[]{:S(2)}, u32[]{:S(2)}) collective-permute-start(f32[512,128]{1,0:T(8,128)S(1)} %get-tuple-element.82), channel_id=1, source_target_pairs={{0,1},{1,0},{2,3},{3,2},{4,5},{5,4},{6,7},{7,6},{8,9},{9,8},{10,11... | collective-permute-start | bytes 786440 | tf_op jit(solution)/shard_map/ppermute | solution.py:81
  64.3 8.8 %collective-permute-start.11 = (f32[512,128]{1,0:T(8,128)S(1)}, f32[512,128]{1,0:T(8,128)S(1)}, u32[]{:S(2)}, u32[]{:S(2)}) collective-permute-start(f32[512,128]{1,0:T(8,128)S(1)} %get-tuple-element.73), channel_id=1, source_target_pairs={{0,8},{8,0},{16,24},{24,16},{1,9},{9,1},{17,25},{25,17},{2,10},{10... | collective-permute-start | bytes 786440 | tf_op jit(solution)/shard_map/ppermute | solution.py:81
  65.8 8.4 %collective-permute-start.14 = (f32[512,128]{1,0:T(8,128)S(1)}, f32[512,128]{1,0:T(8,128)S(1)}, u32[]{:S(2)}, u32[]{:S(2)}) collective-permute-start(f32[512,128]{1,0:T(8,128)S(1)} %get-tuple-element.77), channel_id=1, source_target_pairs={{0,16},{8,24},{16,0},{24,8},{1,17},{9,25},{17,1},{25,9},{2,18},{10... | collective-permute-start | bytes 786440 | tf_op jit(solution)/shard_map/ppermute | solution.py:81
  66.4 8.9 %collective-permute-start.18 = (f32[256,128]{1,0:T(8,128)S(1)}, f32[256,128]{1,0:T(8,128)S(1)}, u32[]{:S(2)}, u32[]{:S(2)}) collective-permute-start(f32[256,128]{1,0:T(8,128)S(1)} %slice.19), channel_id=1, source_target_pairs={{0,2},{1,3},{2,0},{3,1},{4,6},{5,7},{6,4},{7,5},{8,10},{9,11},{10,... | collective-permute-start | bytes 393224 | tf_op jit(solution)/shard_map/ppermute | solution.py:81
  73.1 8.0 %collective-permute-start.12 = (f32[512,128]{1,0:T(8,128)S(1)}, f32[512,128]{1,0:T(8,128)S(1)}, u32[]{:S(2)}, u32[]{:S(2)}) collective-permute-start(f32[512,128]{1,0:T(8,128)S(1)} %add.49), channel_id=1, source_target_pairs={{0,16},{8,24},{16,0},{24,8},{1,17},{9,25},{17,1},{25,9},{2,18},{10... | collective-permute-start | bytes 786440 | tf_op jit(solution)/shard_map/ppermute | solution.py:81
  74.3 7.7 %collective-permute-start.15 = (f32[512,128]{1,0:T(8,128)S(1)}, f32[512,128]{1,0:T(8,128)S(1)}, u32[]{:S(2)}, u32[]{:S(2)}) collective-permute-start(f32[512,128]{1,0:T(8,128)S(1)} %add.51), channel_id=1, source_target_pairs={{0,8},{8,0},{16,24},{24,16},{1,9},{9,1},{17,25},{25,17},{2,10},{10... | collective-permute-start | bytes 786440 | tf_op jit(solution)/shard_map/ppermute | solution.py:81
  75.3 8.9 %collective-permute-start.19 = (f32[256,128]{1,0:T(8,128)S(1)}, f32[256,128]{1,0:T(8,128)S(1)}, u32[]{:S(2)}, u32[]{:S(2)}) collective-permute-start(f32[256,128]{1,0:T(8,128)S(1)} %slice_add_fusion), channel_id=1, source_target_pairs={{0,4},{1,5},{2,6},{3,7},{4,0},{5,1},{6,2},{7,3},{8,12},{9,13},{10,... | collective-permute-start | bytes 393224 | tf_op jit(solution)/shard_map/ppermute | solution.py:81
  84.2 5.5 %collective-permute-start.20 = (f32[256,128]{1,0:T(8,128)S(1)}, f32[256,128]{1,0:T(8,128)S(1)}, u32[]{:S(2)}, u32[]{:S(2)}) collective-permute-start(f32[256,128]{1,0:T(8,128)S(1)} %add.55), channel_id=1, source_target_pairs={{0,2},{1,3},{2,0},{3,1},{4,6},{5,7},{6,4},{7,5},{8,10},{9,11},{10,... | collective-permute-start | bytes 393224 | tf_op jit(solution)/shard_map/ppermute | solution.py:81
  84.3 8.3 %collective-permute-start.13 = (f32[512,128]{1,0:T(8,128)S(1)}, f32[512,128]{1,0:T(8,128)S(1)}, u32[]{:S(2)}, u32[]{:S(2)}) collective-permute-start(f32[512,128]{1,0:T(8,128)S(1)} %add.50.refs_0_), channel_id=1, source_target_pairs={{0,8},{8,0},{16,24},{24,16},{1,9},{9,1},{17,25},{25,17},{2,10},{10... | collective-permute-start | bytes 786440 | tf_op jit(solution)/shard_map/ppermute | solution.py:81
  85.4 7.9 %collective-permute-start.16 = (f32[512,128]{1,0:T(8,128)S(1)}, f32[512,128]{1,0:T(8,128)S(1)}, u32[]{:S(2)}, u32[]{:S(2)}) collective-permute-start(f32[512,128]{1,0:T(8,128)S(1)} %add.52.refs_2_), channel_id=1, source_target_pairs={{0,16},{8,24},{16,0},{24,8},{1,17},{9,25},{17,1},{25,9},{2,18},{10... | collective-permute-start | bytes 786440 | tf_op jit(solution)/shard_map/ppermute | solution.py:81
  89.7 3.6 %collective-permute-start.21 = (f32[512,128]{1,0:T(8,128)S(1)}, f32[512,128]{1,0:T(8,128)S(1)}, u32[]{:S(2)}, u32[]{:S(2)}) collective-permute-start(f32[512,128]{1,0:T(8,128)S(1)} %pad_maximum_fusion.1.refs_7_), channel_id=1, source_target_pairs={{0,1},{1,0},{2,3},{3,2},{4,5},{5,4},{6,7},{7,6},{8,9},{9,8},{10,11... | collective-permute-start | bytes 786440 | tf_op jit(solution)/shard_map/ppermute | solution.py:81
  (4 other events, 39.3 us)

commit v4 on v3

--- a/solution.py
+++ b/solution.py
@@ -18,7 +18,8 @@
 BF16 = jnp.bfloat16
 MIB = 1 << 20
 LIMIT = 16
-HALVES = 1
+HALVES = 2
+ADD_FLOPS = 4 * 10**9
 
 
 def chebyshev_coefs():
@@ -90,42 +91,73 @@
     def steps(self):
         return 2 * self.plan.levels + 1
 
-    def advance(self, after=None):
+    def terms(self):
+        own = self.halves[0] if self.step < self.plan.levels else self.current
+        return (own, self.flying) if self.step <= self.plan.levels else None
+
+    def advance(self, total=None):
         plan, levels = self.plan, self.plan.levels
-        arrived = self.flying
-        if after is not None:
-            arrived, _ = lax.optimization_barrier((arrived, after))
-        if self.step < levels:
-            self.current = self.halves[0] + arrived
-            nxt = self.step + 1
-            if nxt < levels:
-                half = self.current.shape[0] // 2
-                self.halves = (self.current[:half], self.current[half:])
-                self.flying = plan.permute(self.halves[1], plan.order[nxt])
-            else:
-                self.flying = plan.permute(self.current, plan.order[levels])
+        if self.step <= levels:
+            own, arrived = self.terms()
+            self.current = own + arrived if total is None else total
         else:
-            if self.step == levels:
-                self.current = self.current + arrived
-            else:
-                self.current = jnp.concatenate([self.current, arrived], axis=0)
-            level = 2 * levels - 1 - self.step
-            self.flying = plan.permute(self.current, plan.order[level])
-        self.step += 1
-        return self.current
+            self.current = jnp.concatenate([self.current, self.flying], axis=0)
+        nxt = self.step + 1
+        if nxt < levels:
+            half = self.current.shape[0] // 2
+            self.halves = (self.current[:half], self.current[half:])
+            self.flying = plan.permute(self.halves[1], plan.order[nxt])
+        else:
+            self.flying = plan.permute(self.current, plan.order[2 * levels - nxt if nxt > levels else levels])
+        self.step = nxt
+
+
+    def wait_for(self, after):
+        self.flying, _ = lax.optimization_barrier((self.flying, after))
 
     def result(self):
         return self.current, self.flying
+
+
+def add_kernel(*refs):
+    count = len(refs) // 3
+    for n in range(count):
+        refs[2 * count + n][...] = refs[2 * n][...] + refs[2 * n + 1][...]
+
+
+def add_all(pairs):
+    vmem = pl.BlockSpec(memory_space=pltpu.VMEM)
+    return pl.pallas_call(
+        add_kernel,
+        out_shape=[pltpu.VMEM(own.shape, F32) for own, _ in pairs],
+        in_specs=[vmem] * (2 * len(pairs)),
+        out_specs=[vmem] * len(pairs),
+        compiler_params=pltpu.CompilerParams(vmem_limit_bytes=LIMIT * MIB),
+        cost_estimate=pl.CostEstimate(flops=ADD_FLOPS, bytes_accessed=MIB, transcendentals=0),
+        name="sums",
+    )(*[x for pair in pairs for x in pair])
+
+
+def step_all(group, before):
+    for one in group:
+        one.wait_for(before)
+    pairs = [one.terms() for one in group]
+    totals = [None] * len(group) if None in pairs else add_all(pairs)
+    for one, total in zip(group, totals):
+        one.advance(total)
+    return [one.current for one in group]
 
 
 def run_sums(waves, feat, last):
     rounds = waves[0][0].steps() - 1
     extra = feat.steps() - 1
-    for turn in range(rounds):
-        after = [one.advance(last if turn == 0 else None) for wave in waves for one in wave]
-        goal = extra if turn + 1 == rounds else extra * (turn + 1) // rounds
-        while feat.step < goal:
-            feat.advance(after if turn + 1 == rounds else None)
+    before, turns = last, rounds * len(waves)
+    for turn in range(turns):
+        before = step_all(waves[turn % len(waves)], before)
+        while feat.step < min(feat.plan.levels, -(-feat.plan.levels * (turn + 1) // (turns - 1))):
+            before = step_all([feat], before)
+    while feat.step < extra:
+        before = step_all([feat], before)
     return [one.result() for wave in waves for one in wave], feat.result()
 
 
@@ -357,21 +389,32 @@
     emit_share(sz, part, half_share, keep_s, send_s)
 
 
-def last_kernel(sz, *refs):
-    coef_out, coef_dual_out, tile_out, share_out, share_dual_out, tile_share_out = refs[-6:]
-    for half in range(HALVES):
-        sum00, sum01, sum10, sum11, half_coef, coef_plus, tile_plus = refs[7 * half:7 * half + 7]
-        sums = ((sum00, sum01), (sum10, sum11))
-        for color, location, offset in coef_places(sz, half):
-            rows = pl.ds(offset, sz.coef_chunk)
-            whole = pl.ds(half * sz.half_rows + offset, sz.coef_chunk)
-            which, row = half_of(location, sz.colors[0].chunks, sz.coef_chunk)
-            total_coef = sums[color][which][pl.ds(row, sz.coef_chunk), :]
-            new = (half_coef[rows, :] + total_coef) / (sz.n_samp + 1)
-            coef_out[whole, :] = new
-            coef_dual_out[whole, :] = coef_plus[rows, :] - new
-            tile_out[whole, :] = tile_plus[rows, :] - new
-    *esums, half_share, share_dual, proj_share = refs[7 * HALVES:7 * HALVES + 5]
+def last_kernel(half, sz, *refs):
+    sum00, sum01, sum10, sum11, half_coef, coef_plus, tile_plus = refs[-14:-7] if not half else refs[3:10]
+    outs, (new_s, dual_s, tile_s), sems = refs[-7:-4], refs[-4:-1], refs[-1]
+    sums = ((sum00, sum01), (sum10, sum11))
+    for color, location, offset in coef_places(sz, half):
+        rows = pl.ds(offset, sz.coef_chunk)
+        which, row = half_of(location, sz.colors[0].chunks, sz.coef_chunk)
+        total_coef = sums[color][which][pl.ds(row, sz.coef_chunk), :]
+        new = (half_coef[rows, :] + total_coef) / (sz.n_samp + 1)
+        new_s[rows, :] = new
+        dual_s[rows, :] = coef_plus[rows, :] - new
+        tile_s[rows, :] = tile_plus[rows, :] - new
+    whole = pl.ds(half * sz.half_rows, sz.half_rows)
+    copies = [
+        pltpu.make_async_copy(src, out.at[whole, :], sems.at[n])
+        for n, (src, out) in enumerate(zip((new_s, dual_s, tile_s), outs))
+    ]
+    for copy in copies:
+        copy.start()
+    for copy in copies:
+        copy.wait()
+
+
+def last_share_kernel(sz, *refs):
+    share_out, share_dual_out, tile_share_out = refs[-3:]
+    *esums, half_share, share_dual, proj_share = refs[:-3]
     for location, offset in share_places(sz):
         rows = pl.ds(offset, sz.share_chunk)
         which, row = half_of(location, sz.feat_plan.chunks, sz.share_chunk)
@@ -392,7 +435,7 @@
     v16 = lambda *shape: pltpu.VMEM(shape, BF16)
     flops = 2 * rows * feats * cols
 
-    def kernel(body, name, outs, scratch, work, limit, *operands, streamed=0):
+    def kernel(body, name, outs, scratch, work, limit, *operands, streamed=0, stored=False):
         vmem = pl.BlockSpec(memory_space=pltpu.VMEM)
         hbm = pl.BlockSpec(memory_space=pltpu.HBM)
         operands = [
@@ -403,8 +446,9 @@
             body,
             out_shape=outs,
             in_specs=[hbm] * streamed + [vmem] * (len(operands) - streamed),
-            out_specs=[vmem] * len(outs),
+            out_specs=[hbm if stored else vmem] * len(outs),
             scratch_shapes=scratch,
+            input_output_aliases={n: n for n in range(streamed)} if stored else {},
             compiler_params=pltpu.CompilerParams(vmem_limit_bytes=limit * MIB),
             cost_estimate=pl.CostEstimate(flops=work, bytes_accessed=8 * MIB, transcendentals=0),
             name=name,
@@ -431,7 +475,6 @@
             pluses.append(plus)
             waves.append([
                 Sum(sz.colors[2 * half], keep0, send0), Sum(sz.colors[2 * half + 1], keep1, send1)])
-        feat.advance()
         sums, esums = run_sums(waves, feat, pluses[-1])
         groups = [sums[2 * half] + sums[2 * half + 1] for half in range(HALVES)]
         return groups, esums, pluses
@@ -448,7 +491,7 @@
     for half in range(HALVES):
         start, tile_now, half_coef, coef_plus, total = kernel(
             functools.partial(update_kernel, half, sz), f"update{half}", [half_coefs] * 4 + [vector],
-            [v16(sz.half_rows, 2 * cols)], 2 * flops // HALVES, LIMIT,
+            [v16(sz.half_rows, 2 * cols)], 2 * ADD_FLOPS, LIMIT,
             a_hi, a_lo, *groups[half], coef, coef_dual, pluses[half], *prod)
         starts.append(start)
         duals.append(tile_now)
@@ -459,13 +502,17 @@
         [wide_t] + share_sends + [v32(sz.own, cols), vector, vector],
         work, 11 * flops, LIMIT, g_hi, g_lo, *prod, *esums, out_sum, targets, share, share_dual)
     groups, esums, pluses = project(wide, keep_s, send_s, starts, duals)
-    halves = []
+    finals = []
     for half in range(HALVES):
-        halves += [*groups[half], *saved[half], pluses[half]]
-    coef_out, coef_dual_out, tile_out, share_out, share_dual_out, tile_share_out = kernel(
-        functools.partial(last_kernel, sz), "last",
-        [f32(feats, cols)] * 3 + [f32(sz.own, cols), f32(rows, cols), f32(rows, cols)],
-        [], flops // 100, LIMIT, *halves, *esums, half_share, dual_now, proj_share)
+        finals = kernel(
+            functools.partial(last_kernel, half, sz), f"last{half}", [f32(feats, cols)] * 3,
+            [half_coefs] * 3 + [pltpu.SemaphoreType.DMA((3,))], 2 * ADD_FLOPS, LIMIT,
+            *finals, *groups[half], *saved[half], pluses[half], streamed=len(finals), stored=True)
+    coef_out, coef_dual_out, tile_out = finals
+    share_out, share_dual_out, tile_share_out = kernel(
+        functools.partial(last_share_kernel, sz), "last_share",
+        [f32(sz.own, cols), f32(rows, cols), f32(rows, cols)],
+        [], flops // 100, LIMIT, *esums, half_share, dual_now, proj_share)
     return (coef_out, coef_dual_out, tile_out[None], share_out, share_dual_out, tile_share_out[None])
 
 

time: 95.7 us -> 91.9 us (0.960)
  waiting for transfers between devices: 33.6 us -> 18.7 us
  starting transfers between devices: 25.3 us -> 34.4 us
  Pallas kernels: 35.3 us -> 37.6 us
    ppermute x22 -> x34, waiting for transfers between devices: 33.6 us -> 18.7 us  [permute(): lax.ppermute(value, self.axis, [(i, i ^ 1 << bit) for i in range(self.siz...]
    ppermute x22 -> x34, starting transfers between devices: 25.3 us -> 34.4 us  [permute(): lax.ppermute(value, self.axis, [(i, i ^ 1 << bit) for i in range(self.siz...]
    pallas_call x6 -> x11, Pallas kernels: 35.3 us -> 37.3 us  [kernel(): pl.pallas_call(body, out_shape=outs, in_specs=[hbm] * streamed + [vmem] *...]
  transfers between devices with their start and end apart: 22 -> 34, of which waited for: 15 -> 15; matrix products, arithmetic and copies ran while one was open for 0% -> 0% of each run, Pallas kernels for 7% -> 9%
where the time goes in v4:
time: 91.9 us; the launch traced here: 91.7 us
  Pallas kernels  37.6 us (41%)
  starting transfers between devices  34.4 us (37%)
  waiting for transfers between devices  18.7 us (20%)
  between operations  0.92 us (1%)
    pallas_call x11, Pallas kernels, kernel(): pl.pallas_call(body, out_shape=outs, in_specs=[hbm] * streamed + [vmem] *...  37.3 us
    ppermute x34, starting transfers between devices, permute(): lax.ppermute(value, self.axis, [(i, i ^ 1 << bit) for i in range(self.siz...  34.4 us
    ppermute x34, waiting for transfers between devices, permute(): lax.ppermute(value, self.axis, [(i, i ^ 1 << bit) for i in range(self.siz...  18.7 us
  transfers between devices with their start and end apart: 34, of which 15 were waited for; matrix products, arithmetic and copies ran while one was open for 0% of the time, Pallas kernels for 9%

profile of v4, /device:TPU:0, one launch (start us, length us, event | category | flops | bytes accessed | tf_op | source)
XLA Modules:
  0.0 91.7 jit_solution(12510822657365741473)
XLA Ops:
  0.6 19.6 %first.1 = (bf16[1024,2048]{1,0:T(8,128)(2,1)S(1)}, bf16[1024,2048]{1,0:T(8,128)(2,1)S(1)}, bf16[1024,1024]{1,0:T(8,128)(2,1)S(1)}, bf16[1024,1024]{1,0:T(8,128)...) custom-call(f32[1024,2048]{1,0:T(8,128)} %data.1, ...), custom_call_target="tpu_custom_call" | custom-call | flops 16106127360 | bytes 8388608 | tf_op jit(solution)/shard_map/first/pallas_call | solution.py:445
  21.4 3.0 %collective-permute-start.2 = (f32[256,128]{1,0:T(8,128)S(1)}, f32[256,128]{1,0:T(8,128)S(1)}, u32[]{:S(2)}, u32[]{:S(2)}) collective-permute-start(f32[256,128]{1,0:T(8,128)S(1)} %get-tuple-element.115), channel_id=1, source_target_pairs={{0,8},{8,0},{16,24},{24,16},{1,9},{9,1},{17,25},{25,17},{2,10},{10... | collective-permute-start | bytes 393224 | tf_op jit(solution)/shard_map/ppermute | solution.py:82
  24.4 1.5 %collective-permute-start.3 = (f32[256,128]{1,0:T(8,128)S(1)}, f32[256,128]{1,0:T(8,128)S(1)}, u32[]{:S(2)}, u32[]{:S(2)}) collective-permute-start(f32[256,128]{1,0:T(8,128)S(1)} %get-tuple-element.119), channel_id=1, source_target_pairs={{0,16},{8,24},{16,0},{24,8},{1,17},{9,25},{17,1},{25,9},{2,18},{10... | collective-permute-start | bytes 393224 | tf_op jit(solution)/shard_map/ppermute | solution.py:82
  27.9 1.5 %collective-permute-done.3.refs_3_ = f32[256,128]{1,0:T(8,128)S(1)} collective-permute-done((f32[256,128]{1,0:T(8,128)S(1)}, f32[256,128]{1,0:T(8,128)S(1)}, u32[]{:S(2)}, u32[]{:S(2)}) %collective-permute-start.3) | collective-permute-done | bytes 131104 | tf_op jit(solution)/shard_map/ppermute | solution.py:82
  29.4 1.6 %collective-permute-start.6 = (f32[256,128]{1,0:T(8,128)S(1)}, f32[256,128]{1,0:T(8,128)S(1)}, u32[]{:S(2)}, u32[]{:S(2)}) collective-permute-start(f32[256,128]{1,0:T(8,128)S(1)} %get-tuple-element.121.refs_0_), channel_id=1, source_target_pairs={{0,16},{8,24},{16,0},{24,8},{1,17},{9,25},{17,1},{25,9},{2,18},{10... | collective-permute-start | bytes 393224 | tf_op jit(solution)/shard_map/ppermute | solution.py:82
  31.6 2.5 %collective-permute-done.4.refs_3_ = f32[256,128]{1,0:T(8,128)S(1)} collective-permute-done((f32[256,128]{1,0:T(8,128)S(1)}, f32[256,128]{1,0:T(8,128)S(1)}, u32[]{:S(2)}, u32[]{:S(2)}) %collective-permute-start.4) | collective-permute-done | bytes 131104 | tf_op jit(solution)/shard_map/ppermute | solution.py:82
  34.1 1.7 %collective-permute-start.7 = (f32[256,128]{1,0:T(8,128)S(1)}, f32[256,128]{1,0:T(8,128)S(1)}, u32[]{:S(2)}, u32[]{:S(2)}) collective-permute-start(f32[256,128]{1,0:T(8,128)S(1)} %get-tuple-element.200), channel_id=1, source_target_pairs={{0,2},{1,3},{2,0},{3,1},{4,6},{5,7},{6,4},{7,5},{8,10},{9,11},{10,... | collective-permute-start | bytes 393224 | tf_op jit(solution)/shard_map/ppermute | solution.py:82
  36.3 1.5 %collective-permute-start.9 = (f32[256,128]{1,0:T(8,128)S(1)}, f32[256,128]{1,0:T(8,128)S(1)}, u32[]{:S(2)}, u32[]{:S(2)}) collective-permute-start(f32[256,128]{1,0:T(8,128)S(1)} %get-tuple-element.129.refs_2_), channel_id=1, source_target_pairs={{0,8},{8,0},{16,24},{24,16},{1,9},{9,1},{17,25},{25,17},{2,10},{10... | collective-permute-start | bytes 393224 | tf_op jit(solution)/shard_map/ppermute | solution.py:82
  39.1 2.7 %collective-permute-start.14 = (f32[256,128]{1,0:T(8,128)S(1)}, f32[256,128]{1,0:T(8,128)S(1)}, u32[]{:S(2)}, u32[]{:S(2)}) collective-permute-start(f32[256,128]{1,0:T(8,128)S(1)} %sums.17.refs_0_), channel_id=1, source_target_pairs={{0,4},{1,5},{2,6},{3,7},{4,0},{5,1},{6,2},{7,3},{8,12},{9,13},{10,... | collective-permute-start | bytes 393224 | tf_op jit(solution)/shard_map/ppermute | solution.py:82
  41.8 1.6 %collective-permute-start.12 = (f32[256,128]{1,0:T(8,128)S(1)}, f32[256,128]{1,0:T(8,128)S(1)}, u32[]{:S(2)}, u32[]{:S(2)}) collective-permute-start(f32[256,128]{1,0:T(8,128)S(1)} %get-tuple-element.133.refs_2_), channel_id=1, source_target_pairs={{0,8},{8,0},{16,24},{24,16},{1,9},{9,1},{17,25},{25,17},{2,10},{10... | collective-permute-start | bytes 393224 | tf_op jit(solution)/shard_map/ppermute | solution.py:82
  44.5 1.5 %collective-permute-start.11 = (f32[256,128]{1,0:T(8,128)S(1)}, f32[256,128]{1,0:T(8,128)S(1)}, u32[]{:S(2)}, u32[]{:S(2)}) collective-permute-start(f32[256,128]{1,0:T(8,128)S(1)} %get-tuple-element.138.refs_4_), channel_id=1, source_target_pairs={{0,16},{8,24},{16,0},{24,8},{1,17},{9,25},{17,1},{25,9},{2,18},{10... | collective-permute-start | bytes 393224 | tf_op jit(solution)/shard_map/ppermute | solution.py:82
  48.3 1.5 %update0.1 = (f32[1024,128]{1,0:T(8,128)S(1)}, f32[1024,128]{1,0:T(8,128)S(1)}, f32[1024,128]{1,0:T(8,128)S(1)}, f32[1024,128]{1,0:T(8,128)S(1)}, f32[1024,128]{1,0:T(8,128)S(1)}) custom-call(bf16[1024,2048]{1,0:T(8,128)(2,1)S(1)} %get-tuple-element.104.a_hi.refs_0_, bf16[1024,2048]{1,0:T(8,128)(2,1)S(1)} %get-tuple-element.105.a_lo.refs_1_, ...), custom_call_target="tpu_custom_call" | custom-call | flops 8000000000 | bytes 8388608 | tf_op jit(solution)/shard_map/update0/pallas_call | solution.py:445
  49.8 1.8 %collective-permute-done.15 = f32[256,128]{1,0:T(8,128)S(1)} collective-permute-done((f32[256,128]{1,0:T(8,128)S(1)}, f32[256,128]{1,0:T(8,128)S(1)}, u32[]{:S(2)}, u32[]{:S(2)}) %collective-permute-start.15) | collective-permute-done | bytes 131104 | tf_op jit(solution)/shard_map/ppermute | solution.py:82
  51.8 1.5 %update1.1 = (f32[1024,128]{1,0:T(8,128)S(1)}, f32[1024,128]{1,0:T(8,128)S(1)}, f32[1024,128]{1,0:T(8,128)S(1)}, f32[1024,128]{1,0:T(8,128)S(1)}, f32[1024,128]{1,0:T(8,128)S(1)}) custom-call(bf16[1024,2048]{1,0:T(8,128)(2,1)S(1)} %get-tuple-element.104.a_hi.refs_0_, bf16[1024,2048]{1,0:T(8,128)(2,1)S(1)} %get-tuple-element.105.a_lo.refs_1_, ...), custom_call_target="tpu_custom_call" | custom-call | flops 8000000000 | bytes 8388608 | tf_op jit(solution)/shard_map/update1/pallas_call | solution.py:445
  53.3 6.4 %second.1 = (bf16[256,1024]{1,0:T(8,128)(2,1)S(1)}, f32[512,128]{1,0:T(8,128)S(1)}, f32[512,128]{1,0:T(8,128)S(1)}, f32[128,128]{1,0:T(8,128)S(1)}, f32[1024,128]{1,0:T(8,128)S(1)}, /*index=5*/f32[1024,128]{1,0:T(8,128)S(1)}) custom-call(bf16[1024,1024]{1,0:T(8,128)(2,1)S(1)} %get-tuple-element.102.g_hi, bf16[1024,1024]{1,0:T(8,128)(2,1)S(1)} %get-tuple-element.103.g_lo, ...), custom_call_target="tpu_custom_call" | custom-call | flops 5905580032 | bytes 8388608 | tf_op jit(solution)/shard_map/second/pallas_call | solution.py:445
  60.9 1.6 %collective-permute-start.17 = (f32[256,128]{1,0:T(8,128)S(1)}, f32[256,128]{1,0:T(8,128)S(1)}, u32[]{:S(2)}, u32[]{:S(2)}) collective-permute-start(f32[256,128]{1,0:T(8,128)S(1)} %get-tuple-element.148), channel_id=1, source_target_pairs={{0,8},{8,0},{16,24},{24,16},{1,9},{9,1},{17,25},{25,17},{2,10},{10... | collective-permute-start | bytes 393224 | tf_op jit(solution)/shard_map/ppermute | solution.py:82
  64.4 1.9 %collective-permute-start.23 = (f32[256,128]{1,0:T(8,128)S(1)}, f32[256,128]{1,0:T(8,128)S(1)}, u32[]{:S(2)}, u32[]{:S(2)}) collective-permute-start(f32[256,128]{1,0:T(8,128)S(1)} %get-tuple-element.167), channel_id=1, source_target_pairs={{0,16},{8,24},{16,0},{24,8},{1,17},{9,25},{17,1},{25,9},{2,18},{10... | collective-permute-start | bytes 393224 | tf_op jit(solution)/shard_map/ppermute | solution.py:82
  66.9 1.9 %collective-permute-done.18.refs_3_ = f32[256,128]{1,0:T(8,128)S(1)} collective-permute-done((f32[256,128]{1,0:T(8,128)S(1)}, f32[256,128]{1,0:T(8,128)S(1)}, u32[]{:S(2)}, u32[]{:S(2)}) %collective-permute-start.18) | collective-permute-done | bytes 131104 | tf_op jit(solution)/shard_map/ppermute | solution.py:82
  69.6 1.9 %collective-permute-done.23.refs_3_ = f32[256,128]{1,0:T(8,128)S(1)} collective-permute-done((f32[256,128]{1,0:T(8,128)S(1)}, f32[256,128]{1,0:T(8,128)S(1)}, u32[]{:S(2)}, u32[]{:S(2)}) %collective-permute-start.23) | collective-permute-done | bytes 131104 | tf_op jit(solution)/shard_map/ppermute | solution.py:82
  73.3 2.0 %collective-permute-start.28 = (f32[256,128]{1,0:T(8,128)S(1)}, f32[256,128]{1,0:T(8,128)S(1)}, u32[]{:S(2)}, u32[]{:S(2)}) collective-permute-start(f32[256,128]{1,0:T(8,128)S(1)} %get-tuple-element.170.refs_2_), channel_id=1, source_target_pairs={{0,8},{8,0},{16,24},{24,16},{1,9},{9,1},{17,25},{25,17},{2,10},{10... | collective-permute-start | bytes 393224 | tf_op jit(solution)/shard_map/ppermute | solution.py:82
  76.6 2.1 %collective-permute-start.31 = (f32[256,128]{1,0:T(8,128)S(1)}, f32[256,128]{1,0:T(8,128)S(1)}, u32[]{:S(2)}, u32[]{:S(2)}) collective-permute-start(f32[256,128]{1,0:T(8,128)S(1)} %sums.24.refs_0_), channel_id=1, source_target_pairs={{0,4},{1,5},{2,6},{3,7},{4,0},{5,1},{6,2},{7,3},{8,12},{9,13},{10,... | collective-permute-start | bytes 393224 | tf_op jit(solution)/shard_map/ppermute | solution.py:82
  79.0 2.8 %collective-permute-start.26 = (f32[256,128]{1,0:T(8,128)S(1)}, f32[256,128]{1,0:T(8,128)S(1)}, u32[]{:S(2)}, u32[]{:S(2)}) collective-permute-start(f32[256,128]{1,0:T(8,128)S(1)} %get-tuple-element.175.refs_2_), channel_id=1, source_target_pairs={{0,16},{8,24},{16,0},{24,8},{1,17},{9,25},{17,1},{25,9},{2,18},{10... | collective-permute-start | bytes 393224 | tf_op jit(solution)/shard_map/ppermute | solution.py:82
  86.3 2.7 %collective-permute-done.32 = f32[256,128]{1,0:T(8,128)S(1)} collective-permute-done((f32[256,128]{1,0:T(8,128)S(1)}, f32[256,128]{1,0:T(8,128)S(1)}, u32[]{:S(2)}, u32[]{:S(2)}) %collective-permute-start.32) | collective-permute-done | bytes 131104 | tf_op jit(solution)/shard_map/ppermute | solution.py:82
  89.2 1.3 %last1.1 = (f32[2048,128]{1,0:T(8,128)}, f32[2048,128]{1,0:T(8,128)}, f32[2048,128]{1,0:T(8,128)}) custom-call(f32[2048,128]{1,0:T(8,128)} %get-tuple-element.178.refs_0_, f32[2048,128]{1,0:T(8,128)} %get-tuple-element.179.refs_1_, f32[2048,128]{1,0:T(8,128)} %get-tuple-element.180.refs_2_, ...), custom_call_target="tpu_custom_call", output_to_operand_aliasing={{0}: (0, {}), {1}: (1, {}), {2}: (2, {})} | custom-call | flops 8000000000 | bytes 8388608 | tf_op jit(solution)/shard_map/last1/pallas_call | solution.py:445
  (85 shorter events, 23.1 us)
Async XLA Ops:
  21.4 6.5 %collective-permute-start.2 = (f32[256,128]{1,0:T(8,128)S(1)}, f32[256,128]{1,0:T(8,128)S(1)}, u32[]{:S(2)}, u32[]{:S(2)}) collective-permute-start(f32[256,128]{1,0:T(8,128)S(1)} %get-tuple-element.115), channel_id=1, source_target_pairs={{0,8},{8,0},{16,24},{24,16},{1,9},{9,1},{17,25},{25,17},{2,10},{10... | collective-permute-start | bytes 393224 | tf_op jit(solution)/shard_map/ppermute | solution.py:82
  25.9 5.6 %collective-permute-start.1 = (f32[512,128]{1,0:T(8,128)S(1)}, f32[512,128]{1,0:T(8,128)S(1)}, u32[]{:S(2)}, u32[]{:S(2)}) collective-permute-start(f32[512,128]{1,0:T(8,128)S(1)} %get-tuple-element.113), channel_id=1, source_target_pairs={{0,1},{1,0},{2,3},{3,2},{4,5},{5,4},{6,7},{7,6},{8,9},{9,8},{10,11... | collective-permute-start | bytes 786440 | tf_op jit(solution)/shard_map/ppermute | solution.py:82
  27.1 7.0 %collective-permute-start = (f32[256,128]{1,0:T(8,128)S(1)}, f32[256,128]{1,0:T(8,128)S(1)}, u32[]{:S(2)}, u32[]{:S(2)}) collective-permute-start(f32[256,128]{1,0:T(8,128)S(1)} %get-tuple-element.111), channel_id=1, source_target_pairs={{0,8},{8,0},{16,24},{24,16},{1,9},{9,1},{17,25},{25,17},{2,10},{10... | collective-permute-start | bytes 393224 | tf_op jit(solution)/shard_map/ppermute | solution.py:82
  27.7 6.3 %collective-permute-start.4 = (f32[256,128]{1,0:T(8,128)S(1)}, f32[256,128]{1,0:T(8,128)S(1)}, u32[]{:S(2)}, u32[]{:S(2)}) collective-permute-start(f32[256,128]{1,0:T(8,128)S(1)} %get-tuple-element.126), channel_id=1, source_target_pairs={{0,16},{8,24},{16,0},{24,8},{1,17},{9,25},{17,1},{25,9},{2,18},{10... | collective-permute-start | bytes 393224 | tf_op jit(solution)/shard_map/ppermute | solution.py:82
  29.4 12.4 %collective-permute-start.6 = (f32[256,128]{1,0:T(8,128)S(1)}, f32[256,128]{1,0:T(8,128)S(1)}, u32[]{:S(2)}, u32[]{:S(2)}) collective-permute-start(f32[256,128]{1,0:T(8,128)S(1)} %get-tuple-element.121.refs_0_), channel_id=1, source_target_pairs={{0,16},{8,24},{16,0},{24,8},{1,17},{9,25},{17,1},{25,9},{2,18},{10... | collective-permute-start | bytes 393224 | tf_op jit(solution)/shard_map/ppermute | solution.py:82
  31.0 10.8 %collective-permute-start.8 = (f32[256,128]{1,0:T(8,128)S(1)}, f32[256,128]{1,0:T(8,128)S(1)}, u32[]{:S(2)}, u32[]{:S(2)}) collective-permute-start(f32[256,128]{1,0:T(8,128)S(1)} %get-tuple-element.122.refs_2_), channel_id=1, source_target_pairs={{0,8},{8,0},{16,24},{24,16},{1,9},{9,1},{17,25},{25,17},{2,10},{10... | collective-permute-start | bytes 393224 | tf_op jit(solution)/shard_map/ppermute | solution.py:82
  35.7 8.1 %collective-permute-start.5 = (f32[256,128]{1,0:T(8,128)S(1)}, f32[256,128]{1,0:T(8,128)S(1)}, u32[]{:S(2)}, u32[]{:S(2)}) collective-permute-start(f32[256,128]{1,0:T(8,128)S(1)} %get-tuple-element.128.refs_0_), channel_id=1, source_target_pairs={{0,16},{8,24},{16,0},{24,8},{1,17},{9,25},{17,1},{25,9},{2,18},{10... | collective-permute-start | bytes 393224 | tf_op jit(solution)/shard_map/ppermute | solution.py:82
  36.3 7.6 %collective-permute-start.9 = (f32[256,128]{1,0:T(8,128)S(1)}, f32[256,128]{1,0:T(8,128)S(1)}, u32[]{:S(2)}, u32[]{:S(2)}) collective-permute-start(f32[256,128]{1,0:T(8,128)S(1)} %get-tuple-element.129.refs_2_), channel_id=1, source_target_pairs={{0,8},{8,0},{16,24},{24,16},{1,9},{9,1},{17,25},{25,17},{2,10},{10... | collective-permute-start | bytes 393224 | tf_op jit(solution)/shard_map/ppermute | solution.py:82
  39.1 7.4 %collective-permute-start.14 = (f32[256,128]{1,0:T(8,128)S(1)}, f32[256,128]{1,0:T(8,128)S(1)}, u32[]{:S(2)}, u32[]{:S(2)}) collective-permute-start(f32[256,128]{1,0:T(8,128)S(1)} %sums.17.refs_0_), channel_id=1, source_target_pairs={{0,4},{1,5},{2,6},{3,7},{4,0},{5,1},{6,2},{7,3},{8,12},{9,13},{10,... | collective-permute-start | bytes 393224 | tf_op jit(solution)/shard_map/ppermute | solution.py:82
  41.8 5.9 %collective-permute-start.12 = (f32[256,128]{1,0:T(8,128)S(1)}, f32[256,128]{1,0:T(8,128)S(1)}, u32[]{:S(2)}, u32[]{:S(2)}) collective-permute-start(f32[256,128]{1,0:T(8,128)S(1)} %get-tuple-element.133.refs_2_), channel_id=1, source_target_pairs={{0,8},{8,0},{16,24},{24,16},{1,9},{9,1},{17,25},{25,17},{2,10},{10... | collective-permute-start | bytes 393224 | tf_op jit(solution)/shard_map/ppermute | solution.py:82
  43.9 7.8 %collective-permute-start.10 = (f32[256,128]{1,0:T(8,128)S(1)}, f32[256,128]{1,0:T(8,128)S(1)}, u32[]{:S(2)}, u32[]{:S(2)}) collective-permute-start(f32[256,128]{1,0:T(8,128)S(1)} %get-tuple-element.137.refs_2_), channel_id=1, source_target_pairs={{0,8},{8,0},{16,24},{24,16},{1,9},{9,1},{17,25},{25,17},{2,10},{10... | collective-permute-start | bytes 393224 | tf_op jit(solution)/shard_map/ppermute | solution.py:82
  44.5 7.2 %collective-permute-start.11 = (f32[256,128]{1,0:T(8,128)S(1)}, f32[256,128]{1,0:T(8,128)S(1)}, u32[]{:S(2)}, u32[]{:S(2)}) collective-permute-start(f32[256,128]{1,0:T(8,128)S(1)} %get-tuple-element.138.refs_4_), channel_id=1, source_target_pairs={{0,16},{8,24},{16,0},{24,8},{1,17},{9,25},{17,1},{25,9},{2,18},{10... | collective-permute-start | bytes 393224 | tf_op jit(solution)/shard_map/ppermute | solution.py:82
  60.9 6.0 %collective-permute-start.17 = (f32[256,128]{1,0:T(8,128)S(1)}, f32[256,128]{1,0:T(8,128)S(1)}, u32[]{:S(2)}, u32[]{:S(2)}) collective-permute-start(f32[256,128]{1,0:T(8,128)S(1)} %get-tuple-element.148), channel_id=1, source_target_pairs={{0,8},{8,0},{16,24},{24,16},{1,9},{9,1},{17,25},{25,17},{2,10},{10... | collective-permute-start | bytes 393224 | tf_op jit(solution)/shard_map/ppermute | solution.py:82
  62.4 6.3 %collective-permute-start.18 = (f32[256,128]{1,0:T(8,128)S(1)}, f32[256,128]{1,0:T(8,128)S(1)}, u32[]{:S(2)}, u32[]{:S(2)}) collective-permute-start(f32[256,128]{1,0:T(8,128)S(1)} %get-tuple-element.156), channel_id=1, source_target_pairs={{0,16},{8,24},{16,0},{24,8},{1,17},{9,25},{17,1},{25,9},{2,18},{10... | collective-permute-start | bytes 393224 | tf_op jit(solution)/shard_map/ppermute | solution.py:82
  64.4 7.2 %collective-permute-start.23 = (f32[256,128]{1,0:T(8,128)S(1)}, f32[256,128]{1,0:T(8,128)S(1)}, u32[]{:S(2)}, u32[]{:S(2)}) collective-permute-start(f32[256,128]{1,0:T(8,128)S(1)} %get-tuple-element.167), channel_id=1, source_target_pairs={{0,16},{8,24},{16,0},{24,8},{1,17},{9,25},{17,1},{25,9},{2,18},{10... | collective-permute-start | bytes 393224 | tf_op jit(solution)/shard_map/ppermute | solution.py:82
  68.8 9.9 %collective-permute-start.19 = (f32[256,128]{1,0:T(8,128)S(1)}, f32[256,128]{1,0:T(8,128)S(1)}, u32[]{:S(2)}, u32[]{:S(2)}) collective-permute-start(f32[256,128]{1,0:T(8,128)S(1)} %get-tuple-element.158.refs_0_), channel_id=1, source_target_pairs={{0,16},{8,24},{16,0},{24,8},{1,17},{9,25},{17,1},{25,9},{2,18},{10... | collective-permute-start | bytes 393224 | tf_op jit(solution)/shard_map/ppermute | solution.py:82
  68.9 9.8 %collective-permute-start.24 = (f32[256,128]{1,0:T(8,128)S(1)}, f32[256,128]{1,0:T(8,128)S(1)}, u32[]{:S(2)}, u32[]{:S(2)}) collective-permute-start(f32[256,128]{1,0:T(8,128)S(1)} %get-tuple-element.161.refs_2_), channel_id=1, source_target_pairs={{0,8},{8,0},{16,24},{24,16},{1,9},{9,1},{17,25},{25,17},{2,10},{10... | collective-permute-start | bytes 393224 | tf_op jit(solution)/shard_map/ppermute | solution.py:82
  72.7 9.1 %collective-permute-start.27 = (f32[256,128]{1,0:T(8,128)S(1)}, f32[256,128]{1,0:T(8,128)S(1)}, u32[]{:S(2)}, u32[]{:S(2)}) collective-permute-start(f32[256,128]{1,0:T(8,128)S(1)} %get-tuple-element.169.refs_0_), channel_id=1, source_target_pairs={{0,16},{8,24},{16,0},{24,8},{1,17},{9,25},{17,1},{25,9},{2,18},{10... | collective-permute-start | bytes 393224 | tf_op jit(solution)/shard_map/ppermute | solution.py:82
  73.3 8.5 %collective-permute-start.28 = (f32[256,128]{1,0:T(8,128)S(1)}, f32[256,128]{1,0:T(8,128)S(1)}, u32[]{:S(2)}, u32[]{:S(2)}) collective-permute-start(f32[256,128]{1,0:T(8,128)S(1)} %get-tuple-element.170.refs_2_), channel_id=1, source_target_pairs={{0,8},{8,0},{16,24},{24,16},{1,9},{9,1},{17,25},{25,17},{2,10},{10... | collective-permute-start | bytes 393224 | tf_op jit(solution)/shard_map/ppermute | solution.py:82
  76.6 7.4 %collective-permute-start.31 = (f32[256,128]{1,0:T(8,128)S(1)}, f32[256,128]{1,0:T(8,128)S(1)}, u32[]{:S(2)}, u32[]{:S(2)}) collective-permute-start(f32[256,128]{1,0:T(8,128)S(1)} %sums.24.refs_0_), channel_id=1, source_target_pairs={{0,4},{1,5},{2,6},{3,7},{4,0},{5,1},{6,2},{7,3},{8,12},{9,13},{10,... | collective-permute-start | bytes 393224 | tf_op jit(solution)/shard_map/ppermute | solution.py:82
  78.7 6.3 %collective-permute-start.25 = (f32[256,128]{1,0:T(8,128)S(1)}, f32[256,128]{1,0:T(8,128)S(1)}, u32[]{:S(2)}, u32[]{:S(2)}) collective-permute-start(f32[256,128]{1,0:T(8,128)S(1)} %get-tuple-element.174.refs_0_), channel_id=1, source_target_pairs={{0,8},{8,0},{16,24},{24,16},{1,9},{9,1},{17,25},{25,17},{2,10},{10... | collective-permute-start | bytes 393224 | tf_op jit(solution)/shard_map/ppermute | solution.py:82
  79.0 6.1 %collective-permute-start.26 = (f32[256,128]{1,0:T(8,128)S(1)}, f32[256,128]{1,0:T(8,128)S(1)}, u32[]{:S(2)}, u32[]{:S(2)}) collective-permute-start(f32[256,128]{1,0:T(8,128)S(1)} %get-tuple-element.175.refs_2_), channel_id=1, source_target_pairs={{0,16},{8,24},{16,0},{24,8},{1,17},{9,25},{17,1},{25,9},{2,18},{10... | collective-permute-start | bytes 393224 | tf_op jit(solution)/shard_map/ppermute | solution.py:82
  81.8 7.4 %collective-permute-start.29 = (f32[256,128]{1,0:T(8,128)S(1)}, f32[256,128]{1,0:T(8,128)S(1)}, u32[]{:S(2)}, u32[]{:S(2)}) collective-permute-start(f32[256,128]{1,0:T(8,128)S(1)} %get-tuple-element.183.refs_3_), channel_id=1, source_target_pairs={{0,8},{8,0},{16,24},{24,16},{1,9},{9,1},{17,25},{25,17},{2,10},{10... | collective-permute-start | bytes 393224 | tf_op jit(solution)/shard_map/ppermute | solution.py:82
  81.9 7.2 %collective-permute-start.30 = (f32[256,128]{1,0:T(8,128)S(1)}, f32[256,128]{1,0:T(8,128)S(1)}, u32[]{:S(2)}, u32[]{:S(2)}) collective-permute-start(f32[256,128]{1,0:T(8,128)S(1)} %get-tuple-element.184.refs_5_), channel_id=1, source_target_pairs={{0,16},{8,24},{16,0},{24,8},{1,17},{9,25},{17,1},{25,9},{2,18},{10... | collective-permute-start | bytes 393224 | tf_op jit(solution)/shard_map/ppermute | solution.py:82
  (16 other events, 73.4 us)

commit v5 on v4

--- a/solution.py
+++ b/solution.py
@@ -19,6 +19,7 @@
 MIB = 1 << 20
 LIMIT = 16
 HALVES = 2
+FULL_STEPS = 4
 ADD_FLOPS = 4 * 10**9
 
 
@@ -154,7 +155,8 @@
     before, turns = last, rounds * len(waves)
     for turn in range(turns):
         before = step_all(waves[turn % len(waves)], before)
-        while feat.step < min(feat.plan.levels, -(-feat.plan.levels * (turn + 1) // (turns - 1))):
+        levels = feat.plan.levels
+        while feat.step < 1 + min(levels, 1 + (levels - 1) * turn // (turns - 1)):
             before = step_all([feat], before)
     while feat.step < extra:
         before = step_all([feat], before)
@@ -235,7 +237,11 @@
         last = step + 1 == CHEB
         now, later = search2.at[step % 2], search2.at[(step + 1) % 2]
         for rows in blocks:
-            prod = triple(g_hi, g_lo, rows, now, cols)
+            if step < FULL_STEPS:
+                prod = triple(g_hi, g_lo, rows, now, cols)
+            else:
+                wide = dot_nn(g_hi[rows, :], now[...])
+                prod = wide[:, :cols] + wide[:, cols:]
             if step == 0:
                 part[rows, :] = prod
             else:
@@ -463,19 +469,19 @@
     work = [vector, vector, v16(2, rows, 2 * cols), vector, vector]
     tile_dual = tile_coef_dual[0]
 
-    def project(wide, keep_s, send_s, starts, duals):
+    def project(wide, keep_s, send_s, starts, duals, early):
         feat = Sum(sz.feat_plan, keep_s, send_s)
         waves, pluses = [], []
         for half in range(HALVES):
             if half:
-                wide, _ = lax.optimization_barrier((wide, pluses[-1]))
+                wide, _ = lax.optimization_barrier((wide, step_all([feat], pluses[-1]) if early else pluses[-1]))
             keep0, keep1, send0, send1, plus = kernel(
                 functools.partial(spread_kernel, half, sz), f"spread{half}", coef_sends + [half_coefs],
                 [half_coefs], 3 * flops // HALVES, LIMIT, wide, a_hi, a_lo, starts[half], duals[half])
             pluses.append(plus)
             waves.append([
                 Sum(sz.colors[2 * half], keep0, send0), Sum(sz.colors[2 * half + 1], keep1, send1)])
-        sums, esums = run_sums(waves, feat, pluses[-1])
+        sums, esums = run_sums(waves, feat, pluses[-1] if early else step_all([feat], pluses[-1]))
         groups = [sums[2 * half] + sums[2 * half + 1] for half in range(HALVES)]
         return groups, esums, pluses
 
@@ -486,7 +492,7 @@
          v32(sz.own, cols), v16(feats, 2 * cols)] + work
         + [pltpu.SemaphoreType.DMA((blocks,)), pltpu.SemaphoreType.DMA((6,))], 30 * flops, 24,
         data, coef, tile_dual, share_dual, tile_share[0], share, targets, streamed=7)
-    groups, esums, pluses = project(wide, keep_s, send_s, [start] * HALVES, [tile_dual] * HALVES)
+    groups, esums, pluses = project(wide, keep_s, send_s, [start] * HALVES, [tile_dual] * HALVES, True)
     starts, duals, saved, prod = [], [], [], []
     for half in range(HALVES):
         start, tile_now, half_coef, coef_plus, total = kernel(
@@ -501,7 +507,7 @@
         functools.partial(second_kernel, sz), "second",
         [wide_t] + share_sends + [v32(sz.own, cols), vector, vector],
         work, 11 * flops, LIMIT, g_hi, g_lo, *prod, *esums, out_sum, targets, share, share_dual)
-    groups, esums, pluses = project(wide, keep_s, send_s, starts, duals)
+    groups, esums, pluses = project(wide, keep_s, send_s, starts, duals, False)
     finals = []
     for half in range(HALVES):
         finals = kernel(

time: 91.9 us -> 94.3 us (1.026)
  waiting for transfers between devices: 18.7 us -> 22.3 us
  Pallas kernels: 37.6 us -> 36.5 us
    ppermute x34, waiting for transfers between devices: 18.7 us -> 22.3 us  [permute(): lax.ppermute(value, self.axis, [(i, i ^ 1 << bit) for i in range(self.siz...]
    pallas_call x11, Pallas kernels: 37.3 us -> 36.2 us  [kernel(): pl.pallas_call(body, out_shape=outs, in_specs=[hbm] * streamed + [vmem] *...]
  transfers between devices with their start and end apart: 34 -> 34, of which waited for: 15 -> 13; matrix products, arithmetic and copies ran while one was open for 0% -> 0% of each run, Pallas kernels for 9% -> 11%
where the time goes in v5:
time: 94.3 us; the launch traced here: 94.1 us
  Pallas kernels  36.5 us (39%)
  starting transfers between devices  34.3 us (36%)
  waiting for transfers between devices  22.3 us (24%)
  between operations  0.98 us (1%)
    pallas_call x11, Pallas kernels, kernel(): pl.pallas_call(body, out_shape=outs, in_specs=[hbm] * streamed + [vmem] *...  36.2 us
    ppermute x34, starting transfers between devices, permute(): lax.ppermute(value, self.axis, [(i, i ^ 1 << bit) for i in range(self.siz...  34.3 us
    ppermute x34, waiting for transfers between devices, permute(): lax.ppermute(value, self.axis, [(i, i ^ 1 << bit) for i in range(self.siz...  22.3 us
  transfers between devices with their start and end apart: 34, of which 13 were waited for; matrix products, arithmetic and copies ran while one was open for 0% of the time, Pallas kernels for 11%

profile of v5, /device:TPU:0, one launch (start us, length us, event | category | flops | bytes accessed | tf_op | source)
XLA Modules:
  0.0 94.1 jit_solution(5424300052704032350)
XLA Ops:
  0.6 19.0 %first.1 = (bf16[1024,2048]{1,0:T(8,128)(2,1)S(1)}, bf16[1024,2048]{1,0:T(8,128)(2,1)S(1)}, bf16[1024,1024]{1,0:T(8,128)(2,1)S(1)}, bf16[1024,1024]{1,0:T(8,128)...) custom-call(f32[1024,2048]{1,0:T(8,128)} %data.1, ...), custom_call_target="tpu_custom_call" | custom-call | flops 16106127360 | bytes 8388608 | tf_op jit(solution)/shard_map/first/pallas_call | solution.py:451
  21.4 2.6 %collective-permute-start.3 = (f32[256,128]{1,0:T(8,128)S(1)}, f32[256,128]{1,0:T(8,128)S(1)}, u32[]{:S(2)}, u32[]{:S(2)}) collective-permute-start(f32[256,128]{1,0:T(8,128)S(1)} %get-tuple-element.116), channel_id=1, source_target_pairs={{0,8},{8,0},{16,24},{24,16},{1,9},{9,1},{17,25},{25,17},{2,10},{10... | collective-permute-start | bytes 393224 | tf_op jit(solution)/shard_map/ppermute | solution.py:83
  23.9 1.5 %collective-permute-start.4 = (f32[256,128]{1,0:T(8,128)S(1)}, f32[256,128]{1,0:T(8,128)S(1)}, u32[]{:S(2)}, u32[]{:S(2)}) collective-permute-start(f32[256,128]{1,0:T(8,128)S(1)} %get-tuple-element.120), channel_id=1, source_target_pairs={{0,16},{8,24},{16,0},{24,8},{1,17},{9,25},{17,1},{25,9},{2,18},{10... | collective-permute-start | bytes 393224 | tf_op jit(solution)/shard_map/ppermute | solution.py:83
  29.5 1.6 %collective-permute-start.2 = (f32[256,128]{1,0:T(8,128)S(1)}, f32[256,128]{1,0:T(8,128)S(1)}, u32[]{:S(2)}, u32[]{:S(2)}) collective-permute-start(f32[256,128]{1,0:T(8,128)S(1)} %get-tuple-element.200), channel_id=1, source_target_pairs={{0,2},{1,3},{2,0},{3,1},{4,6},{5,7},{6,4},{7,5},{8,10},{9,11},{10,... | collective-permute-start | bytes 393224 | tf_op jit(solution)/shard_map/ppermute | solution.py:83
  31.1 2.3 %collective-permute-start.7 = (f32[256,128]{1,0:T(8,128)S(1)}, f32[256,128]{1,0:T(8,128)S(1)}, u32[]{:S(2)}, u32[]{:S(2)}) collective-permute-start(f32[256,128]{1,0:T(8,128)S(1)} %get-tuple-element.122.refs_0_), channel_id=1, source_target_pairs={{0,16},{8,24},{16,0},{24,8},{1,17},{9,25},{17,1},{25,9},{2,18},{10... | collective-permute-start | bytes 393224 | tf_op jit(solution)/shard_map/ppermute | solution.py:83
  34.5 2.7 %collective-permute-start.14 = (f32[256,128]{1,0:T(8,128)S(1)}, f32[256,128]{1,0:T(8,128)S(1)}, u32[]{:S(2)}, u32[]{:S(2)}) collective-permute-start(f32[256,128]{1,0:T(8,128)S(1)} %sums.16.refs_0_), channel_id=1, source_target_pairs={{0,4},{1,5},{2,6},{3,7},{4,0},{5,1},{6,2},{7,3},{8,12},{9,13},{10,... | collective-permute-start | bytes 393224 | tf_op jit(solution)/shard_map/ppermute | solution.py:83
  37.2 2.3 %collective-permute-start.6 = (f32[256,128]{1,0:T(8,128)S(1)}, f32[256,128]{1,0:T(8,128)S(1)}, u32[]{:S(2)}, u32[]{:S(2)}) collective-permute-start(f32[256,128]{1,0:T(8,128)S(1)} %get-tuple-element.129.refs_0_), channel_id=1, source_target_pairs={{0,16},{8,24},{16,0},{24,8},{1,17},{9,25},{17,1},{25,9},{2,18},{10... | collective-permute-start | bytes 393224 | tf_op jit(solution)/shard_map/ppermute | solution.py:83
  39.6 2.0 %collective-permute-start.12 = (f32[256,128]{1,0:T(8,128)S(1)}, f32[256,128]{1,0:T(8,128)S(1)}, u32[]{:S(2)}, u32[]{:S(2)}) collective-permute-start(f32[256,128]{1,0:T(8,128)S(1)} %get-tuple-element.133.refs_2_), channel_id=1, source_target_pairs={{0,8},{8,0},{16,24},{24,16},{1,9},{9,1},{17,25},{25,17},{2,10},{10... | collective-permute-start | bytes 393224 | tf_op jit(solution)/shard_map/ppermute | solution.py:83
  41.7 1.7 %collective-permute-done.6.refs_1_ = f32[256,128]{1,0:T(8,128)S(1)} collective-permute-done((f32[256,128]{1,0:T(8,128)S(1)}, f32[256,128]{1,0:T(8,128)S(1)}, u32[]{:S(2)}, u32[]{:S(2)}) %collective-permute-start.6) | collective-permute-done | bytes 131104 | tf_op jit(solution)/shard_map/ppermute | solution.py:83
  43.4 2.3 %collective-permute-done.9.refs_3_ = f32[256,128]{1,0:T(8,128)S(1)} collective-permute-done((f32[256,128]{1,0:T(8,128)S(1)}, f32[256,128]{1,0:T(8,128)S(1)}, u32[]{:S(2)}, u32[]{:S(2)}) %collective-permute-start.9) | collective-permute-done | bytes 131104 | tf_op jit(solution)/shard_map/ppermute | solution.py:83
  46.0 1.6 %collective-permute-start.15 = (f32[256,128]{1,0:T(8,128)S(1)}, f32[256,128]{1,0:T(8,128)S(1)}, u32[]{:S(2)}, u32[]{:S(2)}) collective-permute-start(f32[256,128]{1,0:T(8,128)S(1)} %sums.20), channel_id=1, source_target_pairs={{0,2},{1,3},{2,0},{3,1},{4,6},{5,7},{6,4},{7,5},{8,10},{9,11},{10,... | collective-permute-start | bytes 393224 | tf_op jit(solution)/shard_map/ppermute | solution.py:83
  47.6 1.5 %update0.1 = (f32[1024,128]{1,0:T(8,128)S(1)}, f32[1024,128]{1,0:T(8,128)S(1)}, f32[1024,128]{1,0:T(8,128)S(1)}, f32[1024,128]{1,0:T(8,128)S(1)}, f32[1024,128]{1,0:T(8,128)S(1)}) custom-call(bf16[1024,2048]{1,0:T(8,128)(2,1)S(1)} %get-tuple-element.104.a_hi.refs_0_, bf16[1024,2048]{1,0:T(8,128)(2,1)S(1)} %get-tuple-element.105.a_lo.refs_1_, ...), custom_call_target="tpu_custom_call" | custom-call | flops 8000000000 | bytes 8388608 | tf_op jit(solution)/shard_map/update0/pallas_call | solution.py:451
  49.1 1.9 %collective-permute-done.15 = f32[256,128]{1,0:T(8,128)S(1)} collective-permute-done((f32[256,128]{1,0:T(8,128)S(1)}, f32[256,128]{1,0:T(8,128)S(1)}, u32[]{:S(2)}, u32[]{:S(2)}) %collective-permute-start.15) | collective-permute-done | bytes 131104 | tf_op jit(solution)/shard_map/ppermute | solution.py:83
  51.1 1.5 %update1.1 = (f32[1024,128]{1,0:T(8,128)S(1)}, f32[1024,128]{1,0:T(8,128)S(1)}, f32[1024,128]{1,0:T(8,128)S(1)}, f32[1024,128]{1,0:T(8,128)S(1)}, f32[1024,128]{1,0:T(8,128)S(1)}) custom-call(bf16[1024,2048]{1,0:T(8,128)(2,1)S(1)} %get-tuple-element.104.a_hi.refs_0_, bf16[1024,2048]{1,0:T(8,128)(2,1)S(1)} %get-tuple-element.105.a_lo.refs_1_, ...), custom_call_target="tpu_custom_call" | custom-call | flops 8000000000 | bytes 8388608 | tf_op jit(solution)/shard_map/update1/pallas_call | solution.py:451
  52.7 5.8 %second.1 = (bf16[256,1024]{1,0:T(8,128)(2,1)S(1)}, f32[512,128]{1,0:T(8,128)S(1)}, f32[512,128]{1,0:T(8,128)S(1)}, f32[128,128]{1,0:T(8,128)S(1)}, f32[1024,128]{1,0:T(8,128)S(1)}, /*index=5*/f32[1024,128]{1,0:T(8,128)S(1)}) custom-call(bf16[1024,1024]{1,0:T(8,128)(2,1)S(1)} %get-tuple-element.102.g_hi, bf16[1024,1024]{1,0:T(8,128)(2,1)S(1)} %get-tuple-element.103.g_lo, ...), custom_call_target="tpu_custom_call" | custom-call | flops 5905580032 | bytes 8388608 | tf_op jit(solution)/shard_map/second/pallas_call | solution.py:451
  61.4 2.0 %collective-permute-start.21 = (f32[256,128]{1,0:T(8,128)S(1)}, f32[256,128]{1,0:T(8,128)S(1)}, u32[]{:S(2)}, u32[]{:S(2)}) collective-permute-start(f32[256,128]{1,0:T(8,128)S(1)} %get-tuple-element.163), channel_id=1, source_target_pairs={{0,8},{8,0},{16,24},{24,16},{1,9},{9,1},{17,25},{25,17},{2,10},{10... | collective-permute-start | bytes 393224 | tf_op jit(solution)/shard_map/ppermute | solution.py:83
  63.4 2.0 %collective-permute-start.23 = (f32[256,128]{1,0:T(8,128)S(1)}, f32[256,128]{1,0:T(8,128)S(1)}, u32[]{:S(2)}, u32[]{:S(2)}) collective-permute-start(f32[256,128]{1,0:T(8,128)S(1)} %get-tuple-element.168), channel_id=1, source_target_pairs={{0,16},{8,24},{16,0},{24,8},{1,17},{9,25},{17,1},{25,9},{2,18},{10... | collective-permute-start | bytes 393224 | tf_op jit(solution)/shard_map/ppermute | solution.py:83
  65.6 6.0 %collective-permute-done.19.refs_3_ = f32[256,128]{1,0:T(8,128)S(1)} collective-permute-done((f32[256,128]{1,0:T(8,128)S(1)}, f32[256,128]{1,0:T(8,128)S(1)}, u32[]{:S(2)}, u32[]{:S(2)}) %collective-permute-start.19) | collective-permute-done | bytes 131104 | tf_op jit(solution)/shard_map/ppermute | solution.py:83
  71.7 1.6 %collective-permute-start.22 = (f32[256,128]{1,0:T(8,128)S(1)}, f32[256,128]{1,0:T(8,128)S(1)}, u32[]{:S(2)}, u32[]{:S(2)}) collective-permute-start(f32[256,128]{1,0:T(8,128)S(1)} %get-tuple-element.198), channel_id=1, source_target_pairs={{0,2},{1,3},{2,0},{3,1},{4,6},{5,7},{6,4},{7,5},{8,10},{9,11},{10,... | collective-permute-start | bytes 393224 | tf_op jit(solution)/shard_map/ppermute | solution.py:83
  73.3 1.8 %collective-permute-start.20 = (f32[256,128]{1,0:T(8,128)S(1)}, f32[256,128]{1,0:T(8,128)S(1)}, u32[]{:S(2)}, u32[]{:S(2)}) collective-permute-start(f32[256,128]{1,0:T(8,128)S(1)} %get-tuple-element.161.refs_0_), channel_id=1, source_target_pairs={{0,16},{8,24},{16,0},{24,8},{1,17},{9,25},{17,1},{25,9},{2,18},{10... | collective-permute-start | bytes 393224 | tf_op jit(solution)/shard_map/ppermute | solution.py:83
  76.8 1.8 %collective-permute-start.27 = (f32[256,128]{1,0:T(8,128)S(1)}, f32[256,128]{1,0:T(8,128)S(1)}, u32[]{:S(2)}, u32[]{:S(2)}) collective-permute-start(f32[256,128]{1,0:T(8,128)S(1)} %get-tuple-element.170.refs_0_), channel_id=1, source_target_pairs={{0,16},{8,24},{16,0},{24,8},{1,17},{9,25},{17,1},{25,9},{2,18},{10... | collective-permute-start | bytes 393224 | tf_op jit(solution)/shard_map/ppermute | solution.py:83
  79.0 2.5 %collective-permute-done.24.refs_3_ = f32[256,128]{1,0:T(8,128)S(1)} collective-permute-done((f32[256,128]{1,0:T(8,128)S(1)}, f32[256,128]{1,0:T(8,128)S(1)}, u32[]{:S(2)}, u32[]{:S(2)}) %collective-permute-start.24) | collective-permute-done | bytes 131104 | tf_op jit(solution)/shard_map/ppermute | solution.py:83
  85.7 2.8 %collective-permute-start.32 = (f32[256,128]{1,0:T(8,128)S(1)}, f32[256,128]{1,0:T(8,128)S(1)}, u32[]{:S(2)}, u32[]{:S(2)}) collective-permute-start(f32[256,128]{1,0:T(8,128)S(1)} %sums.27), channel_id=1, source_target_pairs={{0,2},{1,3},{2,0},{3,1},{4,6},{5,7},{6,4},{7,5},{8,10},{9,11},{10,... | collective-permute-start | bytes 393224 | tf_op jit(solution)/shard_map/ppermute | solution.py:83
  89.8 1.6 %collective-permute-done.32 = f32[256,128]{1,0:T(8,128)S(1)} collective-permute-done((f32[256,128]{1,0:T(8,128)S(1)}, f32[256,128]{1,0:T(8,128)S(1)}, u32[]{:S(2)}, u32[]{:S(2)}) %collective-permute-start.32) | collective-permute-done | bytes 131104 | tf_op jit(solution)/shard_map/ppermute | solution.py:83
  (85 shorter events, 20.7 us)
Async XLA Ops:
  19.7 5.8 %collective-permute-start = (f32[512,128]{1,0:T(8,128)S(1)}, f32[512,128]{1,0:T(8,128)S(1)}, u32[]{:S(2)}, u32[]{:S(2)}) collective-permute-start(f32[512,128]{1,0:T(8,128)S(1)} %get-tuple-element.108), channel_id=1, source_target_pairs={{0,1},{1,0},{2,3},{3,2},{4,5},{5,4},{6,7},{7,6},{8,9},{9,8},{10,11... | collective-permute-start | bytes 786440 | tf_op jit(solution)/shard_map/ppermute | solution.py:83
  21.4 6.7 %collective-permute-start.3 = (f32[256,128]{1,0:T(8,128)S(1)}, f32[256,128]{1,0:T(8,128)S(1)}, u32[]{:S(2)}, u32[]{:S(2)}) collective-permute-start(f32[256,128]{1,0:T(8,128)S(1)} %get-tuple-element.116), channel_id=1, source_target_pairs={{0,8},{8,0},{16,24},{24,16},{1,9},{9,1},{17,25},{25,17},{2,10},{10... | collective-permute-start | bytes 393224 | tf_op jit(solution)/shard_map/ppermute | solution.py:83
  26.6 10.5 %collective-permute-start.1 = (f32[256,128]{1,0:T(8,128)S(1)}, f32[256,128]{1,0:T(8,128)S(1)}, u32[]{:S(2)}, u32[]{:S(2)}) collective-permute-start(f32[256,128]{1,0:T(8,128)S(1)} %get-tuple-element.114), channel_id=1, source_target_pairs={{0,8},{8,0},{16,24},{24,16},{1,9},{9,1},{17,25},{25,17},{2,10},{10... | collective-permute-start | bytes 393224 | tf_op jit(solution)/shard_map/ppermute | solution.py:83
  27.2 9.9 %collective-permute-start.5 = (f32[256,128]{1,0:T(8,128)S(1)}, f32[256,128]{1,0:T(8,128)S(1)}, u32[]{:S(2)}, u32[]{:S(2)}) collective-permute-start(f32[256,128]{1,0:T(8,128)S(1)} %get-tuple-element.127), channel_id=1, source_target_pairs={{0,16},{8,24},{16,0},{24,8},{1,17},{9,25},{17,1},{25,9},{2,18},{10... | collective-permute-start | bytes 393224 | tf_op jit(solution)/shard_map/ppermute | solution.py:83
  31.1 8.4 %collective-permute-start.7 = (f32[256,128]{1,0:T(8,128)S(1)}, f32[256,128]{1,0:T(8,128)S(1)}, u32[]{:S(2)}, u32[]{:S(2)}) collective-permute-start(f32[256,128]{1,0:T(8,128)S(1)} %get-tuple-element.122.refs_0_), channel_id=1, source_target_pairs={{0,16},{8,24},{16,0},{24,8},{1,17},{9,25},{17,1},{25,9},{2,18},{10... | collective-permute-start | bytes 393224 | tf_op jit(solution)/shard_map/ppermute | solution.py:83
  33.5 6.1 %collective-permute-start.8 = (f32[256,128]{1,0:T(8,128)S(1)}, f32[256,128]{1,0:T(8,128)S(1)}, u32[]{:S(2)}, u32[]{:S(2)}) collective-permute-start(f32[256,128]{1,0:T(8,128)S(1)} %get-tuple-element.123.refs_2_), channel_id=1, source_target_pairs={{0,8},{8,0},{16,24},{24,16},{1,9},{9,1},{17,25},{25,17},{2,10},{10... | collective-permute-start | bytes 393224 | tf_op jit(solution)/shard_map/ppermute | solution.py:83
  34.5 11.4 %collective-permute-start.14 = (f32[256,128]{1,0:T(8,128)S(1)}, f32[256,128]{1,0:T(8,128)S(1)}, u32[]{:S(2)}, u32[]{:S(2)}) collective-permute-start(f32[256,128]{1,0:T(8,128)S(1)} %sums.16.refs_0_), channel_id=1, source_target_pairs={{0,4},{1,5},{2,6},{3,7},{4,0},{5,1},{6,2},{7,3},{8,12},{9,13},{10,... | collective-permute-start | bytes 393224 | tf_op jit(solution)/shard_map/ppermute | solution.py:83
  37.2 6.2 %collective-permute-start.6 = (f32[256,128]{1,0:T(8,128)S(1)}, f32[256,128]{1,0:T(8,128)S(1)}, u32[]{:S(2)}, u32[]{:S(2)}) collective-permute-start(f32[256,128]{1,0:T(8,128)S(1)} %get-tuple-element.129.refs_0_), channel_id=1, source_target_pairs={{0,16},{8,24},{16,0},{24,8},{1,17},{9,25},{17,1},{25,9},{2,18},{10... | collective-permute-start | bytes 393224 | tf_op jit(solution)/shard_map/ppermute | solution.py:83
  39.5 6.2 %collective-permute-start.9 = (f32[256,128]{1,0:T(8,128)S(1)}, f32[256,128]{1,0:T(8,128)S(1)}, u32[]{:S(2)}, u32[]{:S(2)}) collective-permute-start(f32[256,128]{1,0:T(8,128)S(1)} %get-tuple-element.130.refs_2_), channel_id=1, source_target_pairs={{0,8},{8,0},{16,24},{24,16},{1,9},{9,1},{17,25},{25,17},{2,10},{10... | collective-permute-start | bytes 393224 | tf_op jit(solution)/shard_map/ppermute | solution.py:83
  39.6 8.0 %collective-permute-start.12 = (f32[256,128]{1,0:T(8,128)S(1)}, f32[256,128]{1,0:T(8,128)S(1)}, u32[]{:S(2)}, u32[]{:S(2)}) collective-permute-start(f32[256,128]{1,0:T(8,128)S(1)} %get-tuple-element.133.refs_2_), channel_id=1, source_target_pairs={{0,8},{8,0},{16,24},{24,16},{1,9},{9,1},{17,25},{25,17},{2,10},{10... | collective-permute-start | bytes 393224 | tf_op jit(solution)/shard_map/ppermute | solution.py:83
  41.7 5.9 %collective-permute-start.13 = (f32[256,128]{1,0:T(8,128)S(1)}, f32[256,128]{1,0:T(8,128)S(1)}, u32[]{:S(2)}, u32[]{:S(2)}) collective-permute-start(f32[256,128]{1,0:T(8,128)S(1)} %get-tuple-element.134.refs_4_), channel_id=1, source_target_pairs={{0,16},{8,24},{16,0},{24,8},{1,17},{9,25},{17,1},{25,9},{2,18},{10... | collective-permute-start | bytes 393224 | tf_op jit(solution)/shard_map/ppermute | solution.py:83
  58.5 7.0 %collective-permute-start.18 = (f32[512,128]{1,0:T(8,128)S(1)}, f32[512,128]{1,0:T(8,128)S(1)}, u32[]{:S(2)}, u32[]{:S(2)}) collective-permute-start(f32[512,128]{1,0:T(8,128)S(1)} %get-tuple-element.150), channel_id=1, source_target_pairs={{0,1},{1,0},{2,3},{3,2},{4,5},{5,4},{6,7},{7,6},{8,9},{9,8},{10,11... | collective-permute-start | bytes 786440 | tf_op jit(solution)/shard_map/ppermute | solution.py:83
  61.4 15.4 %collective-permute-start.21 = (f32[256,128]{1,0:T(8,128)S(1)}, f32[256,128]{1,0:T(8,128)S(1)}, u32[]{:S(2)}, u32[]{:S(2)}) collective-permute-start(f32[256,128]{1,0:T(8,128)S(1)} %get-tuple-element.163), channel_id=1, source_target_pairs={{0,8},{8,0},{16,24},{24,16},{1,9},{9,1},{17,25},{25,17},{2,10},{10... | collective-permute-start | bytes 393224 | tf_op jit(solution)/shard_map/ppermute | solution.py:83
  63.4 13.4 %collective-permute-start.23 = (f32[256,128]{1,0:T(8,128)S(1)}, f32[256,128]{1,0:T(8,128)S(1)}, u32[]{:S(2)}, u32[]{:S(2)}) collective-permute-start(f32[256,128]{1,0:T(8,128)S(1)} %get-tuple-element.168), channel_id=1, source_target_pairs={{0,16},{8,24},{16,0},{24,8},{1,17},{9,25},{17,1},{25,9},{2,18},{10... | collective-permute-start | bytes 393224 | tf_op jit(solution)/shard_map/ppermute | solution.py:83
  65.4 6.2 %collective-permute-start.17 = (f32[256,128]{1,0:T(8,128)S(1)}, f32[256,128]{1,0:T(8,128)S(1)}, u32[]{:S(2)}, u32[]{:S(2)}) collective-permute-start(f32[256,128]{1,0:T(8,128)S(1)} %get-tuple-element.148), channel_id=1, source_target_pairs={{0,8},{8,0},{16,24},{24,16},{1,9},{9,1},{17,25},{25,17},{2,10},{10... | collective-permute-start | bytes 393224 | tf_op jit(solution)/shard_map/ppermute | solution.py:83
  65.5 6.1 %collective-permute-start.19 = (f32[256,128]{1,0:T(8,128)S(1)}, f32[256,128]{1,0:T(8,128)S(1)}, u32[]{:S(2)}, u32[]{:S(2)}) collective-permute-start(f32[256,128]{1,0:T(8,128)S(1)} %get-tuple-element.159), channel_id=1, source_target_pairs={{0,16},{8,24},{16,0},{24,8},{1,17},{9,25},{17,1},{25,9},{2,18},{10... | collective-permute-start | bytes 393224 | tf_op jit(solution)/shard_map/ppermute | solution.py:83
  73.3 8.2 %collective-permute-start.20 = (f32[256,128]{1,0:T(8,128)S(1)}, f32[256,128]{1,0:T(8,128)S(1)}, u32[]{:S(2)}, u32[]{:S(2)}) collective-permute-start(f32[256,128]{1,0:T(8,128)S(1)} %get-tuple-element.161.refs_0_), channel_id=1, source_target_pairs={{0,16},{8,24},{16,0},{24,8},{1,17},{9,25},{17,1},{25,9},{2,18},{10... | collective-permute-start | bytes 393224 | tf_op jit(solution)/shard_map/ppermute | solution.py:83
  75.1 6.4 %collective-permute-start.24 = (f32[256,128]{1,0:T(8,128)S(1)}, f32[256,128]{1,0:T(8,128)S(1)}, u32[]{:S(2)}, u32[]{:S(2)}) collective-permute-start(f32[256,128]{1,0:T(8,128)S(1)} %get-tuple-element.164.refs_2_), channel_id=1, source_target_pairs={{0,8},{8,0},{16,24},{24,16},{1,9},{9,1},{17,25},{25,17},{2,10},{10... | collective-permute-start | bytes 393224 | tf_op jit(solution)/shard_map/ppermute | solution.py:83
  76.7 9.0 %collective-permute-start.31 = (f32[256,128]{1,0:T(8,128)S(1)}, f32[256,128]{1,0:T(8,128)S(1)}, u32[]{:S(2)}, u32[]{:S(2)}) collective-permute-start(f32[256,128]{1,0:T(8,128)S(1)} %sums.23.refs_0_), channel_id=1, source_target_pairs={{0,4},{1,5},{2,6},{3,7},{4,0},{5,1},{6,2},{7,3},{8,12},{9,13},{10,... | collective-permute-start | bytes 393224 | tf_op jit(solution)/shard_map/ppermute | solution.py:83
  76.8 6.3 %collective-permute-start.27 = (f32[256,128]{1,0:T(8,128)S(1)}, f32[256,128]{1,0:T(8,128)S(1)}, u32[]{:S(2)}, u32[]{:S(2)}) collective-permute-start(f32[256,128]{1,0:T(8,128)S(1)} %get-tuple-element.170.refs_0_), channel_id=1, source_target_pairs={{0,16},{8,24},{16,0},{24,8},{1,17},{9,25},{17,1},{25,9},{2,18},{10... | collective-permute-start | bytes 393224 | tf_op jit(solution)/shard_map/ppermute | solution.py:83
  81.5 7.0 %collective-permute-start.25 = (f32[256,128]{1,0:T(8,128)S(1)}, f32[256,128]{1,0:T(8,128)S(1)}, u32[]{:S(2)}, u32[]{:S(2)}) collective-permute-start(f32[256,128]{1,0:T(8,128)S(1)} %get-tuple-element.174.refs_0_), channel_id=1, source_target_pairs={{0,8},{8,0},{16,24},{24,16},{1,9},{9,1},{17,25},{25,17},{2,10},{10... | collective-permute-start | bytes 393224 | tf_op jit(solution)/shard_map/ppermute | solution.py:83
  81.6 6.9 %collective-permute-start.26 = (f32[256,128]{1,0:T(8,128)S(1)}, f32[256,128]{1,0:T(8,128)S(1)}, u32[]{:S(2)}, u32[]{:S(2)}) collective-permute-start(f32[256,128]{1,0:T(8,128)S(1)} %get-tuple-element.175.refs_2_), channel_id=1, source_target_pairs={{0,16},{8,24},{16,0},{24,8},{1,17},{9,25},{17,1},{25,9},{2,18},{10... | collective-permute-start | bytes 393224 | tf_op jit(solution)/shard_map/ppermute | solution.py:83
  84.3 7.2 %collective-permute-start.29 = (f32[256,128]{1,0:T(8,128)S(1)}, f32[256,128]{1,0:T(8,128)S(1)}, u32[]{:S(2)}, u32[]{:S(2)}) collective-permute-start(f32[256,128]{1,0:T(8,128)S(1)} %get-tuple-element.183.refs_3_), channel_id=1, source_target_pairs={{0,8},{8,0},{16,24},{24,16},{1,9},{9,1},{17,25},{25,17},{2,10},{10... | collective-permute-start | bytes 393224 | tf_op jit(solution)/shard_map/ppermute | solution.py:83
  84.7 6.8 %collective-permute-start.30 = (f32[256,128]{1,0:T(8,128)S(1)}, f32[256,128]{1,0:T(8,128)S(1)}, u32[]{:S(2)}, u32[]{:S(2)}) collective-permute-start(f32[256,128]{1,0:T(8,128)S(1)} %get-tuple-element.184.refs_5_), channel_id=1, source_target_pairs={{0,16},{8,24},{16,0},{24,8},{1,17},{9,25},{17,1},{25,9},{2,18},{10... | collective-permute-start | bytes 393224 | tf_op jit(solution)/shard_map/ppermute | solution.py:83
  (16 other events, 73.6 us)

commit v6 on v5

--- a/solution.py
+++ b/solution.py
@@ -149,18 +149,26 @@
     return [one.current for one in group]
 
 
-def run_sums(waves, feat, last):
+def run_sums(waves, feat, last, early):
     rounds = waves[0][0].steps() - 1
-    extra = feat.steps() - 1
-    before, turns = last, rounds * len(waves)
+    levels, turns = feat.plan.levels, rounds * len(waves)
+    before = last
     for turn in range(turns):
         before = step_all(waves[turn % len(waves)], before)
-        levels = feat.plan.levels
-        while feat.step < 1 + min(levels, 1 + (levels - 1) * turn // (turns - 1)):
+        if early:
+            goal = 2 + (levels - 1) * turn // (turns - 2)
+        else:
+            goal = -(-levels * (turn + 1) // (turns - 1))
+        while feat.step < min(goal, levels + 1):
             before = step_all([feat], before)
-    while feat.step < extra:
-        before = step_all([feat], before)
-    return [one.result() for wave in waves for one in wave], feat.result()
+    return [one.result() for wave in waves for one in wave]
+
+
+def finish(feat, after):
+    while feat.step < feat.steps() - 1:
+        feat.wait_for(after)
+        feat.advance()
+    return feat.result()
 
 
 class Sizes:
@@ -481,9 +489,9 @@
             pluses.append(plus)
             waves.append([
                 Sum(sz.colors[2 * half], keep0, send0), Sum(sz.colors[2 * half + 1], keep1, send1)])
-        sums, esums = run_sums(waves, feat, pluses[-1] if early else step_all([feat], pluses[-1]))
+        sums = run_sums(waves, feat, pluses[-1], early)
         groups = [sums[2 * half] + sums[2 * half + 1] for half in range(HALVES)]
-        return groups, esums, pluses
+        return groups, feat, pluses
 
     a_hi, a_lo, g_hi, g_lo, start, wide, keep_s, send_s, out_sum = kernel(
         functools.partial(first_kernel, sz), "first",
@@ -492,7 +500,8 @@
          v32(sz.own, cols), v16(feats, 2 * cols)] + work
         + [pltpu.SemaphoreType.DMA((blocks,)), pltpu.SemaphoreType.DMA((6,))], 30 * flops, 24,
         data, coef, tile_dual, share_dual, tile_share[0], share, targets, streamed=7)
-    groups, esums, pluses = project(wide, keep_s, send_s, [start] * HALVES, [tile_dual] * HALVES, True)
+    groups, feat, pluses = project(wide, keep_s, send_s, [start] * HALVES, [tile_dual] * HALVES, True)
+    esums = finish(feat, groups[0][0])
     starts, duals, saved, prod = [], [], [], []
     for half in range(HALVES):
         start, tile_now, half_coef, coef_plus, total = kernel(
@@ -507,7 +516,7 @@
         functools.partial(second_kernel, sz), "second",
         [wide_t] + share_sends + [v32(sz.own, cols), vector, vector],
         work, 11 * flops, LIMIT, g_hi, g_lo, *prod, *esums, out_sum, targets, share, share_dual)
-    groups, esums, pluses = project(wide, keep_s, send_s, starts, duals, False)
+    groups, feat, pluses = project(wide, keep_s, send_s, starts, duals, False)
     finals = []
     for half in range(HALVES):
         finals = kernel(
@@ -515,6 +524,7 @@
             [half_coefs] * 3 + [pltpu.SemaphoreType.DMA((3,))], 2 * ADD_FLOPS, LIMIT,
             *finals, *groups[half], *saved[half], pluses[half], streamed=len(finals), stored=True)
     coef_out, coef_dual_out, tile_out = finals
+    esums = finish(feat, coef_out)
     share_out, share_dual_out, tile_share_out = kernel(
         functools.partial(last_share_kernel, sz), "last_share",
         [f32(sz.own, cols), f32(rows, cols), f32(rows, cols)],

time: 94.3 us -> 90.3 us (0.958)
  waiting for transfers between devices: 22.3 us -> 15.4 us
  starting transfers between devices: 34.3 us -> 37.3 us
    ppermute x34, waiting for transfers between devices: 22.3 us -> 15.4 us  [permute(): lax.ppermute(value, self.axis, [(i, i ^ 1 << bit) for i in range(self.siz...]
    ppermute x34, starting transfers between devices: 34.3 us -> 37.3 us  [permute(): lax.ppermute(value, self.axis, [(i, i ^ 1 << bit) for i in range(self.siz...]
  transfers between devices with their start and end apart: 34 -> 34, of which waited for: 13 -> 15; matrix products, arithmetic and copies ran while one was open for 0% -> 0% of each run, Pallas kernels for 11% -> 10%
where the time goes in v6:
time: 90.3 us; the launch traced here: 90.2 us
  starting transfers between devices  37.3 us (41%)
  Pallas kernels  36.4 us (40%)
  waiting for transfers between devices  15.4 us (17%)
  between operations  0.92 us (1%)
    ppermute x34, starting transfers between devices, permute(): lax.ppermute(value, self.axis, [(i, i ^ 1 << bit) for i in range(self.siz...  37.3 us
    pallas_call x11, Pallas kernels, kernel(): pl.pallas_call(body, out_shape=outs, in_specs=[hbm] * streamed + [vmem] *...  36.1 us
    ppermute x34, waiting for transfers between devices, permute(): lax.ppermute(value, self.axis, [(i, i ^ 1 << bit) for i in range(self.siz...  15.4 us
  transfers between devices with their start and end apart: 34, of which 15 were waited for; matrix products, arithmetic and copies ran while one was open for 0% of the time, Pallas kernels for 10%

profile of v6, /device:TPU:0, one launch (start us, length us, event | category | flops | bytes accessed | tf_op | source)
XLA Modules:
  0.0 90.2 jit_solution(2145749039339885623)
XLA Ops:
  0.6 19.0 %first.1 = (bf16[1024,2048]{1,0:T(8,128)(2,1)S(1)}, bf16[1024,2048]{1,0:T(8,128)(2,1)S(1)}, bf16[1024,1024]{1,0:T(8,128)(2,1)S(1)}, bf16[1024,1024]{1,0:T(8,128)...) custom-call(f32[1024,2048]{1,0:T(8,128)} %data.1, ...), custom_call_target="tpu_custom_call" | custom-call | flops 16106127360 | bytes 8388608 | tf_op jit(solution)/shard_map/first/pallas_call | solution.py:459
  21.4 2.6 %collective-permute-start.3 = (f32[256,128]{1,0:T(8,128)S(1)}, f32[256,128]{1,0:T(8,128)S(1)}, u32[]{:S(2)}, u32[]{:S(2)}) collective-permute-start(f32[256,128]{1,0:T(8,128)S(1)} %get-tuple-element.116), channel_id=1, source_target_pairs={{0,8},{8,0},{16,24},{24,16},{1,9},{9,1},{17,25},{25,17},{2,10},{10... | collective-permute-start | bytes 393224 | tf_op jit(solution)/shard_map/ppermute | solution.py:83
  23.9 1.5 %collective-permute-start.4 = (f32[256,128]{1,0:T(8,128)S(1)}, f32[256,128]{1,0:T(8,128)S(1)}, u32[]{:S(2)}, u32[]{:S(2)}) collective-permute-start(f32[256,128]{1,0:T(8,128)S(1)} %get-tuple-element.120), channel_id=1, source_target_pairs={{0,16},{8,24},{16,0},{24,8},{1,17},{9,25},{17,1},{25,9},{2,18},{10... | collective-permute-start | bytes 393224 | tf_op jit(solution)/shard_map/ppermute | solution.py:83
  28.1 1.4 %collective-permute-done.4.refs_3_ = f32[256,128]{1,0:T(8,128)S(1)} collective-permute-done((f32[256,128]{1,0:T(8,128)S(1)}, f32[256,128]{1,0:T(8,128)S(1)}, u32[]{:S(2)}, u32[]{:S(2)}) %collective-permute-start.4) | collective-permute-done | bytes 131104 | tf_op jit(solution)/shard_map/ppermute | solution.py:83
  29.5 1.6 %collective-permute-start.2 = (f32[256,128]{1,0:T(8,128)S(1)}, f32[256,128]{1,0:T(8,128)S(1)}, u32[]{:S(2)}, u32[]{:S(2)}) collective-permute-start(f32[256,128]{1,0:T(8,128)S(1)} %get-tuple-element.200), channel_id=1, source_target_pairs={{0,2},{1,3},{2,0},{3,1},{4,6},{5,7},{6,4},{7,5},{8,10},{9,11},{10,... | collective-permute-start | bytes 393224 | tf_op jit(solution)/shard_map/ppermute | solution.py:83
  31.1 2.3 %collective-permute-start.8 = (f32[256,128]{1,0:T(8,128)S(1)}, f32[256,128]{1,0:T(8,128)S(1)}, u32[]{:S(2)}, u32[]{:S(2)}) collective-permute-start(f32[256,128]{1,0:T(8,128)S(1)} %get-tuple-element.122.refs_0_), channel_id=1, source_target_pairs={{0,16},{8,24},{16,0},{24,8},{1,17},{9,25},{17,1},{25,9},{2,18},{10... | collective-permute-start | bytes 393224 | tf_op jit(solution)/shard_map/ppermute | solution.py:83
  34.5 2.7 %collective-permute-start.7 = (f32[256,128]{1,0:T(8,128)S(1)}, f32[256,128]{1,0:T(8,128)S(1)}, u32[]{:S(2)}, u32[]{:S(2)}) collective-permute-start(f32[256,128]{1,0:T(8,128)S(1)} %sums.16.refs_0_), channel_id=1, source_target_pairs={{0,4},{1,5},{2,6},{3,7},{4,0},{5,1},{6,2},{7,3},{8,12},{9,13},{10,... | collective-permute-start | bytes 393224 | tf_op jit(solution)/shard_map/ppermute | solution.py:83
  37.2 2.3 %collective-permute-start.6 = (f32[256,128]{1,0:T(8,128)S(1)}, f32[256,128]{1,0:T(8,128)S(1)}, u32[]{:S(2)}, u32[]{:S(2)}) collective-permute-start(f32[256,128]{1,0:T(8,128)S(1)} %get-tuple-element.129.refs_0_), channel_id=1, source_target_pairs={{0,16},{8,24},{16,0},{24,8},{1,17},{9,25},{17,1},{25,9},{2,18},{10... | collective-permute-start | bytes 393224 | tf_op jit(solution)/shard_map/ppermute | solution.py:83
  42.1 1.3 %collective-permute-start.15 = (f32[256,128]{1,0:T(8,128)S(1)}, f32[256,128]{1,0:T(8,128)S(1)}, u32[]{:S(2)}, u32[]{:S(2)}) collective-permute-start(f32[256,128]{1,0:T(8,128)S(1)} %sums.19), channel_id=1, source_target_pairs={{0,2},{1,3},{2,0},{3,1},{4,6},{5,7},{6,4},{7,5},{8,10},{9,11},{10,... | collective-permute-start | bytes 393224 | tf_op jit(solution)/shard_map/ppermute | solution.py:83
  43.4 2.3 %collective-permute-done.10.refs_3_ = f32[256,128]{1,0:T(8,128)S(1)} collective-permute-done((f32[256,128]{1,0:T(8,128)S(1)}, f32[256,128]{1,0:T(8,128)S(1)}, u32[]{:S(2)}, u32[]{:S(2)}) %collective-permute-start.10) | collective-permute-done | bytes 131104 | tf_op jit(solution)/shard_map/ppermute | solution.py:83
  47.3 1.5 %update0.1 = (f32[1024,128]{1,0:T(8,128)S(1)}, f32[1024,128]{1,0:T(8,128)S(1)}, f32[1024,128]{1,0:T(8,128)S(1)}, f32[1024,128]{1,0:T(8,128)S(1)}, f32[1024,128]{1,0:T(8,128)S(1)}) custom-call(bf16[1024,2048]{1,0:T(8,128)(2,1)S(1)} %get-tuple-element.104.a_hi.refs_0_, bf16[1024,2048]{1,0:T(8,128)(2,1)S(1)} %get-tuple-element.105.a_lo.refs_1_, ...), custom_call_target="tpu_custom_call" | custom-call | flops 8000000000 | bytes 8388608 | tf_op jit(solution)/shard_map/update0/pallas_call | solution.py:459
  48.9 1.9 %collective-permute-done.11.refs_3_ = f32[256,128]{1,0:T(8,128)S(1)} collective-permute-done((f32[256,128]{1,0:T(8,128)S(1)}, f32[256,128]{1,0:T(8,128)S(1)}, u32[]{:S(2)}, u32[]{:S(2)}) %collective-permute-start.11) | collective-permute-done | bytes 131104 | tf_op jit(solution)/shard_map/ppermute | solution.py:83
  50.9 1.5 %update1.1 = (f32[1024,128]{1,0:T(8,128)S(1)}, f32[1024,128]{1,0:T(8,128)S(1)}, f32[1024,128]{1,0:T(8,128)S(1)}, f32[1024,128]{1,0:T(8,128)S(1)}, f32[1024,128]{1,0:T(8,128)S(1)}) custom-call(bf16[1024,2048]{1,0:T(8,128)(2,1)S(1)} %get-tuple-element.104.a_hi.refs_0_, bf16[1024,2048]{1,0:T(8,128)(2,1)S(1)} %get-tuple-element.105.a_lo.refs_1_, ...), custom_call_target="tpu_custom_call" | custom-call | flops 8000000000 | bytes 8388608 | tf_op jit(solution)/shard_map/update1/pallas_call | solution.py:459
  52.4 5.8 %second.1 = (bf16[256,1024]{1,0:T(8,128)(2,1)S(1)}, f32[512,128]{1,0:T(8,128)S(1)}, f32[512,128]{1,0:T(8,128)S(1)}, f32[128,128]{1,0:T(8,128)S(1)}, f32[1024,128]{1,0:T(8,128)S(1)}, /*index=5*/f32[1024,128]{1,0:T(8,128)S(1)}) custom-call(bf16[1024,1024]{1,0:T(8,128)(2,1)S(1)} %get-tuple-element.102.g_hi, bf16[1024,1024]{1,0:T(8,128)(2,1)S(1)} %get-tuple-element.103.g_lo, ...), custom_call_target="tpu_custom_call" | custom-call | flops 5905580032 | bytes 8388608 | tf_op jit(solution)/shard_map/second/pallas_call | solution.py:459
  59.4 2.0 %collective-permute-start.17 = (f32[256,128]{1,0:T(8,128)S(1)}, f32[256,128]{1,0:T(8,128)S(1)}, u32[]{:S(2)}, u32[]{:S(2)}) collective-permute-start(f32[256,128]{1,0:T(8,128)S(1)} %get-tuple-element.148), channel_id=1, source_target_pairs={{0,8},{8,0},{16,24},{24,16},{1,9},{9,1},{17,25},{25,17},{2,10},{10... | collective-permute-start | bytes 393224 | tf_op jit(solution)/shard_map/ppermute | solution.py:83
  63.1 1.7 %collective-permute-start.23 = (f32[256,128]{1,0:T(8,128)S(1)}, f32[256,128]{1,0:T(8,128)S(1)}, u32[]{:S(2)}, u32[]{:S(2)}) collective-permute-start(f32[256,128]{1,0:T(8,128)S(1)} %get-tuple-element.167), channel_id=1, source_target_pairs={{0,16},{8,24},{16,0},{24,8},{1,17},{9,25},{17,1},{25,9},{2,18},{10... | collective-permute-start | bytes 393224 | tf_op jit(solution)/shard_map/ppermute | solution.py:83
  64.9 1.9 %collective-permute-done.18.refs_3_ = f32[256,128]{1,0:T(8,128)S(1)} collective-permute-done((f32[256,128]{1,0:T(8,128)S(1)}, f32[256,128]{1,0:T(8,128)S(1)}, u32[]{:S(2)}, u32[]{:S(2)}) %collective-permute-start.18) | collective-permute-done | bytes 131104 | tf_op jit(solution)/shard_map/ppermute | solution.py:83
  68.6 1.5 %collective-permute-start.21 = (f32[256,128]{1,0:T(8,128)S(1)}, f32[256,128]{1,0:T(8,128)S(1)}, u32[]{:S(2)}, u32[]{:S(2)}) collective-permute-start(f32[256,128]{1,0:T(8,128)S(1)} %get-tuple-element.198), channel_id=1, source_target_pairs={{0,2},{1,3},{2,0},{3,1},{4,6},{5,7},{6,4},{7,5},{8,10},{9,11},{10,... | collective-permute-start | bytes 393224 | tf_op jit(solution)/shard_map/ppermute | solution.py:83
  70.2 2.5 %collective-permute-start.27 = (f32[256,128]{1,0:T(8,128)S(1)}, f32[256,128]{1,0:T(8,128)S(1)}, u32[]{:S(2)}, u32[]{:S(2)}) collective-permute-start(f32[256,128]{1,0:T(8,128)S(1)} %get-tuple-element.169.refs_0_), channel_id=1, source_target_pairs={{0,16},{8,24},{16,0},{24,8},{1,17},{9,25},{17,1},{25,9},{2,18},{10... | collective-permute-start | bytes 393224 | tf_op jit(solution)/shard_map/ppermute | solution.py:83
  72.8 2.0 %collective-permute-start.28 = (f32[256,128]{1,0:T(8,128)S(1)}, f32[256,128]{1,0:T(8,128)S(1)}, u32[]{:S(2)}, u32[]{:S(2)}) collective-permute-start(f32[256,128]{1,0:T(8,128)S(1)} %get-tuple-element.170.refs_2_), channel_id=1, source_target_pairs={{0,8},{8,0},{16,24},{24,16},{1,9},{9,1},{17,25},{25,17},{2,10},{10... | collective-permute-start | bytes 393224 | tf_op jit(solution)/shard_map/ppermute | solution.py:83
  74.7 1.8 %collective-permute-start.31 = (f32[256,128]{1,0:T(8,128)S(1)}, f32[256,128]{1,0:T(8,128)S(1)}, u32[]{:S(2)}, u32[]{:S(2)}) collective-permute-start(f32[256,128]{1,0:T(8,128)S(1)} %sums.24.refs_0_), channel_id=1, source_target_pairs={{0,4},{1,5},{2,6},{3,7},{4,0},{5,1},{6,2},{7,3},{8,12},{9,13},{10,... | collective-permute-start | bytes 393224 | tf_op jit(solution)/shard_map/ppermute | solution.py:83
  76.5 3.3 %collective-permute-start.25 = (f32[256,128]{1,0:T(8,128)S(1)}, f32[256,128]{1,0:T(8,128)S(1)}, u32[]{:S(2)}, u32[]{:S(2)}) collective-permute-start(f32[256,128]{1,0:T(8,128)S(1)} %get-tuple-element.174.refs_0_), channel_id=1, source_target_pairs={{0,8},{8,0},{16,24},{24,16},{1,9},{9,1},{17,25},{25,17},{2,10},{10... | collective-permute-start | bytes 393224 | tf_op jit(solution)/shard_map/ppermute | solution.py:83
  82.8 2.0 %collective-permute-done.26.refs_3_ = f32[256,128]{1,0:T(8,128)S(1)} collective-permute-done((f32[256,128]{1,0:T(8,128)S(1)}, f32[256,128]{1,0:T(8,128)S(1)}, u32[]{:S(2)}, u32[]{:S(2)}) %collective-permute-start.26) | collective-permute-done | bytes 131104 | tf_op jit(solution)/shard_map/ppermute | solution.py:83
  87.6 1.5 %collective-permute-done.33.refs_1_ = f32[512,128]{1,0:T(8,128)S(1)} collective-permute-done((f32[512,128]{1,0:T(8,128)S(1)}, f32[512,128]{1,0:T(8,128)S(1)}, u32[]{:S(2)}, u32[]{:S(2)}) %collective-permute-start.33) | collective-permute-done | bytes 262176 | tf_op jit(solution)/shard_map/ppermute | solution.py:83
  (85 shorter events, 21.4 us)
Async XLA Ops:
  19.7 5.8 %collective-permute-start = (f32[512,128]{1,0:T(8,128)S(1)}, f32[512,128]{1,0:T(8,128)S(1)}, u32[]{:S(2)}, u32[]{:S(2)}) collective-permute-start(f32[512,128]{1,0:T(8,128)S(1)} %get-tuple-element.108), channel_id=1, source_target_pairs={{0,1},{1,0},{2,3},{3,2},{4,5},{5,4},{6,7},{7,6},{8,9},{9,8},{10,11... | collective-permute-start | bytes 786440 | tf_op jit(solution)/shard_map/ppermute | solution.py:83
  21.4 6.7 %collective-permute-start.3 = (f32[256,128]{1,0:T(8,128)S(1)}, f32[256,128]{1,0:T(8,128)S(1)}, u32[]{:S(2)}, u32[]{:S(2)}) collective-permute-start(f32[256,128]{1,0:T(8,128)S(1)} %get-tuple-element.116), channel_id=1, source_target_pairs={{0,8},{8,0},{16,24},{24,16},{1,9},{9,1},{17,25},{25,17},{2,10},{10... | collective-permute-start | bytes 393224 | tf_op jit(solution)/shard_map/ppermute | solution.py:83
  23.9 5.6 %collective-permute-start.4 = (f32[256,128]{1,0:T(8,128)S(1)}, f32[256,128]{1,0:T(8,128)S(1)}, u32[]{:S(2)}, u32[]{:S(2)}) collective-permute-start(f32[256,128]{1,0:T(8,128)S(1)} %get-tuple-element.120), channel_id=1, source_target_pairs={{0,16},{8,24},{16,0},{24,8},{1,17},{9,25},{17,1},{25,9},{2,18},{10... | collective-permute-start | bytes 393224 | tf_op jit(solution)/shard_map/ppermute | solution.py:83
  26.6 10.5 %collective-permute-start.1 = (f32[256,128]{1,0:T(8,128)S(1)}, f32[256,128]{1,0:T(8,128)S(1)}, u32[]{:S(2)}, u32[]{:S(2)}) collective-permute-start(f32[256,128]{1,0:T(8,128)S(1)} %get-tuple-element.114), channel_id=1, source_target_pairs={{0,8},{8,0},{16,24},{24,16},{1,9},{9,1},{17,25},{25,17},{2,10},{10... | collective-permute-start | bytes 393224 | tf_op jit(solution)/shard_map/ppermute | solution.py:83
  27.2 9.9 %collective-permute-start.5 = (f32[256,128]{1,0:T(8,128)S(1)}, f32[256,128]{1,0:T(8,128)S(1)}, u32[]{:S(2)}, u32[]{:S(2)}) collective-permute-start(f32[256,128]{1,0:T(8,128)S(1)} %get-tuple-element.127), channel_id=1, source_target_pairs={{0,16},{8,24},{16,0},{24,8},{1,17},{9,25},{17,1},{25,9},{2,18},{10... | collective-permute-start | bytes 393224 | tf_op jit(solution)/shard_map/ppermute | solution.py:83
  31.1 8.4 %collective-permute-start.8 = (f32[256,128]{1,0:T(8,128)S(1)}, f32[256,128]{1,0:T(8,128)S(1)}, u32[]{:S(2)}, u32[]{:S(2)}) collective-permute-start(f32[256,128]{1,0:T(8,128)S(1)} %get-tuple-element.122.refs_0_), channel_id=1, source_target_pairs={{0,16},{8,24},{16,0},{24,8},{1,17},{9,25},{17,1},{25,9},{2,18},{10... | collective-permute-start | bytes 393224 | tf_op jit(solution)/shard_map/ppermute | solution.py:83
  33.5 6.1 %collective-permute-start.9 = (f32[256,128]{1,0:T(8,128)S(1)}, f32[256,128]{1,0:T(8,128)S(1)}, u32[]{:S(2)}, u32[]{:S(2)}) collective-permute-start(f32[256,128]{1,0:T(8,128)S(1)} %get-tuple-element.123.refs_2_), channel_id=1, source_target_pairs={{0,8},{8,0},{16,24},{24,16},{1,9},{9,1},{17,25},{25,17},{2,10},{10... | collective-permute-start | bytes 393224 | tf_op jit(solution)/shard_map/ppermute | solution.py:83
  34.5 7.5 %collective-permute-start.7 = (f32[256,128]{1,0:T(8,128)S(1)}, f32[256,128]{1,0:T(8,128)S(1)}, u32[]{:S(2)}, u32[]{:S(2)}) collective-permute-start(f32[256,128]{1,0:T(8,128)S(1)} %sums.16.refs_0_), channel_id=1, source_target_pairs={{0,4},{1,5},{2,6},{3,7},{4,0},{5,1},{6,2},{7,3},{8,12},{9,13},{10,... | collective-permute-start | bytes 393224 | tf_op jit(solution)/shard_map/ppermute | solution.py:83
  37.2 8.5 %collective-permute-start.6 = (f32[256,128]{1,0:T(8,128)S(1)}, f32[256,128]{1,0:T(8,128)S(1)}, u32[]{:S(2)}, u32[]{:S(2)}) collective-permute-start(f32[256,128]{1,0:T(8,128)S(1)} %get-tuple-element.129.refs_0_), channel_id=1, source_target_pairs={{0,16},{8,24},{16,0},{24,8},{1,17},{9,25},{17,1},{25,9},{2,18},{10... | collective-permute-start | bytes 393224 | tf_op jit(solution)/shard_map/ppermute | solution.py:83
  39.5 6.2 %collective-permute-start.10 = (f32[256,128]{1,0:T(8,128)S(1)}, f32[256,128]{1,0:T(8,128)S(1)}, u32[]{:S(2)}, u32[]{:S(2)}) collective-permute-start(f32[256,128]{1,0:T(8,128)S(1)} %get-tuple-element.130.refs_2_), channel_id=1, source_target_pairs={{0,8},{8,0},{16,24},{24,16},{1,9},{9,1},{17,25},{25,17},{2,10},{10... | collective-permute-start | bytes 393224 | tf_op jit(solution)/shard_map/ppermute | solution.py:83
  39.6 6.7 %collective-permute-start.14 = (f32[256,128]{1,0:T(8,128)S(1)}, f32[256,128]{1,0:T(8,128)S(1)}, u32[]{:S(2)}, u32[]{:S(2)}) collective-permute-start(f32[256,128]{1,0:T(8,128)S(1)} %get-tuple-element.134.refs_4_), channel_id=1, source_target_pairs={{0,16},{8,24},{16,0},{24,8},{1,17},{9,25},{17,1},{25,9},{2,18},{10... | collective-permute-start | bytes 393224 | tf_op jit(solution)/shard_map/ppermute | solution.py:83
  40.4 6.9 %collective-permute-start.13 = (f32[256,128]{1,0:T(8,128)S(1)}, f32[256,128]{1,0:T(8,128)S(1)}, u32[]{:S(2)}, u32[]{:S(2)}) collective-permute-start(f32[256,128]{1,0:T(8,128)S(1)} %get-tuple-element.133.refs_2_), channel_id=1, source_target_pairs={{0,8},{8,0},{16,24},{24,16},{1,9},{9,1},{17,25},{25,17},{2,10},{10... | collective-permute-start | bytes 393224 | tf_op jit(solution)/shard_map/ppermute | solution.py:83
  42.1 6.7 %collective-permute-start.15 = (f32[256,128]{1,0:T(8,128)S(1)}, f32[256,128]{1,0:T(8,128)S(1)}, u32[]{:S(2)}, u32[]{:S(2)}) collective-permute-start(f32[256,128]{1,0:T(8,128)S(1)} %sums.19), channel_id=1, source_target_pairs={{0,2},{1,3},{2,0},{3,1},{4,6},{5,7},{6,4},{7,5},{8,10},{9,11},{10,... | collective-permute-start | bytes 393224 | tf_op jit(solution)/shard_map/ppermute | solution.py:83
  59.4 5.5 %collective-permute-start.17 = (f32[256,128]{1,0:T(8,128)S(1)}, f32[256,128]{1,0:T(8,128)S(1)}, u32[]{:S(2)}, u32[]{:S(2)}) collective-permute-start(f32[256,128]{1,0:T(8,128)S(1)} %get-tuple-element.148), channel_id=1, source_target_pairs={{0,8},{8,0},{16,24},{24,16},{1,9},{9,1},{17,25},{25,17},{2,10},{10... | collective-permute-start | bytes 393224 | tf_op jit(solution)/shard_map/ppermute | solution.py:83
  63.1 5.5 %collective-permute-start.23 = (f32[256,128]{1,0:T(8,128)S(1)}, f32[256,128]{1,0:T(8,128)S(1)}, u32[]{:S(2)}, u32[]{:S(2)}) collective-permute-start(f32[256,128]{1,0:T(8,128)S(1)} %get-tuple-element.167), channel_id=1, source_target_pairs={{0,16},{8,24},{16,0},{24,8},{1,17},{9,25},{17,1},{25,9},{2,18},{10... | collective-permute-start | bytes 393224 | tf_op jit(solution)/shard_map/ppermute | solution.py:83
  66.8 9.7 %collective-permute-start.19 = (f32[256,128]{1,0:T(8,128)S(1)}, f32[256,128]{1,0:T(8,128)S(1)}, u32[]{:S(2)}, u32[]{:S(2)}) collective-permute-start(f32[256,128]{1,0:T(8,128)S(1)} %get-tuple-element.158.refs_0_), channel_id=1, source_target_pairs={{0,16},{8,24},{16,0},{24,8},{1,17},{9,25},{17,1},{25,9},{2,18},{10... | collective-permute-start | bytes 393224 | tf_op jit(solution)/shard_map/ppermute | solution.py:83
  67.8 8.7 %collective-permute-start.24 = (f32[256,128]{1,0:T(8,128)S(1)}, f32[256,128]{1,0:T(8,128)S(1)}, u32[]{:S(2)}, u32[]{:S(2)}) collective-permute-start(f32[256,128]{1,0:T(8,128)S(1)} %get-tuple-element.161.refs_2_), channel_id=1, source_target_pairs={{0,8},{8,0},{16,24},{24,16},{1,9},{9,1},{17,25},{25,17},{2,10},{10... | collective-permute-start | bytes 393224 | tf_op jit(solution)/shard_map/ppermute | solution.py:83
  68.6 6.1 %collective-permute-start.21 = (f32[256,128]{1,0:T(8,128)S(1)}, f32[256,128]{1,0:T(8,128)S(1)}, u32[]{:S(2)}, u32[]{:S(2)}) collective-permute-start(f32[256,128]{1,0:T(8,128)S(1)} %get-tuple-element.198), channel_id=1, source_target_pairs={{0,2},{1,3},{2,0},{3,1},{4,6},{5,7},{6,4},{7,5},{8,10},{9,11},{10,... | collective-permute-start | bytes 393224 | tf_op jit(solution)/shard_map/ppermute | solution.py:83
  70.2 9.6 %collective-permute-start.27 = (f32[256,128]{1,0:T(8,128)S(1)}, f32[256,128]{1,0:T(8,128)S(1)}, u32[]{:S(2)}, u32[]{:S(2)}) collective-permute-start(f32[256,128]{1,0:T(8,128)S(1)} %get-tuple-element.169.refs_0_), channel_id=1, source_target_pairs={{0,16},{8,24},{16,0},{24,8},{1,17},{9,25},{17,1},{25,9},{2,18},{10... | collective-permute-start | bytes 393224 | tf_op jit(solution)/shard_map/ppermute | solution.py:83
  72.8 7.1 %collective-permute-start.28 = (f32[256,128]{1,0:T(8,128)S(1)}, f32[256,128]{1,0:T(8,128)S(1)}, u32[]{:S(2)}, u32[]{:S(2)}) collective-permute-start(f32[256,128]{1,0:T(8,128)S(1)} %get-tuple-element.170.refs_2_), channel_id=1, source_target_pairs={{0,8},{8,0},{16,24},{24,16},{1,9},{9,1},{17,25},{25,17},{2,10},{10... | collective-permute-start | bytes 393224 | tf_op jit(solution)/shard_map/ppermute | solution.py:83
  74.7 7.3 %collective-permute-start.31 = (f32[256,128]{1,0:T(8,128)S(1)}, f32[256,128]{1,0:T(8,128)S(1)}, u32[]{:S(2)}, u32[]{:S(2)}) collective-permute-start(f32[256,128]{1,0:T(8,128)S(1)} %sums.24.refs_0_), channel_id=1, source_target_pairs={{0,4},{1,5},{2,6},{3,7},{4,0},{5,1},{6,2},{7,3},{8,12},{9,13},{10,... | collective-permute-start | bytes 393224 | tf_op jit(solution)/shard_map/ppermute | solution.py:83
  76.5 6.2 %collective-permute-start.25 = (f32[256,128]{1,0:T(8,128)S(1)}, f32[256,128]{1,0:T(8,128)S(1)}, u32[]{:S(2)}, u32[]{:S(2)}) collective-permute-start(f32[256,128]{1,0:T(8,128)S(1)} %get-tuple-element.174.refs_0_), channel_id=1, source_target_pairs={{0,8},{8,0},{16,24},{24,16},{1,9},{9,1},{17,25},{25,17},{2,10},{10... | collective-permute-start | bytes 393224 | tf_op jit(solution)/shard_map/ppermute | solution.py:83
  79.9 6.2 %collective-permute-start.29 = (f32[256,128]{1,0:T(8,128)S(1)}, f32[256,128]{1,0:T(8,128)S(1)}, u32[]{:S(2)}, u32[]{:S(2)}) collective-permute-start(f32[256,128]{1,0:T(8,128)S(1)} %get-tuple-element.183.refs_3_), channel_id=1, source_target_pairs={{0,8},{8,0},{16,24},{24,16},{1,9},{9,1},{17,25},{25,17},{2,10},{10... | collective-permute-start | bytes 393224 | tf_op jit(solution)/shard_map/ppermute | solution.py:83
  82.1 5.4 %collective-permute-start.32 = (f32[256,128]{1,0:T(8,128)S(1)}, f32[256,128]{1,0:T(8,128)S(1)}, u32[]{:S(2)}, u32[]{:S(2)}) collective-permute-start(f32[256,128]{1,0:T(8,128)S(1)} %sums.27), channel_id=1, source_target_pairs={{0,2},{1,3},{2,0},{3,1},{4,6},{5,7},{6,4},{7,5},{8,10},{9,11},{10,... | collective-permute-start | bytes 393224 | tf_op jit(solution)/shard_map/ppermute | solution.py:83
  (16 other events, 78.8 us)

commit v7 on v6

--- a/solution.py
+++ b/solution.py
@@ -237,6 +237,7 @@
     cols, block = sz.cols, sz.row_block
     blocks = [pl.ds(r * block, block) for r in range(sz.rows // block)]
     for rows in blocks:
+        part[rows, :] = resid[rows, :]
         first = resid[rows, :] * (1.0 / theta)
         search[rows, :] = first
         total[rows, :] = first
@@ -250,11 +251,10 @@
             else:
                 wide = dot_nn(g_hi[rows, :], now[...])
                 prod = wide[:, :cols] + wide[:, cols:]
-            if step == 0:
-                part[rows, :] = prod
+            if last:
+                settled = resid[rows, :] + (total[rows, :] - search[rows, :])
+                part[rows, :] = (part[rows, :] - settled) + prod
             else:
-                part[rows, :] += prod
-            if not last:
                 c_old, c_res = pairs[step]
                 old = search[rows, :]
                 res = resid[rows, :] - old - prod
@@ -523,8 +523,9 @@
             functools.partial(last_kernel, half, sz), f"last{half}", [f32(feats, cols)] * 3,
             [half_coefs] * 3 + [pltpu.SemaphoreType.DMA((3,))], 2 * ADD_FLOPS, LIMIT,
             *finals, *groups[half], *saved[half], pluses[half], streamed=len(finals), stored=True)
+        if half == 0:
+            esums = finish(feat, finals[0])
     coef_out, coef_dual_out, tile_out = finals
-    esums = finish(feat, coef_out)
     share_out, share_dual_out, tile_share_out = kernel(
         functools.partial(last_share_kernel, sz), "last_share",
         [f32(sz.own, cols), f32(rows, cols), f32(rows, cols)],

time: 90.3 us -> 90.3 us (level)
  transfers between devices with their start and end apart: 34 -> 34, of which waited for: 15 -> 15; matrix products, arithmetic and copies ran while one was open for 0% -> 0% of each run, Pallas kernels for 10% -> 11%
where the time goes in v7:
time: 90.3 us; the launch traced here: 89.8 us
  starting transfers between devices  37.3 us (41%)
  Pallas kernels  36.5 us (40%)
  waiting for transfers between devices  15 us (17%)
  between operations  0.92 us (1%)
    ppermute x34, starting transfers between devices, permute(): lax.ppermute(value, self.axis, [(i, i ^ 1 << bit) for i in range(self.siz...  37.3 us
    pallas_call x11, Pallas kernels, kernel(): pl.pallas_call(body, out_shape=outs, in_specs=[hbm] * streamed + [vmem] *...  36.1 us
    ppermute x34, waiting for transfers between devices, permute(): lax.ppermute(value, self.axis, [(i, i ^ 1 << bit) for i in range(self.siz...  15 us
  transfers between devices with their start and end apart: 34, of which 15 were waited for; matrix products, arithmetic and copies ran while one was open for 0% of the time, Pallas kernels for 11%

profile of v7, /device:TPU:0, one launch (start us, length us, event | category | flops | bytes accessed | tf_op | source)
XLA Modules:
  0.0 89.8 jit_solution(2027881326430031081)
XLA Ops:
  0.6 19.0 %first.1 = (bf16[1024,2048]{1,0:T(8,128)(2,1)S(1)}, bf16[1024,2048]{1,0:T(8,128)(2,1)S(1)}, bf16[1024,1024]{1,0:T(8,128)(2,1)S(1)}, bf16[1024,1024]{1,0:T(8,128)...) custom-call(f32[1024,2048]{1,0:T(8,128)} %data.1, ...), custom_call_target="tpu_custom_call" | custom-call | flops 16106127360 | bytes 8388608 | tf_op jit(solution)/shard_map/first/pallas_call | solution.py:459
  21.4 2.6 %collective-permute-start.3 = (f32[256,128]{1,0:T(8,128)S(1)}, f32[256,128]{1,0:T(8,128)S(1)}, u32[]{:S(2)}, u32[]{:S(2)}) collective-permute-start(f32[256,128]{1,0:T(8,128)S(1)} %get-tuple-element.116), channel_id=1, source_target_pairs={{0,8},{8,0},{16,24},{24,16},{1,9},{9,1},{17,25},{25,17},{2,10},{10... | collective-permute-start | bytes 393224 | tf_op jit(solution)/shard_map/ppermute | solution.py:83
  23.9 1.5 %collective-permute-start.4 = (f32[256,128]{1,0:T(8,128)S(1)}, f32[256,128]{1,0:T(8,128)S(1)}, u32[]{:S(2)}, u32[]{:S(2)}) collective-permute-start(f32[256,128]{1,0:T(8,128)S(1)} %get-tuple-element.120), channel_id=1, source_target_pairs={{0,16},{8,24},{16,0},{24,8},{1,17},{9,25},{17,1},{25,9},{2,18},{10... | collective-permute-start | bytes 393224 | tf_op jit(solution)/shard_map/ppermute | solution.py:83
  28.1 1.4 %collective-permute-done.4.refs_3_ = f32[256,128]{1,0:T(8,128)S(1)} collective-permute-done((f32[256,128]{1,0:T(8,128)S(1)}, f32[256,128]{1,0:T(8,128)S(1)}, u32[]{:S(2)}, u32[]{:S(2)}) %collective-permute-start.4) | collective-permute-done | bytes 131104 | tf_op jit(solution)/shard_map/ppermute | solution.py:83
  29.5 1.6 %collective-permute-start.2 = (f32[256,128]{1,0:T(8,128)S(1)}, f32[256,128]{1,0:T(8,128)S(1)}, u32[]{:S(2)}, u32[]{:S(2)}) collective-permute-start(f32[256,128]{1,0:T(8,128)S(1)} %get-tuple-element.200), channel_id=1, source_target_pairs={{0,2},{1,3},{2,0},{3,1},{4,6},{5,7},{6,4},{7,5},{8,10},{9,11},{10,... | collective-permute-start | bytes 393224 | tf_op jit(solution)/shard_map/ppermute | solution.py:83
  31.1 2.3 %collective-permute-start.8 = (f32[256,128]{1,0:T(8,128)S(1)}, f32[256,128]{1,0:T(8,128)S(1)}, u32[]{:S(2)}, u32[]{:S(2)}) collective-permute-start(f32[256,128]{1,0:T(8,128)S(1)} %get-tuple-element.122.refs_0_), channel_id=1, source_target_pairs={{0,16},{8,24},{16,0},{24,8},{1,17},{9,25},{17,1},{25,9},{2,18},{10... | collective-permute-start | bytes 393224 | tf_op jit(solution)/shard_map/ppermute | solution.py:83
  34.5 2.7 %collective-permute-start.7 = (f32[256,128]{1,0:T(8,128)S(1)}, f32[256,128]{1,0:T(8,128)S(1)}, u32[]{:S(2)}, u32[]{:S(2)}) collective-permute-start(f32[256,128]{1,0:T(8,128)S(1)} %sums.16.refs_0_), channel_id=1, source_target_pairs={{0,4},{1,5},{2,6},{3,7},{4,0},{5,1},{6,2},{7,3},{8,12},{9,13},{10,... | collective-permute-start | bytes 393224 | tf_op jit(solution)/shard_map/ppermute | solution.py:83
  37.2 2.3 %collective-permute-start.6 = (f32[256,128]{1,0:T(8,128)S(1)}, f32[256,128]{1,0:T(8,128)S(1)}, u32[]{:S(2)}, u32[]{:S(2)}) collective-permute-start(f32[256,128]{1,0:T(8,128)S(1)} %get-tuple-element.129.refs_0_), channel_id=1, source_target_pairs={{0,16},{8,24},{16,0},{24,8},{1,17},{9,25},{17,1},{25,9},{2,18},{10... | collective-permute-start | bytes 393224 | tf_op jit(solution)/shard_map/ppermute | solution.py:83
  40.4 1.3 %collective-permute-start.13 = (f32[256,128]{1,0:T(8,128)S(1)}, f32[256,128]{1,0:T(8,128)S(1)}, u32[]{:S(2)}, u32[]{:S(2)}) collective-permute-start(f32[256,128]{1,0:T(8,128)S(1)} %get-tuple-element.133.refs_2_), channel_id=1, source_target_pairs={{0,8},{8,0},{16,24},{24,16},{1,9},{9,1},{17,25},{25,17},{2,10},{10... | collective-permute-start | bytes 393224 | tf_op jit(solution)/shard_map/ppermute | solution.py:83
  42.1 1.4 %collective-permute-start.15 = (f32[256,128]{1,0:T(8,128)S(1)}, f32[256,128]{1,0:T(8,128)S(1)}, u32[]{:S(2)}, u32[]{:S(2)}) collective-permute-start(f32[256,128]{1,0:T(8,128)S(1)} %sums.19), channel_id=1, source_target_pairs={{0,2},{1,3},{2,0},{3,1},{4,6},{5,7},{6,4},{7,5},{8,10},{9,11},{10,... | collective-permute-start | bytes 393224 | tf_op jit(solution)/shard_map/ppermute | solution.py:83
  43.4 2.3 %collective-permute-done.10.refs_3_ = f32[256,128]{1,0:T(8,128)S(1)} collective-permute-done((f32[256,128]{1,0:T(8,128)S(1)}, f32[256,128]{1,0:T(8,128)S(1)}, u32[]{:S(2)}, u32[]{:S(2)}) %collective-permute-start.10) | collective-permute-done | bytes 131104 | tf_op jit(solution)/shard_map/ppermute | solution.py:83
  47.3 1.5 %update0.1 = (f32[1024,128]{1,0:T(8,128)S(1)}, f32[1024,128]{1,0:T(8,128)S(1)}, f32[1024,128]{1,0:T(8,128)S(1)}, f32[1024,128]{1,0:T(8,128)S(1)}, f32[1024,128]{1,0:T(8,128)S(1)}) custom-call(bf16[1024,2048]{1,0:T(8,128)(2,1)S(1)} %get-tuple-element.104.a_hi.refs_0_, bf16[1024,2048]{1,0:T(8,128)(2,1)S(1)} %get-tuple-element.105.a_lo.refs_1_, ...), custom_call_target="tpu_custom_call" | custom-call | flops 8000000000 | bytes 8388608 | tf_op jit(solution)/shard_map/update0/pallas_call | solution.py:459
  48.9 1.9 %collective-permute-done.11.refs_3_ = f32[256,128]{1,0:T(8,128)S(1)} collective-permute-done((f32[256,128]{1,0:T(8,128)S(1)}, f32[256,128]{1,0:T(8,128)S(1)}, u32[]{:S(2)}, u32[]{:S(2)}) %collective-permute-start.11) | collective-permute-done | bytes 131104 | tf_op jit(solution)/shard_map/ppermute | solution.py:83
  50.9 1.5 %update1.1 = (f32[1024,128]{1,0:T(8,128)S(1)}, f32[1024,128]{1,0:T(8,128)S(1)}, f32[1024,128]{1,0:T(8,128)S(1)}, f32[1024,128]{1,0:T(8,128)S(1)}, f32[1024,128]{1,0:T(8,128)S(1)}) custom-call(bf16[1024,2048]{1,0:T(8,128)(2,1)S(1)} %get-tuple-element.104.a_hi.refs_0_, bf16[1024,2048]{1,0:T(8,128)(2,1)S(1)} %get-tuple-element.105.a_lo.refs_1_, ...), custom_call_target="tpu_custom_call" | custom-call | flops 8000000000 | bytes 8388608 | tf_op jit(solution)/shard_map/update1/pallas_call | solution.py:459
  52.4 5.8 %second.1 = (bf16[256,1024]{1,0:T(8,128)(2,1)S(1)}, f32[512,128]{1,0:T(8,128)S(1)}, f32[512,128]{1,0:T(8,128)S(1)}, f32[128,128]{1,0:T(8,128)S(1)}, f32[1024,128]{1,0:T(8,128)S(1)}, /*index=5*/f32[1024,128]{1,0:T(8,128)S(1)}) custom-call(bf16[1024,1024]{1,0:T(8,128)(2,1)S(1)} %get-tuple-element.102.g_hi, bf16[1024,1024]{1,0:T(8,128)(2,1)S(1)} %get-tuple-element.103.g_lo, ...), custom_call_target="tpu_custom_call" | custom-call | flops 5905580032 | bytes 8388608 | tf_op jit(solution)/shard_map/second/pallas_call | solution.py:459
  59.4 2.0 %collective-permute-start.17 = (f32[256,128]{1,0:T(8,128)S(1)}, f32[256,128]{1,0:T(8,128)S(1)}, u32[]{:S(2)}, u32[]{:S(2)}) collective-permute-start(f32[256,128]{1,0:T(8,128)S(1)} %get-tuple-element.148), channel_id=1, source_target_pairs={{0,8},{8,0},{16,24},{24,16},{1,9},{9,1},{17,25},{25,17},{2,10},{10... | collective-permute-start | bytes 393224 | tf_op jit(solution)/shard_map/ppermute | solution.py:83
  63.1 1.7 %collective-permute-start.23 = (f32[256,128]{1,0:T(8,128)S(1)}, f32[256,128]{1,0:T(8,128)S(1)}, u32[]{:S(2)}, u32[]{:S(2)}) collective-permute-start(f32[256,128]{1,0:T(8,128)S(1)} %get-tuple-element.167), channel_id=1, source_target_pairs={{0,16},{8,24},{16,0},{24,8},{1,17},{9,25},{17,1},{25,9},{2,18},{10... | collective-permute-start | bytes 393224 | tf_op jit(solution)/shard_map/ppermute | solution.py:83
  65.0 1.9 %collective-permute-done.18.refs_3_ = f32[256,128]{1,0:T(8,128)S(1)} collective-permute-done((f32[256,128]{1,0:T(8,128)S(1)}, f32[256,128]{1,0:T(8,128)S(1)}, u32[]{:S(2)}, u32[]{:S(2)}) %collective-permute-start.18) | collective-permute-done | bytes 131104 | tf_op jit(solution)/shard_map/ppermute | solution.py:83
  68.7 1.6 %collective-permute-start.21 = (f32[256,128]{1,0:T(8,128)S(1)}, f32[256,128]{1,0:T(8,128)S(1)}, u32[]{:S(2)}, u32[]{:S(2)}) collective-permute-start(f32[256,128]{1,0:T(8,128)S(1)} %get-tuple-element.198), channel_id=1, source_target_pairs={{0,2},{1,3},{2,0},{3,1},{4,6},{5,7},{6,4},{7,5},{8,10},{9,11},{10,... | collective-permute-start | bytes 393224 | tf_op jit(solution)/shard_map/ppermute | solution.py:83
  70.2 2.5 %collective-permute-start.27 = (f32[256,128]{1,0:T(8,128)S(1)}, f32[256,128]{1,0:T(8,128)S(1)}, u32[]{:S(2)}, u32[]{:S(2)}) collective-permute-start(f32[256,128]{1,0:T(8,128)S(1)} %get-tuple-element.169.refs_0_), channel_id=1, source_target_pairs={{0,16},{8,24},{16,0},{24,8},{1,17},{9,25},{17,1},{25,9},{2,18},{10... | collective-permute-start | bytes 393224 | tf_op jit(solution)/shard_map/ppermute | solution.py:83
  72.8 2.0 %collective-permute-start.28 = (f32[256,128]{1,0:T(8,128)S(1)}, f32[256,128]{1,0:T(8,128)S(1)}, u32[]{:S(2)}, u32[]{:S(2)}) collective-permute-start(f32[256,128]{1,0:T(8,128)S(1)} %get-tuple-element.170.refs_2_), channel_id=1, source_target_pairs={{0,8},{8,0},{16,24},{24,16},{1,9},{9,1},{17,25},{25,17},{2,10},{10... | collective-permute-start | bytes 393224 | tf_op jit(solution)/shard_map/ppermute | solution.py:83
  74.8 1.7 %collective-permute-start.31 = (f32[256,128]{1,0:T(8,128)S(1)}, f32[256,128]{1,0:T(8,128)S(1)}, u32[]{:S(2)}, u32[]{:S(2)}) collective-permute-start(f32[256,128]{1,0:T(8,128)S(1)} %sums.24.refs_0_), channel_id=1, source_target_pairs={{0,4},{1,5},{2,6},{3,7},{4,0},{5,1},{6,2},{7,3},{8,12},{9,13},{10,... | collective-permute-start | bytes 393224 | tf_op jit(solution)/shard_map/ppermute | solution.py:83
  76.5 3.3 %collective-permute-start.25 = (f32[256,128]{1,0:T(8,128)S(1)}, f32[256,128]{1,0:T(8,128)S(1)}, u32[]{:S(2)}, u32[]{:S(2)}) collective-permute-start(f32[256,128]{1,0:T(8,128)S(1)} %get-tuple-element.174.refs_0_), channel_id=1, source_target_pairs={{0,8},{8,0},{16,24},{24,16},{1,9},{9,1},{17,25},{25,17},{2,10},{10... | collective-permute-start | bytes 393224 | tf_op jit(solution)/shard_map/ppermute | solution.py:83
  82.8 2.0 %collective-permute-done.26.refs_3_ = f32[256,128]{1,0:T(8,128)S(1)} collective-permute-done((f32[256,128]{1,0:T(8,128)S(1)}, f32[256,128]{1,0:T(8,128)S(1)}, u32[]{:S(2)}, u32[]{:S(2)}) %collective-permute-start.26) | collective-permute-done | bytes 131104 | tf_op jit(solution)/shard_map/ppermute | solution.py:83
  (85 shorter events, 21.2 us)
Async XLA Ops:
  19.7 5.8 %collective-permute-start = (f32[512,128]{1,0:T(8,128)S(1)}, f32[512,128]{1,0:T(8,128)S(1)}, u32[]{:S(2)}, u32[]{:S(2)}) collective-permute-start(f32[512,128]{1,0:T(8,128)S(1)} %get-tuple-element.108), channel_id=1, source_target_pairs={{0,1},{1,0},{2,3},{3,2},{4,5},{5,4},{6,7},{7,6},{8,9},{9,8},{10,11... | collective-permute-start | bytes 786440 | tf_op jit(solution)/shard_map/ppermute | solution.py:83
  21.4 6.7 %collective-permute-start.3 = (f32[256,128]{1,0:T(8,128)S(1)}, f32[256,128]{1,0:T(8,128)S(1)}, u32[]{:S(2)}, u32[]{:S(2)}) collective-permute-start(f32[256,128]{1,0:T(8,128)S(1)} %get-tuple-element.116), channel_id=1, source_target_pairs={{0,8},{8,0},{16,24},{24,16},{1,9},{9,1},{17,25},{25,17},{2,10},{10... | collective-permute-start | bytes 393224 | tf_op jit(solution)/shard_map/ppermute | solution.py:83
  23.9 5.6 %collective-permute-start.4 = (f32[256,128]{1,0:T(8,128)S(1)}, f32[256,128]{1,0:T(8,128)S(1)}, u32[]{:S(2)}, u32[]{:S(2)}) collective-permute-start(f32[256,128]{1,0:T(8,128)S(1)} %get-tuple-element.120), channel_id=1, source_target_pairs={{0,16},{8,24},{16,0},{24,8},{1,17},{9,25},{17,1},{25,9},{2,18},{10... | collective-permute-start | bytes 393224 | tf_op jit(solution)/shard_map/ppermute | solution.py:83
  26.7 10.5 %collective-permute-start.1 = (f32[256,128]{1,0:T(8,128)S(1)}, f32[256,128]{1,0:T(8,128)S(1)}, u32[]{:S(2)}, u32[]{:S(2)}) collective-permute-start(f32[256,128]{1,0:T(8,128)S(1)} %get-tuple-element.114), channel_id=1, source_target_pairs={{0,8},{8,0},{16,24},{24,16},{1,9},{9,1},{17,25},{25,17},{2,10},{10... | collective-permute-start | bytes 393224 | tf_op jit(solution)/shard_map/ppermute | solution.py:83
  27.3 9.9 %collective-permute-start.5 = (f32[256,128]{1,0:T(8,128)S(1)}, f32[256,128]{1,0:T(8,128)S(1)}, u32[]{:S(2)}, u32[]{:S(2)}) collective-permute-start(f32[256,128]{1,0:T(8,128)S(1)} %get-tuple-element.127), channel_id=1, source_target_pairs={{0,16},{8,24},{16,0},{24,8},{1,17},{9,25},{17,1},{25,9},{2,18},{10... | collective-permute-start | bytes 393224 | tf_op jit(solution)/shard_map/ppermute | solution.py:83
  31.1 8.4 %collective-permute-start.8 = (f32[256,128]{1,0:T(8,128)S(1)}, f32[256,128]{1,0:T(8,128)S(1)}, u32[]{:S(2)}, u32[]{:S(2)}) collective-permute-start(f32[256,128]{1,0:T(8,128)S(1)} %get-tuple-element.122.refs_0_), channel_id=1, source_target_pairs={{0,16},{8,24},{16,0},{24,8},{1,17},{9,25},{17,1},{25,9},{2,18},{10... | collective-permute-start | bytes 393224 | tf_op jit(solution)/shard_map/ppermute | solution.py:83
  33.5 6.1 %collective-permute-start.9 = (f32[256,128]{1,0:T(8,128)S(1)}, f32[256,128]{1,0:T(8,128)S(1)}, u32[]{:S(2)}, u32[]{:S(2)}) collective-permute-start(f32[256,128]{1,0:T(8,128)S(1)} %get-tuple-element.123.refs_2_), channel_id=1, source_target_pairs={{0,8},{8,0},{16,24},{24,16},{1,9},{9,1},{17,25},{25,17},{2,10},{10... | collective-permute-start | bytes 393224 | tf_op jit(solution)/shard_map/ppermute | solution.py:83
  34.5 7.5 %collective-permute-start.7 = (f32[256,128]{1,0:T(8,128)S(1)}, f32[256,128]{1,0:T(8,128)S(1)}, u32[]{:S(2)}, u32[]{:S(2)}) collective-permute-start(f32[256,128]{1,0:T(8,128)S(1)} %sums.16.refs_0_), channel_id=1, source_target_pairs={{0,4},{1,5},{2,6},{3,7},{4,0},{5,1},{6,2},{7,3},{8,12},{9,13},{10,... | collective-permute-start | bytes 393224 | tf_op jit(solution)/shard_map/ppermute | solution.py:83
  37.2 8.5 %collective-permute-start.6 = (f32[256,128]{1,0:T(8,128)S(1)}, f32[256,128]{1,0:T(8,128)S(1)}, u32[]{:S(2)}, u32[]{:S(2)}) collective-permute-start(f32[256,128]{1,0:T(8,128)S(1)} %get-tuple-element.129.refs_0_), channel_id=1, source_target_pairs={{0,16},{8,24},{16,0},{24,8},{1,17},{9,25},{17,1},{25,9},{2,18},{10... | collective-permute-start | bytes 393224 | tf_op jit(solution)/shard_map/ppermute | solution.py:83
  39.5 6.2 %collective-permute-start.10 = (f32[256,128]{1,0:T(8,128)S(1)}, f32[256,128]{1,0:T(8,128)S(1)}, u32[]{:S(2)}, u32[]{:S(2)}) collective-permute-start(f32[256,128]{1,0:T(8,128)S(1)} %get-tuple-element.130.refs_2_), channel_id=1, source_target_pairs={{0,8},{8,0},{16,24},{24,16},{1,9},{9,1},{17,25},{25,17},{2,10},{10... | collective-permute-start | bytes 393224 | tf_op jit(solution)/shard_map/ppermute | solution.py:83
  39.6 6.7 %collective-permute-start.14 = (f32[256,128]{1,0:T(8,128)S(1)}, f32[256,128]{1,0:T(8,128)S(1)}, u32[]{:S(2)}, u32[]{:S(2)}) collective-permute-start(f32[256,128]{1,0:T(8,128)S(1)} %get-tuple-element.134.refs_4_), channel_id=1, source_target_pairs={{0,16},{8,24},{16,0},{24,8},{1,17},{9,25},{17,1},{25,9},{2,18},{10... | collective-permute-start | bytes 393224 | tf_op jit(solution)/shard_map/ppermute | solution.py:83
  40.4 6.9 %collective-permute-start.13 = (f32[256,128]{1,0:T(8,128)S(1)}, f32[256,128]{1,0:T(8,128)S(1)}, u32[]{:S(2)}, u32[]{:S(2)}) collective-permute-start(f32[256,128]{1,0:T(8,128)S(1)} %get-tuple-element.133.refs_2_), channel_id=1, source_target_pairs={{0,8},{8,0},{16,24},{24,16},{1,9},{9,1},{17,25},{25,17},{2,10},{10... | collective-permute-start | bytes 393224 | tf_op jit(solution)/shard_map/ppermute | solution.py:83
  42.1 6.7 %collective-permute-start.15 = (f32[256,128]{1,0:T(8,128)S(1)}, f32[256,128]{1,0:T(8,128)S(1)}, u32[]{:S(2)}, u32[]{:S(2)}) collective-permute-start(f32[256,128]{1,0:T(8,128)S(1)} %sums.19), channel_id=1, source_target_pairs={{0,2},{1,3},{2,0},{3,1},{4,6},{5,7},{6,4},{7,5},{8,10},{9,11},{10,... | collective-permute-start | bytes 393224 | tf_op jit(solution)/shard_map/ppermute | solution.py:83
  59.4 5.5 %collective-permute-start.17 = (f32[256,128]{1,0:T(8,128)S(1)}, f32[256,128]{1,0:T(8,128)S(1)}, u32[]{:S(2)}, u32[]{:S(2)}) collective-permute-start(f32[256,128]{1,0:T(8,128)S(1)} %get-tuple-element.148), channel_id=1, source_target_pairs={{0,8},{8,0},{16,24},{24,16},{1,9},{9,1},{17,25},{25,17},{2,10},{10... | collective-permute-start | bytes 393224 | tf_op jit(solution)/shard_map/ppermute | solution.py:83
  63.1 5.5 %collective-permute-start.23 = (f32[256,128]{1,0:T(8,128)S(1)}, f32[256,128]{1,0:T(8,128)S(1)}, u32[]{:S(2)}, u32[]{:S(2)}) collective-permute-start(f32[256,128]{1,0:T(8,128)S(1)} %get-tuple-element.167), channel_id=1, source_target_pairs={{0,16},{8,24},{16,0},{24,8},{1,17},{9,25},{17,1},{25,9},{2,18},{10... | collective-permute-start | bytes 393224 | tf_op jit(solution)/shard_map/ppermute | solution.py:83
  66.9 9.6 %collective-permute-start.19 = (f32[256,128]{1,0:T(8,128)S(1)}, f32[256,128]{1,0:T(8,128)S(1)}, u32[]{:S(2)}, u32[]{:S(2)}) collective-permute-start(f32[256,128]{1,0:T(8,128)S(1)} %get-tuple-element.158.refs_0_), channel_id=1, source_target_pairs={{0,16},{8,24},{16,0},{24,8},{1,17},{9,25},{17,1},{25,9},{2,18},{10... | collective-permute-start | bytes 393224 | tf_op jit(solution)/shard_map/ppermute | solution.py:83
  67.8 8.7 %collective-permute-start.24 = (f32[256,128]{1,0:T(8,128)S(1)}, f32[256,128]{1,0:T(8,128)S(1)}, u32[]{:S(2)}, u32[]{:S(2)}) collective-permute-start(f32[256,128]{1,0:T(8,128)S(1)} %get-tuple-element.161.refs_2_), channel_id=1, source_target_pairs={{0,8},{8,0},{16,24},{24,16},{1,9},{9,1},{17,25},{25,17},{2,10},{10... | collective-permute-start | bytes 393224 | tf_op jit(solution)/shard_map/ppermute | solution.py:83
  68.7 6.1 %collective-permute-start.21 = (f32[256,128]{1,0:T(8,128)S(1)}, f32[256,128]{1,0:T(8,128)S(1)}, u32[]{:S(2)}, u32[]{:S(2)}) collective-permute-start(f32[256,128]{1,0:T(8,128)S(1)} %get-tuple-element.198), channel_id=1, source_target_pairs={{0,2},{1,3},{2,0},{3,1},{4,6},{5,7},{6,4},{7,5},{8,10},{9,11},{10,... | collective-permute-start | bytes 393224 | tf_op jit(solution)/shard_map/ppermute | solution.py:83
  70.2 9.6 %collective-permute-start.27 = (f32[256,128]{1,0:T(8,128)S(1)}, f32[256,128]{1,0:T(8,128)S(1)}, u32[]{:S(2)}, u32[]{:S(2)}) collective-permute-start(f32[256,128]{1,0:T(8,128)S(1)} %get-tuple-element.169.refs_0_), channel_id=1, source_target_pairs={{0,16},{8,24},{16,0},{24,8},{1,17},{9,25},{17,1},{25,9},{2,18},{10... | collective-permute-start | bytes 393224 | tf_op jit(solution)/shard_map/ppermute | solution.py:83
  72.8 7.1 %collective-permute-start.28 = (f32[256,128]{1,0:T(8,128)S(1)}, f32[256,128]{1,0:T(8,128)S(1)}, u32[]{:S(2)}, u32[]{:S(2)}) collective-permute-start(f32[256,128]{1,0:T(8,128)S(1)} %get-tuple-element.170.refs_2_), channel_id=1, source_target_pairs={{0,8},{8,0},{16,24},{24,16},{1,9},{9,1},{17,25},{25,17},{2,10},{10... | collective-permute-start | bytes 393224 | tf_op jit(solution)/shard_map/ppermute | solution.py:83
  74.8 7.3 %collective-permute-start.31 = (f32[256,128]{1,0:T(8,128)S(1)}, f32[256,128]{1,0:T(8,128)S(1)}, u32[]{:S(2)}, u32[]{:S(2)}) collective-permute-start(f32[256,128]{1,0:T(8,128)S(1)} %sums.24.refs_0_), channel_id=1, source_target_pairs={{0,4},{1,5},{2,6},{3,7},{4,0},{5,1},{6,2},{7,3},{8,12},{9,13},{10,... | collective-permute-start | bytes 393224 | tf_op jit(solution)/shard_map/ppermute | solution.py:83
  76.5 6.2 %collective-permute-start.25 = (f32[256,128]{1,0:T(8,128)S(1)}, f32[256,128]{1,0:T(8,128)S(1)}, u32[]{:S(2)}, u32[]{:S(2)}) collective-permute-start(f32[256,128]{1,0:T(8,128)S(1)} %get-tuple-element.174.refs_0_), channel_id=1, source_target_pairs={{0,8},{8,0},{16,24},{24,16},{1,9},{9,1},{17,25},{25,17},{2,10},{10... | collective-permute-start | bytes 393224 | tf_op jit(solution)/shard_map/ppermute | solution.py:83
  79.9 7.3 %collective-permute-start.29 = (f32[256,128]{1,0:T(8,128)S(1)}, f32[256,128]{1,0:T(8,128)S(1)}, u32[]{:S(2)}, u32[]{:S(2)}) collective-permute-start(f32[256,128]{1,0:T(8,128)S(1)} %get-tuple-element.183.refs_3_), channel_id=1, source_target_pairs={{0,8},{8,0},{16,24},{24,16},{1,9},{9,1},{17,25},{25,17},{2,10},{10... | collective-permute-start | bytes 393224 | tf_op jit(solution)/shard_map/ppermute | solution.py:83
  81.0 6.2 %collective-permute-start.30 = (f32[256,128]{1,0:T(8,128)S(1)}, f32[256,128]{1,0:T(8,128)S(1)}, u32[]{:S(2)}, u32[]{:S(2)}) collective-permute-start(f32[256,128]{1,0:T(8,128)S(1)} %get-tuple-element.184.refs_5_), channel_id=1, source_target_pairs={{0,16},{8,24},{16,0},{24,8},{1,17},{9,25},{17,1},{25,9},{2,18},{10... | collective-permute-start | bytes 393224 | tf_op jit(solution)/shard_map/ppermute | solution.py:83
  (16 other events, 78.6 us)
